TPU v7x, 32 devices: a whole 2x2x4 slice. The times are simulated.
32 devices in a mesh: group: 2 (over y), expert: 4 (over z), dp: 4 (over x, core).
Axes of the slice: x: 2, y: 2, z: 4, core: 2. Of those that a mesh axis runs over, the one named last changes fastest.
Arguments:
- tokens: bfloat16 [4096, 2048], P(('group', 'expert', 'dp')), parts along dimension 0, may hold values from -6 to 6
- cotangent: bfloat16 [4096, 2048], P(('group', 'expert', 'dp')), parts along dimension 0, may hold values from -4 to 4
- expert_ids: int32 [4096, 8], P(('group', 'expert', 'dp')), parts along dimension 0, may hold values from 0 to 15, as said below
- gates: bfloat16 [4096, 8], P(('group', 'expert', 'dp')), parts along dimension 0, may hold values from 0.029907227 to 0.5
- w_gate: bfloat16 [16, 2048, 384], P(('expert', 'dp')), may hold values from -0.125 to 0.125
- w_up: bfloat16 [16, 2048, 384], P(('expert', 'dp')), may hold values from -0.125 to 0.125
- w_down: bfloat16 [16, 384, 2048], P(('expert', 'dp')), may hold values from -0.3125 to 0.3125
Outputs:
- tokens_grad: bfloat16 [4096, 2048], P(('group', 'expert', 'dp')), parts along dimension 0
- gates_grad: bfloat16 [4096, 8], P(('group', 'expert', 'dp')), parts along dimension 0
- grad_gate: bfloat16 [32, 2048, 384], P(('group', 'expert', 'dp')), parts along dimension 0
- grad_up: bfloat16 [32, 2048, 384], P(('group', 'expert', 'dp')), parts along dimension 0
- grad_down: bfloat16 [32, 384, 2048], P(('group', 'expert', 'dp')), parts along dimension 0
There are 2 independent parts, one for each index of `group`. A program takes and returns all parts, laid end to end along the dimension named above; an argument that names none is the same for every part. Nothing has to cross between parts.
Inputs may be any that keep to these rules, and one draw needn't show every extreme that they name: `expert_ids`: each row names 8 different experts; the 128 rows of one device (aligned blocks) name every expert exactly 128 * 8 // 16 times.
All inputs are finite; a program needn't handle non-finite values.
Results may differ from a plain program's by a relative error of at most 0.0085.
Values may be sent and summed in bfloat16 or wider, within the bound.
No kernel may reach another device: no remote copies, remote signals or barrier semaphores. Data moves between devices by JAX's collectives and lax.ppermute only.
A program may use at most 128 MiB of HBM per device.

v0:
```python
import jax
import jax.numpy as jnp
from jax import lax
from jax.sharding import PartitionSpec as P


def contract_rows(left, right):
    return lax.dot_general(
        left, right, (((0,), (0,)), ((), ())), preferred_element_type=jnp.float32
    )


def contract_cols(left, right):
    return lax.dot_general(
        left, right, (((1,), (1,)), ((), ())), preferred_element_type=jnp.float32
    )


def expert_math(rows_in, rows_cot, row_gate, w_one, u_one, d_one):
    pre_gate = jnp.dot(rows_in, w_one, preferred_element_type=jnp.float32)
    pre_up = jnp.dot(rows_in, u_one, preferred_element_type=jnp.float32)
    sigma = jax.nn.sigmoid(pre_gate)
    active = pre_gate * sigma
    hidden = (active * pre_up).astype(jnp.bfloat16)
    back_hidden = contract_cols(rows_cot, d_one)
    expert_out = jnp.dot(hidden, d_one, preferred_element_type=jnp.float32)
    gate_term = jnp.sum(rows_cot.astype(jnp.float32) * expert_out, axis=1)
    weight_col = row_gate.astype(jnp.float32)[:, None]
    scaled_back = weight_col * back_hidden
    grad_pre_gate = (scaled_back * pre_up * sigma * (1.0 + pre_gate * (1.0 - sigma))).astype(
        jnp.bfloat16
    )
    grad_pre_up = (scaled_back * active).astype(jnp.bfloat16)
    scaled_hidden = (weight_col * active * pre_up).astype(jnp.bfloat16)
    row_grad = (contract_cols(grad_pre_gate, w_one) + contract_cols(grad_pre_up, u_one)).astype(
        jnp.bfloat16
    )
    return (row_grad, gate_term.astype(jnp.bfloat16), grad_pre_gate, grad_pre_up, scaled_hidden)


def per_device(tokens, cotangent, expert_ids, gates, w_gate, w_up, w_down):
    token_count = tokens.shape[0]
    model_width = tokens.shape[1]
    top_count = expert_ids.shape[1]
    expert_count = lax.axis_size("expert") * lax.axis_size("dp")
    assigned = token_count * top_count
    slot_count = assigned // expert_count
    position = jnp.arange(assigned, dtype=jnp.int32)
    order = jnp.argsort(expert_ids.reshape(-1) * assigned + position)
    rank = jnp.zeros((assigned,), jnp.int32).at[order].set(position)
    source = order // top_count
    send_in = tokens[source].reshape(expert_count, slot_count, model_width)
    send_cot = cotangent[source].reshape(expert_count, slot_count, model_width)
    send_gate = gates.reshape(-1)[order].reshape(expert_count, slot_count)
    w_one = w_gate[0]
    u_one = w_up[0]
    d_one = w_down[0]
    rows_in = lax.all_to_all(send_in, ("expert", "dp"), split_axis=0, concat_axis=0, tiled=True)
    rows_cot = lax.all_to_all(send_cot, ("expert", "dp"), split_axis=0, concat_axis=0, tiled=True)
    row_gate = lax.all_to_all(send_gate, ("expert", "dp"), split_axis=0, concat_axis=0, tiled=True)
    senders = rows_in.shape[0]
    width_slots = rows_in.shape[1]
    outputs = expert_math(
        rows_in.reshape(-1, model_width),
        rows_cot.reshape(-1, model_width),
        row_gate.reshape(-1),
        w_one,
        u_one,
        d_one,
    )
    back_rows = lax.all_to_all(
        outputs[0].reshape(senders, width_slots, model_width),
        ("expert", "dp"),
        split_axis=0,
        concat_axis=0,
        tiled=True,
    )
    back_gate = lax.all_to_all(
        outputs[1].reshape(senders, width_slots),
        ("expert", "dp"),
        split_axis=0,
        concat_axis=0,
        tiled=True,
    )
    results = (
        back_rows,
        back_gate,
        rows_in,
        rows_cot,
        outputs[2].reshape(senders, width_slots, -1),
        outputs[3].reshape(senders, width_slots, -1),
        outputs[4].reshape(senders, width_slots, -1),
    )
    back_rows, back_gate, recv_in, recv_cot, grad_pre_gate, grad_pre_up, scaled_hidden = results
    recv_in = recv_in.reshape(-1, model_width)
    recv_cot = recv_cot.reshape(-1, model_width)
    grad_pre_gate = grad_pre_gate.reshape(assigned, -1)
    grad_pre_up = grad_pre_up.reshape(assigned, -1)
    scaled_hidden = scaled_hidden.reshape(assigned, -1)
    grad_w_gate = contract_rows(recv_in, grad_pre_gate).astype(jnp.bfloat16)
    grad_w_up = contract_rows(recv_in, grad_pre_up).astype(jnp.bfloat16)
    grad_w_down = contract_rows(scaled_hidden, recv_cot).astype(jnp.bfloat16)
    back_flat = back_rows.reshape(assigned, model_width)[rank]
    tokens_grad = jnp.sum(
        back_flat.reshape(token_count, top_count, model_width).astype(jnp.float32), axis=1
    )
    gates_grad = back_gate.reshape(-1)[rank].reshape(token_count, top_count)
    return (
        tokens_grad.astype(jnp.bfloat16),
        gates_grad,
        grad_w_gate[None],
        grad_w_up[None],
        grad_w_down[None],
    )


def solution(mesh):
    placed = (
        P(("group", "expert", "dp"), None),
        P(("group", "expert", "dp"), None),
        P(("group", "expert", "dp"), None),
        P(("group", "expert", "dp"), None),
        P(("expert", "dp"), None, None),
        P(("expert", "dp"), None, None),
        P(("expert", "dp"), None, None),
    )
    return jax.shard_map(
        per_device,
        mesh=mesh,
        in_specs=placed,
        out_specs=(
            P(("group", "expert", "dp"), None),
            P(("group", "expert", "dp"), None),
            P(("group", "expert", "dp"), None, None),
            P(("group", "expert", "dp"), None, None),
            P(("group", "expert", "dp"), None, None),
        ),
        check_vma=False,
    )
```

profile of v0, /device:TPU:11, one launch (start us, length us, event | category | flops | bytes accessed | tf_op | source)
XLA Modules:
  0.0 363.9 jit_solution(9158764356494314116)
XLA Ops:
  0.6 0.0 copy-start
  0.6 0.0 copy-start.1
  0.7 0.8 broadcast_multiply_fusion
  1.5 0.8 copy.15
  2.3 0.1 reshape.74
  2.4 0.1 copy.16
  2.5 0.1 mul.48
  2.6 4.4 %sort.17 = (s32[1024]{0:T(1024)}, s32[1024]{0:T(1024)S(1)}) sort(s32[1024]{0:T(1024)S(1)} %iota_add_fusion, s32[1024]{0:T(1024)S(1)} %iota.10), dimensions={0}, to_apply=%region_0.0 | sort | flops 10240 | bytes 16384 | tf_op jit(solution)/shard_map/jit(argsort)/sort | solution.py:49
  7.0 6.8 %gather_fusion = bf16[1024]{0:T(1024)(128)(2,1)S(1)} fusion(bf16[1024]{0:T(1024)(128)(2,1)S(1)} %reshape.74, s32[1024]{0:T(1024)S(1)} %get-tuple-element.20), kind=kCustom, calls=%fused_computation | custom fusion | bytes 8192 | tf_op jit(solution)/shard_map/gather | solution.py:54
  13.8 0.7 all_to_all.25
  14.5 6.6 %all-to-all-start = ((bf16[16,1,64]{2,1,0:T(2,128)(2,1)}), bf16[16,1,64]{2,1,0:T(2,128)(2,1)S(1)}, u32[]{:S(2)}, u32[]{:S(2)}) async-start(bf16[16,1,64]{2,1,0:T(2,128)(2,1)} %all_to_all.25), calls=%async_computation | async-start | bytes 16384 | tf_op jit(solution)/shard_map/all_to_all | solution.py:60
  21.0 0.0 copy-done.1
  21.0 6.0 %gather_fusion.2 = bf16[1024,2048]{1,0:T(8,128)(2,1)} fusion(bf16[128,2048]{1,0:T(8,128)(2,1)S(1)} %copy-done.1, s32[1024]{0:T(1024)S(1)} %get-tuple-element.21), kind=kCustom, calls=%fused_computation.2 | custom fusion | bytes 8392704 | tf_op jit(solution)/shard_map/gather | solution.py:52
  27.1 0.0 all-to-all-done
  27.1 0.0 copy-start.2
  27.1 6.2 %all-to-all-start.2 = ((bf16[16,64,2048]{2,1,0:T(8,128)(2,1)}), bf16[16,64,2048]{2,1,0:T(8,128)(2,1)}, u32[]{:S(2)}, u32[]{:S(2)}) async-start(bf16[16,64,2048]{2,1,0:T(8,128)(2,1)} %bitcast.46), calls=%async_computation.2 | async-start | bytes 8388608 | tf_op jit(solution)/shard_map/all_to_all | solution.py:58
  33.2 0.0 copy-done.2
  33.2 6.1 %gather_fusion.1 = bf16[1024,2048]{1,0:T(8,128)(2,1)} fusion(bf16[128,2048]{1,0:T(8,128)(2,1)S(1)} %copy-done.2, s32[1024]{0:T(1024)S(1)} %get-tuple-element.21), kind=kCustom, calls=%fused_computation.1 | custom fusion | bytes 8392704 | tf_op jit(solution)/shard_map/gather | solution.py:53
  39.3 86.4 %all-to-all-done.2 = bf16[16,64,2048]{2,1,0:T(8,128)(2,1)} async-done(((bf16[16,64,2048]{2,1,0:T(8,128)(2,1)}), bf16[16,64,2048]{2,1,0:T(8,128)(2,1)}, u32[]{:S(2)}, u32[]{:S(2)}) %all-to-all-start.2) | async-done | bytes 4194336 | tf_op jit(solution)/shard_map/all_to_all | solution.py:58
  125.7 4.9 %all-to-all-start.1 = ((bf16[16,64,2048]{2,1,0:T(8,128)(2,1)}), bf16[16,64,2048]{2,1,0:T(8,128)(2,1)}, u32[]{:S(2)}, u32[]{:S(2)}) async-start(bf16[16,64,2048]{2,1,0:T(8,128)(2,1)} %bitcast.45), calls=%async_computation.1 | async-start | bytes 8388608 | tf_op jit(solution)/shard_map/all_to_all | solution.py:59
  130.6 0.1 reshape.84
  130.7 0.0 copy-done
  130.7 0.0 copy-start.3
  130.7 5.8 %fusion.5 = f32[1024,384]{1,0:T(8,128)} fusion(bf16[1024,2048]{1,0:T(8,128)(2,1)} %bitcast.4, bf16[1,2048,384]{2,1,0:T(8,128)(2,1)S(1)} %copy-done), kind=kOutput, calls=%fused_computation.17 | convolution fusion | flops 1610612736 | bytes 7340032 | tf_op jit(solution)/shard_map/dot_general | solution.py:20
  136.5 0.0 copy-done.3
  136.5 5.7 %fusion.8 = f32[1024,384]{1,0:T(8,128)} fusion(bf16[1024,2048]{1,0:T(8,128)(2,1)} %bitcast.4, bf16[1,2048,384]{2,1,0:T(8,128)(2,1)S(1)} %copy-done.3), kind=kOutput, calls=%fused_computation.20 | convolution fusion | flops 1610612736 | bytes 7340032 | tf_op jit(solution)/shard_map/dot_general | solution.py:21
  142.2 80.9 %all-to-all-done.1 = bf16[16,64,2048]{2,1,0:T(8,128)(2,1)} async-done(((bf16[16,64,2048]{2,1,0:T(8,128)(2,1)}), bf16[16,64,2048]{2,1,0:T(8,128)(2,1)}, u32[]{:S(2)}, u32[]{:S(2)}) %all-to-all-start.1) | async-done | bytes 4194336 | tf_op jit(solution)/shard_map/all_to_all | solution.py:59
  223.1 6.1 %multiply_reduce_fusion = bf16[1024]{0:T(1024)(128)(2,1)S(1)} fusion(bf16[1024,2048]{1,0:T(8,128)(2,1)} %bitcast.1, bf16[1,384,2048]{2,1,0:T(8,128)(2,1)} %param.13, f32[1024,384]{1,0:T(8,128)} %fusion.8, f32[1024,384]{1,0:T(8,128)} %fusion.5), kind=kOutput, calls=%fused_computation.6 | convolution fusion | flops 1619262464 | bytes 8914944 | tf_op jit(solution)/shard_map/dot_general | solution.py:26
  229.1 0.7 convert_element_type.67
  229.8 4.9 %all-to-all-start.4 = ((bf16[16,1,64]{2,1,0:T(2,128)(2,1)}), bf16[16,1,64]{2,1,0:T(2,128)(2,1)S(1)}, u32[]{:S(2)}, u32[]{:S(2)}) async-start(bf16[16,1,64]{2,1,0:T(2,128)(2,1)} %convert_element_type.67), calls=%async_computation.4 | async-start | bytes 16384 | tf_op jit(solution)/shard_map/all_to_all | solution.py:78
  234.7 6.4 %multiply_convert_fusion.2 = (bf16[1024,384]{1,0:T(8,128)(2,1)S(1)}, bf16[1024,384]{1,0:T(8,128)(2,1)S(1)}) fusion(f32[1024,384]{1,0:T(8,128)} %fusion.5, f32[1024,384]{1,0:T(8,128)} %fusion.8, bf16[1024,2048]{1,0:T(8,128)(2,1)} %bitcast.1, bf16[1,384,2048]{2,1,0:T(8,128)(2,1)} %param.13, f32[1024]{0:T(1024)S(1)} %reshape.84), kind=kOutput, calls=%fused_computation.27 | convolution fusion | flops 1616117760 | bytes 10489856 | tf_op jit(solution)/shard_map/dot_general | solution.py:14
  241.1 0.0 copy-start.4
  241.1 0.0 copy-start.6
  241.1 2.4 fusion.3
  243.5 0.0 copy-done.4
  243.5 0.0 copy-done.6
  243.5 4.3 %add_convert_fusion = bf16[1024,2048]{1,0:T(8,128)(2,1)} fusion(f32[1024,2048]{1,0:T(8,128)S(1)} %fusion.3, bf16[1024,384]{1,0:T(8,128)(2,1)S(1)} %get-tuple-element.17, bf16[1,2048,384]{2,1,0:T(8,128)(2,1)S(1)} %copy-done.3), kind=kOutput, calls=%fused_computation.7 | convolution fusion | flops 1614807040 | bytes 14942208 | tf_op jit(solution)/shard_map/dot_general | solution.py:14
  247.9 0.0 all-to-all-done.4
  247.9 0.0 copy-start.7
  247.9 6.1 %all-to-all-start.3 = ((bf16[16,64,2048]{2,1,0:T(8,128)(2,1)}), bf16[16,64,2048]{2,1,0:T(8,128)(2,1)}, u32[]{:S(2)}, u32[]{:S(2)}) async-start(bf16[16,64,2048]{2,1,0:T(8,128)(2,1)} %bitcast.44), calls=%async_computation.3 | async-start | bytes 8388608 | tf_op jit(solution)/shard_map/all_to_all | solution.py:71
  254.0 4.5 %scatter_custom_fusion = s32[1024]{0:T(1024)S(1)} fusion(s32[1024]{0:T(1024)S(1)} %get-tuple-element.19, s32[1024]{0:T(1024)S(1)} %iota.11, s32[]{:T(128)} %constant.18.clone.1), kind=kCustom, calls=%fused_computation.48 | custom fusion | bytes 4100 | tf_op jit(solution)/shard_map/scatter | solution.py:50
  258.6 0.0 copy-done.7
  258.6 0.0 copy-start.5
  258.6 5.8 %fusion.1 = bf16[1,2048,384]{2,1,0:T(8,128)(2,1)} fusion(bf16[1024,2048]{1,0:T(8,128)(2,1)} %bitcast.4, bf16[1024,384]{1,0:T(8,128)(2,1)S(1)} %copy-done.7), kind=kOutput, calls=%fused_computation.13 | convolution fusion | flops 1611399168 | bytes 6553600 | tf_op jit(solution)/shard_map/dot_general | solution.py:8
  264.4 0.0 copy-done.5
  264.4 0.0 copy-start.8
  264.4 0.0 copy-start.9
  264.4 5.9 %fusion = bf16[1,2048,384]{2,1,0:T(8,128)(2,1)} fusion(bf16[1024,2048]{1,0:T(8,128)(2,1)} %bitcast.4, bf16[1024,384]{1,0:T(8,128)(2,1)S(1)} %copy-done.5), kind=kOutput, calls=%fused_computation.12 | convolution fusion | flops 1611399168 | bytes 6553600 | tf_op jit(solution)/shard_map/dot_general | solution.py:8
  270.3 0.0 copy-done.8
  270.3 0.0 copy-done.9
  270.3 5.4 %fusion.2 = bf16[1,384,2048]{2,1,0:T(8,128)(2,1)} fusion(bf16[1024,2048]{1,0:T(8,128)(2,1)} %bitcast.1, f32[1024,384]{1,0:T(8,128)S(1)} %copy-done.9, f32[1024]{0:T(1024)S(1)} %reshape.84, f32[1024,384]{1,0:T(8,128)S(1)} %copy-done.8), kind=kOutput, calls=%fused_computation.14 | convolution fusion | flops 1614151680 | bytes 8916992 | tf_op jit(solution)/shard_map/dot_general | solution.py:8
  275.8 0.1 reshape.82
  275.9 6.8 %gather_fusion.4 = bf16[1024]{0:T(1024)(128)(2,1)S(1)} fusion(bf16[1024]{0:T(1024)(128)(2,1)S(1)} %reshape.82, s32[1024]{0:T(1024)S(1)} %fusion.20), kind=kCustom, calls=%fused_computation.4 | custom fusion | bytes 8192 | tf_op jit(solution)/shard_map/gather | solution.py:107
  282.7 0.1 reshape.83
  282.7 0.7 copy.19
  283.4 63.1 %all-to-all-done.3 = bf16[16,64,2048]{2,1,0:T(8,128)(2,1)} async-done(((bf16[16,64,2048]{2,1,0:T(8,128)(2,1)}), bf16[16,64,2048]{2,1,0:T(8,128)(2,1)}, u32[]{:S(2)}, u32[]{:S(2)}) %all-to-all-start.3) | async-done | bytes 4194336 | tf_op jit(solution)/shard_map/all_to_all | solution.py:71
  346.5 11.6 %gather_fusion.3 = bf16[1024,2048]{1,0:T(8,128)(2,1)} fusion(bf16[1024,2048]{1,0:T(8,128)(2,1)} %bitcast.8, s32[1024]{0:T(1024)S(1)} %fusion.20), kind=kCustom, calls=%fused_computation.3 | custom fusion | bytes 8392704 | tf_op jit(solution)/shard_map/gather | solution.py:103
  358.1 5.9 %bitcast_reduce_fusion = bf16[128,2048]{1,0:T(8,128)(2,1)} fusion(bf16[1024,2048]{1,0:T(8,128)(2,1)} %gather_fusion.3), kind=kLoop, calls=%fused_computation.8 | loop fusion | flops 1835008 | bytes 4718592 | tf_op jit(solution)/shard_map/reduce_sum | solution.py:104
  (7 shorter events, 0.1 us)
Async XLA Ops:
  0.6 130.1 %copy-start = (bf16[1,2048,384]{2,1,0:T(8,128)(2,1)S(1)}, bf16[1,2048,384]{2,1,0:T(8,128)(2,1)}, u32[]{:S(2)}) copy-start(bf16[1,2048,384]{2,1,0:T(8,128)(2,1)} %param.11) | copy-start | bytes 4718596
  0.6 20.4 %copy-start.1 = (bf16[128,2048]{1,0:T(8,128)(2,1)S(1)}, bf16[128,2048]{1,0:T(8,128)(2,1)}, u32[]{:S(2)}) copy-start(bf16[128,2048]{1,0:T(8,128)(2,1)} %param.7) | copy-start | bytes 1572868
  14.5 12.6 %all-to-all-start = ((bf16[16,1,64]{2,1,0:T(2,128)(2,1)}), bf16[16,1,64]{2,1,0:T(2,128)(2,1)S(1)}, u32[]{:S(2)}, u32[]{:S(2)}) async-start(bf16[16,1,64]{2,1,0:T(2,128)(2,1)} %all_to_all.25), calls=%async_computation | async-start | bytes 16384 | tf_op jit(solution)/shard_map/all_to_all | solution.py:60
  27.1 6.2 %copy-start.2 = (bf16[128,2048]{1,0:T(8,128)(2,1)S(1)}, bf16[128,2048]{1,0:T(8,128)(2,1)}, u32[]{:S(2)}) copy-start(bf16[128,2048]{1,0:T(8,128)(2,1)} %param.8) | copy-start | bytes 1572868
  27.1 98.6 %all-to-all-start.2 = ((bf16[16,64,2048]{2,1,0:T(8,128)(2,1)}), bf16[16,64,2048]{2,1,0:T(8,128)(2,1)}, u32[]{:S(2)}, u32[]{:S(2)}) async-start(bf16[16,64,2048]{2,1,0:T(8,128)(2,1)} %bitcast.46), calls=%async_computation.2 | async-start | bytes 8388608 | tf_op jit(solution)/shard_map/all_to_all | solution.py:58
  125.7 97.4 %all-to-all-start.1 = ((bf16[16,64,2048]{2,1,0:T(8,128)(2,1)}), bf16[16,64,2048]{2,1,0:T(8,128)(2,1)}, u32[]{:S(2)}, u32[]{:S(2)}) async-start(bf16[16,64,2048]{2,1,0:T(8,128)(2,1)} %bitcast.45), calls=%async_computation.1 | async-start | bytes 8388608 | tf_op jit(solution)/shard_map/all_to_all | solution.py:59
  130.7 5.8 %copy-start.3 = (bf16[1,2048,384]{2,1,0:T(8,128)(2,1)S(1)}, bf16[1,2048,384]{2,1,0:T(8,128)(2,1)}, u32[]{:S(2)}) copy-start(bf16[1,2048,384]{2,1,0:T(8,128)(2,1)} %param.12) | copy-start | bytes 4718596
  229.8 18.1 %all-to-all-start.4 = ((bf16[16,1,64]{2,1,0:T(2,128)(2,1)}), bf16[16,1,64]{2,1,0:T(2,128)(2,1)S(1)}, u32[]{:S(2)}, u32[]{:S(2)}) async-start(bf16[16,1,64]{2,1,0:T(2,128)(2,1)} %convert_element_type.67), calls=%async_computation.4 | async-start | bytes 16384 | tf_op jit(solution)/shard_map/all_to_all | solution.py:78
  241.1 2.4 copy-start.4
  241.1 2.4 copy-start.6
  247.9 10.7 %copy-start.7 = (bf16[1024,384]{1,0:T(8,128)(2,1)S(1)}, bf16[1024,384]{1,0:T(8,128)(2,1)}, u32[]{:S(2)}) copy-start(bf16[1024,384]{1,0:T(8,128)(2,1)} %copy-done.6) | copy-start | bytes 2359300
  247.9 98.6 %all-to-all-start.3 = ((bf16[16,64,2048]{2,1,0:T(8,128)(2,1)}), bf16[16,64,2048]{2,1,0:T(8,128)(2,1)}, u32[]{:S(2)}, u32[]{:S(2)}) async-start(bf16[16,64,2048]{2,1,0:T(8,128)(2,1)} %bitcast.44), calls=%async_computation.3 | async-start | bytes 8388608 | tf_op jit(solution)/shard_map/all_to_all | solution.py:71
  258.6 5.8 %copy-start.5 = (bf16[1024,384]{1,0:T(8,128)(2,1)S(1)}, bf16[1024,384]{1,0:T(8,128)(2,1)}, u32[]{:S(2)}) copy-start(bf16[1024,384]{1,0:T(8,128)(2,1)} %copy-done.4) | copy-start | bytes 2359300
  264.4 5.9 %copy-start.8 = (f32[1024,384]{1,0:T(8,128)S(1)}, f32[1024,384]{1,0:T(8,128)}, u32[]{:S(2)}) copy-start(f32[1024,384]{1,0:T(8,128)} %fusion.5) | copy-start | bytes 4718596
  264.4 5.9 %copy-start.9 = (f32[1024,384]{1,0:T(8,128)S(1)}, f32[1024,384]{1,0:T(8,128)}, u32[]{:S(2)}) copy-start(f32[1024,384]{1,0:T(8,128)} %fusion.8) | copy-start | bytes 4718596
where the time goes:
time: 365 us; the launch traced here: 364 us
  waiting for transfers between devices  230 us (63%)
  matrix products  47.7 us (13%)
  local copies, waits for them, and re-layouts  45.2 us (12%)
  starting transfers between devices  28.7 us (8%)
  other arithmetic  11.2 us (3%)
    all_to_all x1, waiting for transfers between devices, per_device(): lax.all_to_all(send_in, ('expert', 'dp'), split_axis=0, concat_axis=0, ti...  86.4 us
    all_to_all x1, waiting for transfers between devices, per_device(): lax.all_to_all(send_cot, ('expert', 'dp'), split_axis=0, concat_axis=0, t...  80.9 us
    all_to_all x1, waiting for transfers between devices, per_device(): lax.all_to_all(outputs[0].reshape(senders, width_slots, model_width), ('e...  63.1 us
    dot_general x3, matrix products, contract_rows(): lax.dot_general(left, right, (((0,), (0,)), ((), ())), preferred_element_...  17.1 us
    dot_general x3, matrix products, contract_cols(): lax.dot_general(left, right, (((1,), (1,)), ((), ())), preferred_element_...  13.1 us
    gather x1, local copies, waits for them, and re-layouts, per_device(): back_flat = back_rows.reshape(assigned, model_width)[rank]  11.6 us
  transfers between devices with their start and end apart: 5, of which 3 were waited for; matrix products, arithmetic and copies ran while one was open for 18% of the time, Pallas kernels for 0%

commit v1 on v0

--- a/solution.py
+++ b/solution.py
@@ -1,6 +1,8 @@
 import jax
 import jax.numpy as jnp
 from jax import lax
+from jax.experimental import pallas as pl
+from jax.experimental.pallas import tpu as pltpu
 from jax.sharding import PartitionSpec as P
 
 
@@ -38,7 +40,7 @@
     return (row_grad, gate_term.astype(jnp.bfloat16), grad_pre_gate, grad_pre_up, scaled_hidden)
 
 
-def per_device(tokens, cotangent, expert_ids, gates, w_gate, w_up, w_down):
+def dispatched(tokens, cotangent, expert_ids, gates, w_gate, w_up, w_down):
     token_count = tokens.shape[0]
     model_width = tokens.shape[1]
     top_count = expert_ids.shape[1]
@@ -113,6 +115,332 @@
         grad_w_down[None],
     )
 
+CORES = 2
+TILE = 256
+LANES = 128
+
+
+def wait_for(copies):
+    for copy in copies:
+        copy.wait()
+
+
+def tiles(count, body):
+    @pl.loop(0, count // TILE)
+    def _(i):
+        body(pl.ds(pl.multiple_of(i * TILE, TILE), TILE))
+
+
+def row_tiles(count, size, body):
+    @pl.loop(0, count // size)
+    def _(i):
+        body(pl.ds(pl.multiple_of(i * size, size), size))
+
+
+def forward_kernel(lines, step, token_count, f, *refs):
+    refs = list(refs)
+    take = lambda n: [refs.pop(0) for _ in range(n)]
+    tok_in, gate_w, up_w = take(lines), take(CORES), take(CORES)
+    if step:
+        take(1)
+    slope_ref, active_ref, product_ref, tok_all = take(4)
+    tok, wg, wu, pre_gate, in_sem, out_sem = take(6)
+    rows = lines * token_count
+    slot = iter(range(64))
+    copy_in = lambda src, dst: pltpu.make_async_copy(src, dst, in_sem.at[next(slot)])
+    columns = [pl.ds(e * f, f) for e in range(CORES)]
+    first = [copy_in(tok_in[i], tok.at[pl.ds(i * token_count, token_count)]) for i in range(lines)]
+    first += [copy_in(gate_w[e], wg.at[:, columns[e]]) for e in range(CORES)]
+    second = [copy_in(up_w[e], wu.at[:, columns[e]]) for e in range(CORES)]
+    for copy in first + second:
+        copy.start()
+    wait_for(first)
+    keep = pltpu.make_async_copy(tok, tok_all.at[pl.ds(step * rows, rows)], out_sem.at[0])
+    keep.start()
+
+    def gate_tile(c):
+        pre_gate[:, c] = jnp.dot(tok[...], wg[:, c], preferred_element_type=jnp.float32)
+
+    def up_tile(c):
+        up = jnp.dot(tok[...], wu[:, c], preferred_element_type=jnp.float32)
+        gate = pre_gate[:, c]
+        sigma = jax.nn.sigmoid(gate)
+        active = gate * sigma
+        slope_ref[:, c] = up * sigma * (1.0 + gate * (1.0 - sigma))
+        active_ref[:, c] = active
+        product_ref[:, c] = active * up
+
+    tiles(CORES * f, gate_tile)
+    wait_for(second)
+    tiles(CORES * f, up_tile)
+    keep.wait()
+
+
+def backward_kernel(lines, step, token_count, f, *refs):
+    refs = list(refs)
+    take = lambda n: [refs.pop(0) for _ in range(n)]
+    cot_in, (pick_ref,), hidden_in = take(lines), take(1), take(3)
+    gate_w, up_w, down_w = take(CORES), take(CORES), take(CORES)
+    if step:
+        take(7)
+    row_own, row_far, terms, cot_all = take(4)
+    factor_all = take(6)
+    cot, wg, wu, wd, slope, active, product, back, gg, gu = take(10)
+    factors = take(6)
+    in_sem, out_sem = take(2)
+    rows = lines * token_count
+    model_width = wd.shape[1]
+    slot = iter(range(64))
+    copy_in = lambda src, dst: pltpu.make_async_copy(src, dst, in_sem.at[next(slot)])
+    columns = [pl.ds(e * f, f) for e in range(CORES)]
+    first = [copy_in(cot_in[i], cot.at[pl.ds(i * token_count, token_count)]) for i in range(lines)]
+    first += [copy_in(down_w[e], wd.at[columns[e]]) for e in range(CORES)]
+    second = [copy_in(a, b) for a, b in zip(hidden_in, (slope, active, product))]
+    third = [copy_in(gate_w[e], wg.at[:, columns[e]]) for e in range(CORES)]
+    third += [copy_in(up_w[e], wu.at[:, columns[e]]) for e in range(CORES)]
+    for copy in first + second + third:
+        copy.start()
+    wait_for(first)
+    at = pl.ds(step * rows, rows)
+    keep = pltpu.make_async_copy(cot.at[:, :model_width], cot_all.at[at], out_sem.at[0])
+    keep.start()
+
+    def back_tile(c):
+        back[:, c] = contract_cols(cot[:, :model_width], wd[c, :])
+
+    def factor_tile(r):
+        gate_cols = jnp.dot(cot[r, model_width:], pick_ref[...], preferred_element_type=jnp.float32)
+        sums = []
+        for e in range(CORES):
+            c = columns[e]
+            bh, prod = back[r, c], product[r, c]
+            hidden = prod.astype(jnp.bfloat16)
+            sums.append(jnp.sum(hidden.astype(jnp.float32) * bh, axis=1, keepdims=True))
+            weight = gate_cols[:, e : e + 1]
+            scaled_back = weight * bh
+            grad_gate = (scaled_back * slope[r, c]).astype(jnp.bfloat16)
+            grad_up = (scaled_back * active[r, c]).astype(jnp.bfloat16)
+            gg[r, c] = grad_gate
+            gu[r, c] = grad_up
+            factors[e][r, :] = grad_gate
+            factors[CORES + e][r, :] = grad_up
+            factors[2 * CORES + e][r, :] = (weight * prod).astype(jnp.bfloat16)
+        lane = lax.broadcasted_iota(jnp.int32, sums[0].shape[:1] + (CORES,), 1)
+        terms[r, :] = jnp.where(lane == 0, sums[0], sums[1])
+
+    def row_tile(c):
+        grad = contract_cols(gg[...], wg[c, :]) + contract_cols(gu[...], wu[c, :])
+        row_own[:, c] = grad[:token_count]
+        row_far[:, c] = grad[token_count:].astype(jnp.bfloat16)
+
+    tiles(CORES * f, back_tile)
+    wait_for(second)
+    row_tiles(rows, 64, factor_tile)
+    out_copies = [
+        pltpu.make_async_copy(a, b.at[at], out_sem.at[1 + i]) for i, (a, b) in enumerate(zip(factors, factor_all))
+    ]
+    for copy in out_copies:
+        copy.start()
+    wait_for(third)
+    tiles(model_width, row_tile)
+    wait_for([keep] + out_copies)
+
+
+HBM = pl.BlockSpec(memory_space=pltpu.HBM)
+VMEM = pl.BlockSpec(memory_space=pltpu.VMEM)
+PARAMS = pltpu.CompilerParams(vmem_limit_bytes=60 * 1024 * 1024)
+
+
+def forward(step, steps, blocks, weights, held):
+    lines = len(blocks)
+    token_count, model_width = blocks[0].shape
+    f = weights[0].shape[1]
+    rows, wide = lines * token_count, CORES * f
+    ins = [*blocks, *weights[: 2 * CORES], *held]
+    hidden = jax.ShapeDtypeStruct((rows, wide), jnp.float32)
+    outs = pl.pallas_call(
+        lambda *refs: forward_kernel(lines, step, token_count, f, *refs),
+        out_shape=[hidden] * 3 + [jax.ShapeDtypeStruct((steps * rows, model_width), jnp.bfloat16)],
+        in_specs=[HBM] * len(ins),
+        out_specs=[VMEM] * 3 + [HBM],
+        scratch_shapes=[
+            pltpu.VMEM((rows, model_width), jnp.bfloat16),
+            pltpu.VMEM((model_width, wide), jnp.bfloat16),
+            pltpu.VMEM((model_width, wide), jnp.bfloat16),
+            pltpu.VMEM((rows, wide), jnp.float32),
+            pltpu.SemaphoreType.DMA((lines + 2 * CORES,)),
+            pltpu.SemaphoreType.DMA((1,)),
+        ],
+        input_output_aliases={len(ins) - 1: 3} if held else {},
+        compiler_params=PARAMS,
+        cost_estimate=pl.CostEstimate(
+            flops=4 * rows * model_width * wide,
+            bytes_accessed=4 * model_width * wide + 4 * rows * model_width,
+            transcendentals=rows * wide,
+        ),
+    )(*ins)
+    return list(outs[:3]), [outs[3]]
+
+
+def backward(step, steps, blocks, pick, hidden, weights, held):
+    lines = len(blocks)
+    token_count, padded = blocks[0].shape
+    model_width, f = weights[0].shape
+    rows, wide = lines * token_count, CORES * f
+    bf = jnp.bfloat16
+    ins = [*blocks, pick, *hidden, *weights, *held]
+    whole = [jax.ShapeDtypeStruct((steps * rows, model_width), bf)]
+    whole += [jax.ShapeDtypeStruct((steps * rows, f), bf)] * 6
+    out_shape = [
+        jax.ShapeDtypeStruct((token_count, model_width), jnp.float32),
+        jax.ShapeDtypeStruct(((lines - 1) * token_count, model_width), bf),
+        jax.ShapeDtypeStruct((rows, CORES), jnp.float32),
+        *whole,
+    ]
+    base = len(ins) - len(held)
+    scratch = [pltpu.VMEM((rows, padded), bf)]
+    scratch += [pltpu.VMEM((model_width, wide), bf)] * 2 + [pltpu.VMEM((wide, model_width), bf)]
+    scratch += [pltpu.VMEM((rows, wide), jnp.float32)] * 4 + [pltpu.VMEM((rows, wide), bf)] * 2
+    scratch += [pltpu.VMEM((rows, f), bf)] * 6
+    scratch += [pltpu.SemaphoreType.DMA((lines + 3 + 3 * CORES,)), pltpu.SemaphoreType.DMA((7,))]
+    outs = pl.pallas_call(
+        lambda *refs: backward_kernel(lines, step, token_count, f, *refs),
+        out_shape=out_shape,
+        in_specs=[HBM] * lines + [VMEM] + [HBM] * (len(ins) - lines - 1),
+        out_specs=[VMEM] * 3 + [HBM] * len(whole),
+        scratch_shapes=scratch,
+        input_output_aliases={base + i: 3 + i for i in range(len(held))},
+        compiler_params=PARAMS,
+        cost_estimate=pl.CostEstimate(
+            flops=6 * rows * model_width * wide,
+            bytes_accessed=6 * model_width * wide + 8 * rows * model_width,
+            transcendentals=0,
+        ),
+    )(*ins)
+    return outs[0], outs[1], outs[2], list(outs[3:])
+
+
+def gathered(tokens, cotangent, expert_ids, gates, w_gate, w_up, w_down):
+    z_count = lax.axis_size("expert")
+    dp_count = lax.axis_size("dp")
+    x_count = dp_count // CORES
+    expert_count = z_count * dp_count
+    token_count = tokens.shape[0]
+    z_here = lax.axis_index("expert")
+    dp_here = lax.axis_index("dp")
+
+    def z_shift(value, step):
+        return lax.ppermute(value, "expert", [(i, (i + step) % z_count) for i in range(z_count)])
+
+    def x_shift(value, step):
+        return lax.ppermute(value, "dp", [(i, (i + CORES * step) % dp_count) for i in range(dp_count)])
+
+    def core_swap(value):
+        return lax.ppermute(value, "dp", [(i, i ^ 1) for i in range(dp_count)])
+
+    expert_range = jnp.arange(expert_count, dtype=jnp.int32)
+    chosen = expert_ids[:, :, None] == expert_range
+    gate_table = jnp.sum(jnp.where(chosen, gates[:, :, None].astype(jnp.float32), 0.0), axis=1).astype(jnp.bfloat16)
+
+    table_width = -(-expert_count // LANES) * LANES
+    gate_table = jnp.pad(gate_table, ((0, 0), (0, table_width - expert_count)))
+    cot_gates = jnp.concatenate([cotangent, gate_table], axis=1)
+    own_expert = z_here * dp_count + dp_here
+    mate_expert = z_here * dp_count + (dp_here ^ 1)
+    pick_row = jnp.arange(table_width, dtype=jnp.int32)[:, None]
+    pick_column = jnp.arange(LANES, dtype=jnp.int32)[None, :]
+    wanted = jnp.where(pick_column == 0, own_expert, mate_expert)
+    pick = ((pick_row == wanted) & (pick_column < CORES)).astype(jnp.bfloat16)
+
+    def after(value, *earlier):
+        return lax.optimization_barrier((value, *earlier))[0]
+
+    def across(block):
+        return [block] + [x_shift(block, s) for s in range(1, x_count)]
+
+    def home(d):
+        line = row_own[d]
+        for s in range(1, x_count):
+            line = line + x_shift(row_far[d][s - 1], x_count - s).astype(jnp.float32)
+        return line.astype(jnp.bfloat16) if d else line
+
+    blocks_in, blocks_cot = [across(tokens)], [across(cot_gates)]
+    ring_in, ring_cot = z_shift(tokens, 1), z_shift(cot_gates, 1)
+    weights = []
+    for own in (w_gate[0], w_up[0], w_down[0]):
+        weights += [own, core_swap(after(own, *weights[-1:]))]
+
+    row_own, row_far, terms, lines, rows_held, held = [], [], [], [None] * z_count, [], []
+    for d in range(z_count):
+        more = d + 1 < z_count
+        if more:
+            blocks_in.append(across(ring_in))
+            next_in = z_shift(ring_in, 1) if d + 2 < z_count else None
+            ready = ring_in
+        elif z_count > 2:
+            ready = lines[1] = home(1)
+        else:
+            ready = pick
+        blocks_in[d][0] = after(blocks_in[d][0], ready)
+        hidden, rows_held = forward(d, z_count, blocks_in[d], weights, rows_held)
+        if more:
+            ring_cot = after(ring_cot, hidden[0])
+            blocks_cot.append(across(ring_cot))
+            next_cot = z_shift(ring_cot, 1) if d + 2 < z_count else None
+            ready = ring_cot
+        own, far, term, held = backward(d, z_count, blocks_cot[d], after(pick, ready), hidden, weights, held)
+        if d + 2 < z_count:
+            ring_in, ring_cot = after(next_in, term), next_cot
+        row_own.append(own)
+        row_far.append(far.reshape(x_count - 1, token_count, -1))
+        terms.append(term)
+    for d in range(2, z_count - 1):
+        row_own[d] = after(row_own[d], terms[-1])
+
+    row_far[0], row_far[-1] = lax.optimization_barrier((row_far[0], row_far[-1]))
+    total = None
+    for d in list(range(1, z_count)) + [0]:
+        line = home(d) if lines[d] is None else lines[d]
+        if d:
+            line = z_shift(line, z_count - d).astype(jnp.float32)
+        total = line if total is None else total + line
+    tokens_grad = total.astype(jnp.bfloat16)
+
+    terms = jnp.stack(terms).astype(jnp.bfloat16).reshape(z_count, x_count, token_count, CORES)
+    columns = [terms[:, 0]] + [x_shift(terms[:, s], x_count - s) for s in range(1, x_count)]
+    columns = jnp.concatenate(columns, axis=2)
+    back = [columns[0]] + [z_shift(columns[d], z_count - d) for d in range(1, z_count)]
+    back = jnp.concatenate(back, axis=1)
+    column_ids = []
+    for d in range(z_count):
+        for s in range(x_count):
+            dp_from = (dp_here + CORES * s) % dp_count
+            first = ((z_here + d) % z_count) * dp_count
+            column_ids += [first + dp_from, first + (dp_from ^ 1)]
+    same = expert_ids[:, :, None] == jnp.stack(column_ids)
+    gates_grad = jnp.sum(jnp.where(same, back[:, None, :].astype(jnp.float32), 0.0), axis=2).astype(jnp.bfloat16)
+
+    all_in, all_cot = rows_held[0], held[0]
+    gate_own, gate_mate, up_own, up_mate, hid_own, hid_mate = held[1:]
+    mate = (
+        contract_rows(all_in, gate_mate).astype(jnp.bfloat16),
+        contract_rows(all_in, up_mate).astype(jnp.bfloat16),
+        contract_rows(hid_mate, all_cot).astype(jnp.bfloat16),
+    )
+    mine = (
+        contract_rows(all_in, gate_own),
+        contract_rows(all_in, up_own),
+        contract_rows(hid_own, all_cot),
+    )
+    grads = [(a + core_swap(b).astype(jnp.float32)).astype(jnp.bfloat16)[None] for a, b in zip(mine, mate)]
+    return (tokens_grad, gates_grad, *grads)
+
+
+def per_device(tokens, cotangent, expert_ids, gates, w_gate, w_up, w_down):
+    expert_count = lax.axis_size("expert") * lax.axis_size("dp")
+    plan = gathered if expert_count <= 4 * expert_ids.shape[1] and lax.axis_size("dp") % CORES == 0 else dispatched
+    return plan(tokens, cotangent, expert_ids, gates, w_gate, w_up, w_down)
+
 
 def solution(mesh):
     placed = (

time: 365 us -> 200 us (0.55)
  the two profiles are of different devices: /device:TPU:11 before, /device:TPU:0 now
where the time goes in v1:
time: 200 us; the launch traced here: 199 us
  Pallas kernels  68 us (34%)
  waiting for transfers between devices  60 us (30%)
  starting transfers between devices  34.6 us (17%)
  matrix products  19.6 us (10%)
  other arithmetic  11.8 us (6%)
  local copies, waits for them, and re-layouts  3.99 us (2%)
    ppermute x12, waiting for transfers between devices, z_shift(): lax.ppermute(value, 'expert', [(i, (i + step) % z_count) for i in range(z...  42.4 us
    pallas_call x4, Pallas kernels, backward(): pl.pallas_call(lambda *refs: backward_kernel(lines, step, token_count, f,...  42 us
    pallas_call x4, Pallas kernels, forward(): pl.pallas_call(lambda *refs: forward_kernel(lines, step, token_count, f,...  26 us
    dot_general x6, matrix products, contract_rows(): lax.dot_general(left, right, (((0,), (0,)), ((), ())), preferred_element_...  19.6 us
    ppermute x12, starting transfers between devices, z_shift(): lax.ppermute(value, 'expert', [(i, (i + step) % z_count) for i in range(z...  17.7 us
    ppermute x13, starting transfers between devices, x_shift(): lax.ppermute(value, 'dp', [(i, (i + CORES * step) % dp_count) for i in ra...  15.5 us
    ppermute x13, waiting for transfers between devices, x_shift(): lax.ppermute(value, 'dp', [(i, (i + CORES * step) % dp_count) for i in ra...  11 us
    ppermute x6, waiting for transfers between devices, core_swap(): return lax.ppermute(value, 'dp', [(i, i ^ 1) for i in range(dp_count)])  6.51 us
  transfers between devices with their start and end apart: 31, of which 10 were waited for; matrix products, arithmetic and copies ran while one was open for 14% of the time, Pallas kernels for 34%

profile of v1, /device:TPU:0, one launch (start us, length us, event | category | flops | bytes accessed | tf_op | source)
XLA Modules:
  0.0 199.0 jit_solution(97271372624745201)
XLA Ops:
  0.6 0.5 collective-permute-start.3
  1.1 3.2 %collective-permute-done.3.refs_3_.refs_7_ = bf16[2048,384]{1,0:T(8,128)(2,1)S(1)} collective-permute-done((bf16[2048,384]{1,0:T(8,128)(2,1)}, bf16[2048,384]{1,0:T(8,128)(2,1)S(1)}, u32[]{:S(2)}, u32[]{:S(2)}) %collective-permute-start.3) | collective-permute-done | bytes 1572896 | tf_op jit(solution)/shard_map/ppermute | solution.py:339
  4.4 0.4 collective-permute-start.4
  4.8 3.2 %collective-permute-done.4.refs_5_.refs_9_ = bf16[2048,384]{1,0:T(8,128)(2,1)S(1)} collective-permute-done((bf16[2048,384]{1,0:T(8,128)(2,1)}, bf16[2048,384]{1,0:T(8,128)(2,1)S(1)}, u32[]{:S(2)}, u32[]{:S(2)}) %collective-permute-start.4) | collective-permute-done | bytes 1572896 | tf_op jit(solution)/shard_map/ppermute | solution.py:339
  8.0 0.4 collective-permute-start.9
  8.4 2.7 %collective-permute-start.1 = (bf16[128,2048]{1,0:T(8,128)(2,1)}, bf16[128,2048]{1,0:T(8,128)(2,1)}, u32[]{:S(2)}, u32[]{:S(2)}) collective-permute-start(bf16[128,2048]{1,0:T(8,128)(2,1)} %refs_0_), channel_id=1, source_target_pairs={{0,4},{4,8},{8,12},{12,0},{1,5},{5,9},{9,13},{13,1},{2,6},{6,10},{... | collective-permute-start | bytes 1572872 | tf_op jit(solution)/shard_map/ppermute | solution.py:333
  11.1 1.5 collective-permute-start.2
  12.6 0.7 convert_element_type.85
  13.3 0.7 select_reduce_fusion.1
  14.0 0.1 copy.55
  14.1 1.9 fusion.4.refs_0_
  16.0 1.6 collective-permute-start
  17.6 0.5 collective-permute-start.8
  18.1 8.1 %collective-permute-done.1.refs_0_ = bf16[128,2048]{1,0:T(8,128)(2,1)} collective-permute-done((bf16[128,2048]{1,0:T(8,128)(2,1)}, bf16[128,2048]{1,0:T(8,128)(2,1)}, u32[]{:S(2)}, u32[]{:S(2)}) %collective-permute-start.1) | collective-permute-done | bytes 524320 | tf_op jit(solution)/shard_map/ppermute | solution.py:333
  26.2 1.7 collective-permute-start.10
  27.9 6.5 %shard_map.110 = (f32[256,768]{1,0:T(8,128)}, f32[256,768]{1,0:T(8,128)}, f32[256,768]{1,0:T(8,128)}, bf16[1024,2048]{1,0:T(8,128)(2,1)}) custom-call(bf16[128,2048]{1,0:T(8,128)(2,1)} %refs_0_, bf16[128,2048]{1,0:T(8,128)(2,1)} %collective-permute-done.2.refs_1_, bf16[2048,384]{1,0:T(8,128)(2,1)} %bitcast.58, bf16[2048,384]{1,0:T(8,128)(2,1)} %copy-done, ...), custom_call_target="tpu_custom_call" | custom-call | flops 1610612736 | bytes 8388608 | tf_op jit(solution)/shard_map/pallas_call | solution.py:261
  34.4 3.8 %collective-permute-done.refs_0_ = bf16[128,2176]{1,0:T(8,128)(2,1)} collective-permute-done((bf16[128,2176]{1,0:T(8,128)(2,1)}, bf16[128,2176]{1,0:T(8,128)(2,1)}, u32[]{:S(2)}, u32[]{:S(2)}) %collective-permute-start) | collective-permute-done | bytes 557088 | tf_op jit(solution)/shard_map/ppermute | solution.py:333
  38.2 1.7 collective-permute-start.5
  39.8 0.6 fusion.6.refs_2_
  40.5 10.5 %shard_map.111 = (f32[128,2048]{1,0:T(8,128)}, bf16[128,2048]{1,0:T(8,128)(2,1)}, f32[256,2]{1,0:T(8,128)}, bf16[1024,2048]{1,0:T(8,128)(2,1)}, bf16[1024,384]{1...) custom-call(bf16[128,2176]{1,0:T(8,128)(2,1)} %fusion.4.refs_0_, ...), custom_call_target="tpu_custom_call" | custom-call | flops 2415919104 | bytes 13631488 | tf_op jit(solution)/shard_map/pallas_call | solution.py:306
  50.9 0.4 collective-permute-start.16
  51.4 1.6 collective-permute-start.15
  52.9 6.5 %shard_map.112 = (f32[256,768]{1,0:T(8,128)}, f32[256,768]{1,0:T(8,128)}, f32[256,768]{1,0:T(8,128)}, bf16[1024,2048]{1,0:T(8,128)(2,1)}) custom-call(bf16[128,2048]{1,0:T(8,128)(2,1)} %collective-permute-done.1.refs_0_, bf16[128,2048]{1,0:T(8,128)(2,1)} %collective-permute-done.10.refs_1_, ...), custom_call_target="tpu_custom_call", output_to_operand_aliasing={{3}: (6, {})} | custom-call | flops 1610612736 | bytes 8388608 | tf_op jit(solution)/shard_map/pallas_call | solution.py:261
  59.4 1.8 collective-permute-done.6.refs_0_
  61.2 0.9 copy-done.16
  62.1 10.5 %shard_map.113 = (f32[128,2048]{1,0:T(8,128)}, bf16[128,2048]{1,0:T(8,128)(2,1)}, f32[256,2]{1,0:T(8,128)}, bf16[1024,2048]{1,0:T(8,128)(2,1)}, bf16[1024,384]{1...) custom-call(bf16[128,2176]{1,0:T(8,128)(2,1)} %collective-permute-do, ...), custom_call_target="tpu_custom_call", output_to_operand_aliasing={{3}: (12, {}), {4}: (13, {}), {5}: (14, {}), {6}: (15, {}),... | custom-call | flops 2415919104 | bytes 13631488 | tf_op jit(solution)/shard_map/pallas_call | solution.py:306
  72.6 1.7 collective-permute-start.11
  74.5 0.4 collective-permute-start.13
  75.0 0.9 convert.17
  76.1 1.7 collective-permute-start.18
  77.8 0.8 copy-done.19
  78.6 6.6 %shard_map.114 = (f32[256,768]{1,0:T(8,128)}, f32[256,768]{1,0:T(8,128)}, f32[256,768]{1,0:T(8,128)}, bf16[1024,2048]{1,0:T(8,128)(2,1)}) custom-call(bf16[128,2048]{1,0:T(8,128)(2,1)} %collective-permute-done.7.refs_0_, bf16[128,2048]{1,0:T(8,128)(2,1)} %copy-done.19, bf16[2048,384]{1,0:T(8,128)(2,1)} %bitcast.62, ...), custom_call_target="tpu_custom_call", output_to_operand_aliasing={{3}: (6, {})} | custom-call | flops 1610612736 | bytes 8388608 | tf_op jit(solution)/shard_map/pallas_call | solution.py:261
  85.2 0.4 collective-permute-start.17
  85.6 2.2 %collective-permute-done.11 = bf16[128,2048]{1,0:T(8,128)(2,1)} collective-permute-done((bf16[128,2048]{1,0:T(8,128)(2,1)}, bf16[128,2048]{1,0:T(8,128)(2,1)}, u32[]{:S(2)}, u32[]{:S(2)}) %collective-permute-start.11) | collective-permute-done | bytes 524320 | tf_op jit(solution)/shard_map/ppermute | solution.py:336
  87.9 1.9 add_convert_fusion.6
  89.8 3.8 %collective-permute-start.12 = (bf16[128,2048]{1,0:T(8,128)(2,1)}, bf16[128,2048]{1,0:T(8,128)(2,1)}, u32[]{:S(2)}, u32[]{:S(2)}) collective-permute-start(bf16[128,2048]{1,0:T(8,128)(2,1)} %add_convert_fusion.6), channel_id=1, source_target_pairs={{0,12},{4,0},{8,4},{12,8},{1,13},{5,1},{9,5},{13,9},{2,14},{6,2},{... | collective-permute-start | bytes 1572872 | tf_op jit(solution)/shard_map/ppermute | solution.py:333
  93.6 6.1 %collective-permute-done.13.refs_1_ = bf16[128,2176]{1,0:T(8,128)(2,1)S(1)} collective-permute-done((bf16[128,2176]{1,0:T(8,128)(2,1)S(1)}, bf16[128,2176]{1,0:T(8,128)(2,1)S(1)}, u32[]{:S(2)}, u32[]{:S(2)}) %collective-permute-start.13) | collective-permute-done | bytes 557088 | tf_op jit(solution)/shard_map/ppermute | solution.py:336
  99.7 0.8 copy-done.17
  100.5 10.6 %shard_map.115 = (f32[128,2048]{1,0:T(8,128)}, bf16[128,2048]{1,0:T(8,128)(2,1)}, f32[256,2]{1,0:T(8,128)}, bf16[1024,2048]{1,0:T(8,128)(2,1)}, bf16[1024,384]{1...) custom-call(bf16[128,2176]{1,0:T(8,128)(2,1)} %copy-done.13, ...), custom_call_target="tpu_custom_call", output_to_operand_aliasing={{3}: (12, {}), {4}: (13, {}), {5}: (14, {}), {6}: (15, {}),... | custom-call | flops 2415919104 | bytes 13631488 | tf_op jit(solution)/shard_map/pallas_call | solution.py:306
  111.1 0.9 convert.18
  112.1 1.7 collective-permute-start.19
  113.8 6.4 %shard_map.116 = (f32[256,768]{1,0:T(8,128)}, f32[256,768]{1,0:T(8,128)}, f32[256,768]{1,0:T(8,128)}, bf16[1024,2048]{1,0:T(8,128)(2,1)}) custom-call(bf16[128,2048]{1,0:T(8,128)(2,1)} %copy-done.18, bf16[128,2048]{1,0:T(8,128)(2,1)} %collective-permute-done.18.refs_1_, bf16[2048,384]{1,0:T(8,128)(2,1)} %bitcast.64, ...), custom_call_target="tpu_custom_call", output_to_operand_aliasing={{3}: (6, {})} | custom-call | flops 1610612736 | bytes 8388608 | tf_op jit(solution)/shard_map/pallas_call | solution.py:261
  120.3 2.6 %collective-permute-done.17.refs_1_ = bf16[128,2176]{1,0:T(8,128)(2,1)S(1)} collective-permute-done((bf16[128,2176]{1,0:T(8,128)(2,1)S(1)}, bf16[128,2176]{1,0:T(8,128)(2,1)S(1)}, u32[]{:S(2)}, u32[]{:S(2)}) %collective-permute-start.17) | collective-permute-done | bytes 557088 | tf_op jit(solution)/shard_map/ppermute | solution.py:336
  122.9 0.8 copy-done.15
  123.7 10.5 %shard_map.117 = (f32[128,2048]{1,0:T(8,128)}, bf16[128,2048]{1,0:T(8,128)(2,1)}, f32[256,2]{1,0:T(8,128)}, bf16[1024,2048]{1,0:T(8,128)(2,1)}, bf16[1024,384]{1...) custom-call(bf16[128,2176]{1,0:T(8,128)(2,1)} %copy-done.14, ...), custom_call_target="tpu_custom_call", output_to_operand_aliasing={{3}: (12, {}), {4}: (13, {}), {5}: (14, {}), {6}: (15, {}),... | custom-call | flops 2415919104 | bytes 13631488 | tf_op jit(solution)/shard_map/pallas_call | solution.py:306
  134.2 0.9 convert.19
  135.2 1.7 collective-permute-start.24
  137.0 0.4 collective-permute-start.21
  137.3 4.4 %convolution_convert_fusion = bf16[384,2048]{1,0:T(8,128)(2,1)S(1)} fusion(bf16[1024,384]{1,0:T(8,128)(2,1)} %get-tuple-element.152, bf16[1024,2048]{1,0:T(8,128)(2,1)} %get-tuple-element.151), kind=kOutput, calls=%fused_computation.3 | convolution fusion | flops 1611399168 | bytes 6553600 | tf_op jit(solution)/shard_map/dot_general | solution.py:10
  141.9 2.4 %convolution_convert_fusion.1 = bf16[2048,384]{1,0:T(8,128)(2,1)S(1)} fusion(bf16[1024,2048]{1,0:T(8,128)(2,1)S(1)} %copy-done.3, bf16[1024,384]{1,0:T(8,128)(2,1)S(1)} %copy-done.8), kind=kOutput, calls=%fused_computation.4 | convolution fusion | flops 1611399168 | bytes 6553600 | tf_op jit(solution)/shard_map/dot_general | solution.py:10
  144.4 0.1 add_convert_fusion.5
  144.5 3.8 %collective-permute-start.25 = (bf16[128,4]{0,1:T(4,128)(2,1)S(1)}, bf16[128,4]{0,1:T(4,128)(2,1)S(1)}, u32[]{:S(2)}, u32[]{:S(2)}) collective-permute-start(bf16[128,4]{0,1:T(4,128)(2,1)S(1)} %get-tuple-element.154), channel_id=1, source_target_pairs={{0,12},{4,0},{8,4},{12,8},{1,13},{5,1},{9,5},{13,9},{2,14},{6,2},{... | collective-permute-start | bytes 3080 | tf_op jit(solution)/shard_map/ppermute | solution.py:333
  148.4 0.8 collective-permute-start.26
  149.3 2.2 %collective-permute-start.20 = (bf16[128,2048]{1,0:T(8,128)(2,1)S(1)}, bf16[128,2048]{1,0:T(8,128)(2,1)S(1)}, u32[]{:S(2)}, u32[]{:S(2)}) collective-permute-start(bf16[128,2048]{1,0:T(8,128)(2,1)S(1)} %add_convert_fusion.5), channel_id=1, source_target_pairs={{0,8},{4,12},{8,0},{12,4},{1,9},{5,13},{9,1},{13,5},{2,10},{6,14},... | collective-permute-start | bytes 1572872 | tf_op jit(solution)/shard_map/ppermute | solution.py:333
  151.5 1.7 collective-permute-start.23
  153.2 0.6 collective-permute-done.27
  153.7 1.3 collective-permute-start.22
  155.0 2.4 %convolution_convert_fusion.2 = bf16[2048,384]{1,0:T(8,128)(2,1)S(1)} fusion(bf16[1024,2048]{1,0:T(8,128)(2,1)S(1)} %copy-done.3, bf16[1024,384]{1,0:T(8,128)(2,1)S(1)} %copy-done.6), kind=kOutput, calls=%fused_computation.5 | convolution fusion | flops 1611399168 | bytes 6553600 | tf_op jit(solution)/shard_map/dot_general | solution.py:10
  157.5 0.7 select_reduce_fusion
  158.1 28.2 %collective-permute-done.20 = bf16[128,2048]{1,0:T(8,128)(2,1)S(1)} collective-permute-done((bf16[128,2048]{1,0:T(8,128)(2,1)S(1)}, bf16[128,2048]{1,0:T(8,128)(2,1)S(1)}, u32[]{:S(2)}, u32[]{:S(2)}) %collective-permute-start.20) | collective-permute-done | bytes 524320 | tf_op jit(solution)/shard_map/ppermute | solution.py:333
  186.4 2.2 %add_convert_fusion.3 = bf16[128,2048]{1,0:T(8,128)(2,1)} fusion(f32[128,2048]{1,0:T(8,128)S(1)} %copy-done.9, bf16[128,2048]{1,0:T(8,128)(2,1)S(1)} %collective-permute-done.23, bf16[128,2048]{1,0:T(8,128)(2,1)S(1)} %collective-permute-done.22, bf16[128,2048]{1,0:T(8,128)(2,1)S(1)} %collective-permute-done.20, bf16[128,2048]{1,0:T(8,128)(2,1)} %collective-permute-done.12), kind=kLoop, calls=%fused_computation.11 | loop fusion | flops 2359296 | bytes 3670016 | tf_op jit(solution)/shard_map/convert_element_type | solution.py:407
  188.6 3.1 %fusion.2 = bf16[1,384,2048]{2,1,0:T(8,128)(2,1)} fusion(bf16[384,2048]{1,0:T(8,128)(2,1)S(1)} %collective-permute-done.30, bf16[1024,384]{1,0:T(8,128)(2,1)S(1)} %copy-done.4, bf16[1024,2048]{1,0:T(8,128)(2,1)S(1)} %copy-done.2), kind=kOutput, calls=%fused_computation.8 | convolution fusion | flops 1612972032 | bytes 8126464 | tf_op jit(solution)/shard_map/dot_general | solution.py:10
  191.7 3.6 %fusion.1 = bf16[1,2048,384]{2,1,0:T(8,128)(2,1)} fusion(bf16[2048,384]{1,0:T(8,128)(2,1)S(1)} %collective-permute-done.29, bf16[1024,2048]{1,0:T(8,128)(2,1)S(1)} %copy-done.3, bf16[1024,384]{1,0:T(8,128)(2,1)S(1)} %copy-done.7), kind=kOutput, calls=%fused_computation.7 | convolution fusion | flops 1612972032 | bytes 8126464 | tf_op jit(solution)/shard_map/dot_general | solution.py:10
  195.3 3.6 %fusion = bf16[1,2048,384]{2,1,0:T(8,128)(2,1)} fusion(bf16[2048,384]{1,0:T(8,128)(2,1)S(1)} %collective-permute-done.28, bf16[1024,2048]{1,0:T(8,128)(2,1)S(1)} %copy-done.3, bf16[1024,384]{1,0:T(8,128)(2,1)S(1)} %copy-done.5), kind=kOutput, calls=%fused_computation.6 | convolution fusion | flops 1612972032 | bytes 8126464 | tf_op jit(solution)/shard_map/dot_general | solution.py:10
  (85 shorter events, 0.9 us)
Async XLA Ops:
  0.6 3.8 %collective-permute-start.3 = (bf16[2048,384]{1,0:T(8,128)(2,1)}, bf16[2048,384]{1,0:T(8,128)(2,1)S(1)}, u32[]{:S(2)}, u32[]{:S(2)}) collective-permute-start(bf16[2048,384]{1,0:T(8,128)(2,1)} %bitcast.57), channel_id=1, source_target_pairs={{0,1},{1,0},{2,3},{3,2},{4,5},{5,4},{6,7},{7,6},{8,9},{9,8},{10,11... | collective-permute-start | bytes 4718600 | tf_op jit(solution)/shard_map/ppermute | solution.py:339
  4.4 23.5 %copy-start = (bf16[2048,384]{1,0:T(8,128)(2,1)}, bf16[2048,384]{1,0:T(8,128)(2,1)S(1)}, u32[]{:S(2)}) copy-start(bf16[2048,384]{1,0:T(8,128)(2,1)S(1)} %collective-permute-done.3.refs_3_.refs_7_) | copy-start | bytes 4718596
  4.4 3.6 %collective-permute-start.4 = (bf16[2048,384]{1,0:T(8,128)(2,1)}, bf16[2048,384]{1,0:T(8,128)(2,1)S(1)}, u32[]{:S(2)}, u32[]{:S(2)}) collective-permute-start(bf16[2048,384]{1,0:T(8,128)(2,1)} %bitcast.66), channel_id=1, source_target_pairs={{0,1},{1,0},{2,3},{3,2},{4,5},{5,4},{6,7},{7,6},{8,9},{9,8},{10,11... | collective-permute-start | bytes 4718600 | tf_op jit(solution)/shard_map/ppermute | solution.py:339
  8.0 19.9 %copy-start.1 = (bf16[2048,384]{1,0:T(8,128)(2,1)}, bf16[2048,384]{1,0:T(8,128)(2,1)S(1)}, u32[]{:S(2)}) copy-start(bf16[2048,384]{1,0:T(8,128)(2,1)S(1)} %collective-permute-done.4.refs_5_.refs_9_) | copy-start | bytes 4718596
  8.0 32.4 %collective-permute-start.9 = (bf16[384,2048]{1,0:T(8,128)(2,1)}, bf16[384,2048]{1,0:T(8,128)(2,1)}, u32[]{:S(2)}, u32[]{:S(2)}) collective-permute-start(bf16[384,2048]{1,0:T(8,128)(2,1)} %bitcast.75), channel_id=1, source_target_pairs={{0,1},{1,0},{2,3},{3,2},{4,5},{5,4},{6,7},{7,6},{8,9},{9,8},{10,11... | collective-permute-start | bytes 4718600 | tf_op jit(solution)/shard_map/ppermute | solution.py:339
  8.4 17.8 %collective-permute-start.1 = (bf16[128,2048]{1,0:T(8,128)(2,1)}, bf16[128,2048]{1,0:T(8,128)(2,1)}, u32[]{:S(2)}, u32[]{:S(2)}) collective-permute-start(bf16[128,2048]{1,0:T(8,128)(2,1)} %refs_0_), channel_id=1, source_target_pairs={{0,4},{4,8},{8,12},{12,0},{1,5},{5,9},{9,13},{13,1},{2,6},{6,10},{... | collective-permute-start | bytes 1572872 | tf_op jit(solution)/shard_map/ppermute | solution.py:333
  11.1 16.8 %collective-permute-start.2 = (bf16[128,2048]{1,0:T(8,128)(2,1)}, bf16[128,2048]{1,0:T(8,128)(2,1)}, u32[]{:S(2)}, u32[]{:S(2)}) collective-permute-start(bf16[128,2048]{1,0:T(8,128)(2,1)} %refs_0_), channel_id=1, source_target_pairs={{0,2},{1,3},{2,0},{3,1},{4,6},{5,7},{6,4},{7,5},{8,10},{9,11},{10,... | collective-permute-start | bytes 1572872 | tf_op jit(solution)/shard_map/ppermute | solution.py:336
  16.0 22.1 %collective-permute-start = (bf16[128,2176]{1,0:T(8,128)(2,1)}, bf16[128,2176]{1,0:T(8,128)(2,1)}, u32[]{:S(2)}, u32[]{:S(2)}) collective-permute-start(bf16[128,2176]{1,0:T(8,128)(2,1)} %fusion.4.refs_0_), channel_id=1, source_target_pairs={{0,4},{4,8},{8,12},{12,0},{1,5},{5,9},{9,13},{13,1},{2,6},{6,10},{... | collective-permute-start | bytes 1671176 | tf_op jit(solution)/shard_map/ppermute | solution.py:333
  17.6 20.6 %collective-permute-start.8 = (bf16[128,2176]{1,0:T(8,128)(2,1)}, bf16[128,2176]{1,0:T(8,128)(2,1)}, u32[]{:S(2)}, u32[]{:S(2)}) collective-permute-start(bf16[128,2176]{1,0:T(8,128)(2,1)} %fusion.4.refs_0_), channel_id=1, source_target_pairs={{0,2},{1,3},{2,0},{3,1},{4,6},{5,7},{6,4},{7,5},{8,10},{9,11},{10,... | collective-permute-start | bytes 1671176 | tf_op jit(solution)/shard_map/ppermute | solution.py:336
  26.2 26.7 %collective-permute-start.10 = (bf16[128,2048]{1,0:T(8,128)(2,1)}, bf16[128,2048]{1,0:T(8,128)(2,1)}, u32[]{:S(2)}, u32[]{:S(2)}) collective-permute-start(bf16[128,2048]{1,0:T(8,128)(2,1)} %collective-permute-done.1.refs_0_), channel_id=1, source_target_pairs={{0,2},{1,3},{2,0},{3,1},{4,6},{5,7},{6,4},{7,5},{8,10},{9,11},{10,... | collective-permute-start | bytes 1572872 | tf_op jit(solution)/shard_map/ppermute | solution.py:336
  27.9 23.0 %collective-permute-start.7 = (bf16[128,2048]{1,0:T(8,128)(2,1)}, bf16[128,2048]{1,0:T(8,128)(2,1)}, u32[]{:S(2)}, u32[]{:S(2)}) collective-permute-start(bf16[128,2048]{1,0:T(8,128)(2,1)} %collective-permute-done.1.refs_0_), channel_id=1, source_target_pairs={{0,4},{4,8},{8,12},{12,0},{1,5},{5,9},{9,13},{13,1},{2,6},{6,10},{... | collective-permute-start | bytes 1572872 | tf_op jit(solution)/shard_map/ppermute | solution.py:333
  38.2 23.1 %collective-permute-start.6 = (bf16[128,2176]{1,0:T(8,128)(2,1)}, bf16[128,2176]{1,0:T(8,128)(2,1)S(1)}, u32[]{:S(2)}, u32[]{:S(2)}) collective-permute-start(bf16[128,2176]{1,0:T(8,128)(2,1)} %collective-permute-done.refs_0_), channel_id=1, source_target_pairs={{0,4},{4,8},{8,12},{12,0},{1,5},{5,9},{9,13},{13,1},{2,6},{6,10},{... | collective-permute-start | bytes 1671176 | tf_op jit(solution)/shard_map/ppermute | solution.py:333
  38.2 23.1 %collective-permute-start.5 = (bf16[128,2176]{1,0:T(8,128)(2,1)}, bf16[128,2176]{1,0:T(8,128)(2,1)S(1)}, u32[]{:S(2)}, u32[]{:S(2)}) collective-permute-start(bf16[128,2176]{1,0:T(8,128)(2,1)} %collective-permute-done.refs_0_), channel_id=1, source_target_pairs={{0,2},{1,3},{2,0},{3,1},{4,6},{5,7},{6,4},{7,5},{8,10},{9,11},{10,... | collective-permute-start | bytes 1671176 | tf_op jit(solution)/shard_map/ppermute | solution.py:336
  50.9 26.9 %collective-permute-start.16 = (bf16[128,2048]{1,0:T(8,128)(2,1)}, bf16[128,2048]{1,0:T(8,128)(2,1)S(1)}, u32[]{:S(2)}, u32[]{:S(2)}) collective-permute-start(bf16[128,2048]{1,0:T(8,128)(2,1)} %collective-permute-done.7.refs_0_), channel_id=1, source_target_pairs={{0,2},{1,3},{2,0},{3,1},{4,6},{5,7},{6,4},{7,5},{8,10},{9,11},{10,... | collective-permute-start | bytes 1572872 | tf_op jit(solution)/shard_map/ppermute | solution.py:336
  51.4 24.7 %collective-permute-start.15 = (bf16[128,2048]{1,0:T(8,128)(2,1)}, bf16[128,2048]{1,0:T(8,128)(2,1)S(1)}, u32[]{:S(2)}, u32[]{:S(2)}) collective-permute-start(bf16[128,2048]{1,0:T(8,128)(2,1)} %collective-permute-done.7.refs_0_), channel_id=1, source_target_pairs={{0,4},{4,8},{8,12},{12,0},{1,5},{5,9},{9,13},{13,1},{2,6},{6,10},{... | collective-permute-start | bytes 1572872 | tf_op jit(solution)/shard_map/ppermute | solution.py:333
  61.2 13.3 %copy-start.13 = (bf16[128,2176]{1,0:T(8,128)(2,1)}, bf16[128,2176]{1,0:T(8,128)(2,1)S(1)}, u32[]{:S(2)}) copy-start(bf16[128,2176]{1,0:T(8,128)(2,1)S(1)} %collective-permute-done.6.refs_0_) | copy-start | bytes 1671172
  61.2 24.0 %collective-permute-start.14 = (bf16[128,2176]{1,0:T(8,128)(2,1)S(1)}, bf16[128,2176]{1,0:T(8,128)(2,1)S(1)}, u32[]{:S(2)}, u32[]{:S(2)}) collective-permute-start(bf16[128,2176]{1,0:T(8,128)(2,1)S(1)} %collective-permute-done.6.refs_0_), channel_id=1, source_target_pairs={{0,4},{4,8},{8,12},{12,0},{1,5},{5,9},{9,13},{13,1},{2,6},{6,10},{... | collective-permute-start | bytes 1671176 | tf_op jit(solution)/shard_map/ppermute | solution.py:333
  61.2 0.9 copy-start.16
  62.1 12.4 %copy-start.20 = (f32[256,2]{1,0:T(8,128)S(1)}, f32[256,2]{1,0:T(8,128)}, u32[]{:S(2)}) copy-start(f32[256,2]{1,0:T(8,128)} %get-tuple-element.87) | copy-start | bytes 6148
  72.6 15.2 %collective-permute-start.11 = (bf16[128,2048]{1,0:T(8,128)(2,1)}, bf16[128,2048]{1,0:T(8,128)(2,1)}, u32[]{:S(2)}, u32[]{:S(2)}) collective-permute-start(bf16[128,2048]{1,0:T(8,128)(2,1)} %get-tuple-element.104), channel_id=1, source_target_pairs={{0,2},{1,3},{2,0},{3,1},{4,6},{5,7},{6,4},{7,5},{8,10},{9,11},{10,... | collective-permute-start | bytes 1572872 | tf_op jit(solution)/shard_map/ppermute | solution.py:336
  74.5 25.2 %collective-permute-start.13 = (bf16[128,2176]{1,0:T(8,128)(2,1)S(1)}, bf16[128,2176]{1,0:T(8,128)(2,1)S(1)}, u32[]{:S(2)}, u32[]{:S(2)}) collective-permute-start(bf16[128,2176]{1,0:T(8,128)(2,1)S(1)} %collective-permute-done.6.refs_0_), channel_id=1, source_target_pairs={{0,2},{1,3},{2,0},{3,1},{4,6},{5,7},{6,4},{7,5},{8,10},{9,11},{10,... | collective-permute-start | bytes 1671176 | tf_op jit(solution)/shard_map/ppermute | solution.py:336
  76.1 9.1 %copy-start.18 = (bf16[128,2048]{1,0:T(8,128)(2,1)}, bf16[128,2048]{1,0:T(8,128)(2,1)S(1)}, u32[]{:S(2)}) copy-start(bf16[128,2048]{1,0:T(8,128)(2,1)S(1)} %collective-permute-done.15.refs_0_) | copy-start | bytes 1572868
  76.1 37.7 %collective-permute-start.18 = (bf16[128,2048]{1,0:T(8,128)(2,1)S(1)}, bf16[128,2048]{1,0:T(8,128)(2,1)}, u32[]{:S(2)}, u32[]{:S(2)}) collective-permute-start(bf16[128,2048]{1,0:T(8,128)(2,1)S(1)} %collective-permute-done.15.refs_0_), channel_id=1, source_target_pairs={{0,2},{1,3},{2,0},{3,1},{4,6},{5,7},{6,4},{7,5},{8,10},{9,11},{10,... | collective-permute-start | bytes 1572872 | tf_op jit(solution)/shard_map/ppermute | solution.py:336
  77.8 0.8 copy-start.19
  78.6 9.3 %copy-start.10 = (f32[128,2048]{1,0:T(8,128)S(1)}, f32[128,2048]{1,0:T(8,128)}, u32[]{:S(2)}) copy-start(f32[128,2048]{1,0:T(8,128)} %get-tuple-element.103) | copy-start | bytes 3145732
  85.2 25.9 %copy-start.14 = (bf16[128,2176]{1,0:T(8,128)(2,1)}, bf16[128,2176]{1,0:T(8,128)(2,1)S(1)}, u32[]{:S(2)}) copy-start(bf16[128,2176]{1,0:T(8,128)(2,1)S(1)} %collective-permute-done.14.refs_0_) | copy-start | bytes 1671172
  85.2 37.7 %collective-permute-start.17 = (bf16[128,2176]{1,0:T(8,128)(2,1)S(1)}, bf16[128,2176]{1,0:T(8,128)(2,1)S(1)}, u32[]{:S(2)}, u32[]{:S(2)}) collective-permute-start(bf16[128,2176]{1,0:T(8,128)(2,1)S(1)} %collective-permute-done.14.refs_0_), channel_id=1, source_target_pairs={{0,2},{1,3},{2,0},{3,1},{4,6},{5,7},{6,4},{7,5},{8,10},{9,11},{10,... | collective-permute-start | bytes 1671176 | tf_op jit(solution)/shard_map/ppermute | solution.py:336
  89.8 59.4 %collective-permute-start.12 = (bf16[128,2048]{1,0:T(8,128)(2,1)}, bf16[128,2048]{1,0:T(8,128)(2,1)}, u32[]{:S(2)}, u32[]{:S(2)}) collective-permute-start(bf16[128,2048]{1,0:T(8,128)(2,1)} %add_convert_fusion.6), channel_id=1, source_target_pairs={{0,12},{4,0},{8,4},{12,8},{1,13},{5,1},{9,5},{13,9},{2,14},{6,2},{... | collective-permute-start | bytes 1572872 | tf_op jit(solution)/shard_map/ppermute | solution.py:333
  99.7 0.8 copy-start.17
  112.1 32.2 %collective-permute-start.19 = (bf16[128,2048]{1,0:T(8,128)(2,1)}, bf16[128,2048]{1,0:T(8,128)(2,1)S(1)}, u32[]{:S(2)}, u32[]{:S(2)}) collective-permute-start(bf16[128,2048]{1,0:T(8,128)(2,1)} %get-tuple-element.137), channel_id=1, source_target_pairs={{0,2},{1,3},{2,0},{3,1},{4,6},{5,7},{6,4},{7,5},{8,10},{9,11},{10,... | collective-permute-start | bytes 1572872 | tf_op jit(solution)/shard_map/ppermute | solution.py:336
  122.9 0.8 copy-start.15
  135.2 9.3 %collective-permute-start.24 = (bf16[4,128,2]{1,0,2:T(4,128)(2,1)S(1)}, bf16[4,128,2]{1,0,2:T(4,128)(2,1)S(1)}, u32[]{:S(2)}, u32[]{:S(2)}) collective-permute-start(bf16[4,128,2]{1,0,2:T(4,128)(2,1)S(1)} %get-tuple-element.158), channel_id=1, source_target_pairs={{0,2},{1,3},{2,0},{3,1},{4,6},{5,7},{6,4},{7,5},{8,10},{9,11},{10,... | collective-permute-start | bytes 6152 | tf_op jit(solution)/shard_map/ppermute | solution.py:336
  137.0 11.4 %collective-permute-start.21 = (bf16[128,2048]{1,0:T(8,128)(2,1)}, bf16[128,2048]{1,0:T(8,128)(2,1)S(1)}, u32[]{:S(2)}, u32[]{:S(2)}) collective-permute-start(bf16[128,2048]{1,0:T(8,128)(2,1)} %get-tuple-element.140), channel_id=1, source_target_pairs={{0,2},{1,3},{2,0},{3,1},{4,6},{5,7},{6,4},{7,5},{8,10},{9,11},{10,... | collective-permute-start | bytes 1572872 | tf_op jit(solution)/shard_map/ppermute | solution.py:336
  137.3 4.5 %copy-start.3 = (bf16[1024,2048]{1,0:T(8,128)(2,1)S(1)}, bf16[1024,2048]{1,0:T(8,128)(2,1)}, u32[]{:S(2)}) copy-start(bf16[1024,2048]{1,0:T(8,128)(2,1)} %get-tuple-element.145) | copy-start | bytes 12582916
  137.3 4.5 %copy-start.8 = (bf16[1024,384]{1,0:T(8,128)(2,1)S(1)}, bf16[1024,384]{1,0:T(8,128)(2,1)}, u32[]{:S(2)}) copy-start(bf16[1024,384]{1,0:T(8,128)(2,1)} %get-tuple-element.149) | copy-start | bytes 2359300
  141.8 46.9 %collective-permute-start.30 = (bf16[384,2048]{1,0:T(8,128)(2,1)S(1)}, bf16[384,2048]{1,0:T(8,128)(2,1)S(1)}, u32[]{:S(2)}, u32[]{:S(2)}) collective-permute-start(bf16[384,2048]{1,0:T(8,128)(2,1)S(1)} %convolution_convert_fusion), channel_id=1, source_target_pairs={{0,1},{1,0},{2,3},{3,2},{4,5},{5,4},{6,7},{7,6},{8,9},{9,8},{10,11... | collective-permute-start | bytes 4718600 | tf_op jit(solution)/shard_map/ppermute | solution.py:339
  141.8 2.5 %copy-start.11 = (f32[128,2048]{1,0:T(8,128)S(1)}, f32[128,2048]{1,0:T(8,128)}, u32[]{:S(2)}) copy-start(f32[128,2048]{1,0:T(8,128)} %get-tuple-element.136) | copy-start | bytes 3145732
  141.9 7.3 %copy-start.12 = (f32[128,2048]{1,0:T(8,128)S(1)}, f32[128,2048]{1,0:T(8,128)}, u32[]{:S(2)}) copy-start(f32[128,2048]{1,0:T(8,128)} %get-tuple-element.138) | copy-start | bytes 3145732
  144.3 7.2 %copy-start.22 = (bf16[128,2048]{1,0:T(8,128)(2,1)S(1)}, bf16[128,2048]{1,0:T(8,128)(2,1)}, u32[]{:S(2)}) copy-start(bf16[128,2048]{1,0:T(8,128)(2,1)} %get-tuple-element.139) | copy-start | bytes 1572868
  144.3 10.7 %copy-start.6 = (bf16[1024,384]{1,0:T(8,128)(2,1)S(1)}, bf16[1024,384]{1,0:T(8,128)(2,1)}, u32[]{:S(2)}) copy-start(bf16[1024,384]{1,0:T(8,128)(2,1)} %get-tuple-element.147) | copy-start | bytes 2359300
  144.5 6.9 %collective-permute-start.25 = (bf16[128,4]{0,1:T(4,128)(2,1)S(1)}, bf16[128,4]{0,1:T(4,128)(2,1)S(1)}, u32[]{:S(2)}, u32[]{:S(2)}) collective-permute-start(bf16[128,4]{0,1:T(4,128)(2,1)S(1)} %get-tuple-element.154), channel_id=1, source_target_pairs={{0,12},{4,0},{8,4},{12,8},{1,13},{5,1},{9,5},{13,9},{2,14},{6,2},{... | collective-permute-start | bytes 3080 | tf_op jit(solution)/shard_map/ppermute | solution.py:333
  148.4 5.4 %collective-permute-start.27 = (bf16[128,4]{0,1:T(4,128)(2,1)S(1)}, bf16[128,4]{0,1:T(4,128)(2,1)S(1)}, u32[]{:S(2)}, u32[]{:S(2)}) collective-permute-start(bf16[128,4]{0,1:T(4,128)(2,1)S(1)} %get-tuple-element.155), channel_id=1, source_target_pairs={{0,4},{4,8},{8,12},{12,0},{1,5},{5,9},{9,13},{13,1},{2,6},{6,10},{... | collective-permute-start | bytes 3080 | tf_op jit(solution)/shard_map/ppermute | solution.py:333
  148.4 5.4 %collective-permute-start.26 = (bf16[128,4]{0,1:T(4,128)(2,1)S(1)}, bf16[128,4]{0,1:T(4,128)(2,1)S(1)}, u32[]{:S(2)}, u32[]{:S(2)}) collective-permute-start(bf16[128,4]{0,1:T(4,128)(2,1)S(1)} %get-tuple-element.156), channel_id=1, source_target_pairs={{0,8},{4,12},{8,0},{12,4},{1,9},{5,13},{9,1},{13,5},{2,10},{6,14},... | collective-permute-start | bytes 3080 | tf_op jit(solution)/shard_map/ppermute | solution.py:333
  149.3 37.1 %collective-permute-start.20 = (bf16[128,2048]{1,0:T(8,128)(2,1)S(1)}, bf16[128,2048]{1,0:T(8,128)(2,1)S(1)}, u32[]{:S(2)}, u32[]{:S(2)}) collective-permute-start(bf16[128,2048]{1,0:T(8,128)(2,1)S(1)} %add_convert_fusion.5), channel_id=1, source_target_pairs={{0,8},{4,12},{8,0},{12,4},{1,9},{5,13},{9,1},{13,5},{2,10},{6,14},... | collective-permute-start | bytes 1572872 | tf_op jit(solution)/shard_map/ppermute | solution.py:333
  151.5 34.9 %collective-permute-start.23 = (bf16[128,2048]{1,0:T(8,128)(2,1)S(1)}, bf16[128,2048]{1,0:T(8,128)(2,1)S(1)}, u32[]{:S(2)}, u32[]{:S(2)}) collective-permute-start(bf16[128,2048]{1,0:T(8,128)(2,1)S(1)} %copy-done.22), channel_id=1, source_target_pairs={{0,2},{1,3},{2,0},{3,1},{4,6},{5,7},{6,4},{7,5},{8,10},{9,11},{10,... | collective-permute-start | bytes 1572872 | tf_op jit(solution)/shard_map/ppermute | solution.py:336
  153.7 37.9 %collective-permute-start.29 = (bf16[2048,384]{1,0:T(8,128)(2,1)S(1)}, bf16[2048,384]{1,0:T(8,128)(2,1)S(1)}, u32[]{:S(2)}, u32[]{:S(2)}) collective-permute-start(bf16[2048,384]{1,0:T(8,128)(2,1)S(1)} %convolution_convert_fusion.1), channel_id=1, source_target_pairs={{0,1},{1,0},{2,3},{3,2},{4,5},{5,4},{6,7},{7,6},{8,9},{9,8},{10,11... | collective-permute-start | bytes 4718600 | tf_op jit(solution)/shard_map/ppermute | solution.py:339
  153.7 32.6 %collective-permute-start.22 = (bf16[128,2048]{1,0:T(8,128)(2,1)S(1)}, bf16[128,2048]{1,0:T(8,128)(2,1)S(1)}, u32[]{:S(2)}, u32[]{:S(2)}) collective-permute-start(bf16[128,2048]{1,0:T(8,128)(2,1)S(1)} %add_convert_fusion.4), channel_id=1, source_target_pairs={{0,4},{4,8},{8,12},{12,0},{1,5},{5,9},{9,13},{13,1},{2,6},{6,10},{... | collective-permute-start | bytes 1572872 | tf_op jit(solution)/shard_map/ppermute | solution.py:333
  155.0 2.5 %copy-start.21 = (s32[128,8]{0,1:T(8,128)S(1)}, s32[128,8]{0,1:T(8,128)}, u32[]{:S(2)}) copy-start(s32[128,8]{0,1:T(8,128)} %param.9) | copy-start | bytes 12292
  155.0 31.4 %copy-start.9 = (f32[128,2048]{1,0:T(8,128)S(1)}, f32[128,2048]{1,0:T(8,128)}, u32[]{:S(2)}) copy-start(f32[128,2048]{1,0:T(8,128)} %get-tuple-element.142) | copy-start | bytes 3145732
  155.0 33.6 %copy-start.2 = (bf16[1024,2048]{1,0:T(8,128)(2,1)S(1)}, bf16[1024,2048]{1,0:T(8,128)(2,1)}, u32[]{:S(2)}) copy-start(bf16[1024,2048]{1,0:T(8,128)(2,1)} %get-tuple-element.151) | copy-start | bytes 12582916
  157.4 31.2 %copy-start.4 = (bf16[1024,384]{1,0:T(8,128)(2,1)S(1)}, bf16[1024,384]{1,0:T(8,128)(2,1)}, u32[]{:S(2)}) copy-start(bf16[1024,384]{1,0:T(8,128)(2,1)} %get-tuple-element.150) | copy-start | bytes 2359300
  186.4 9.0 %collective-permute-start.28 = (bf16[2048,384]{1,0:T(8,128)(2,1)S(1)}, bf16[2048,384]{1,0:T(8,128)(2,1)S(1)}, u32[]{:S(2)}, u32[]{:S(2)}) collective-permute-start(bf16[2048,384]{1,0:T(8,128)(2,1)S(1)} %convolution_convert_fusion.2), channel_id=1, source_target_pairs={{0,1},{1,0},{2,3},{3,2},{4,5},{5,4},{6,7},{7,6},{8,9},{9,8},{10,11... | collective-permute-start | bytes 4718600 | tf_op jit(solution)/shard_map/ppermute | solution.py:339
  188.6 3.1 %copy-start.7 = (bf16[1024,384]{1,0:T(8,128)(2,1)S(1)}, bf16[1024,384]{1,0:T(8,128)(2,1)}, u32[]{:S(2)}) copy-start(bf16[1024,384]{1,0:T(8,128)(2,1)} %get-tuple-element.148) | copy-start | bytes 2359300
  191.7 3.6 %copy-start.5 = (bf16[1024,384]{1,0:T(8,128)(2,1)S(1)}, bf16[1024,384]{1,0:T(8,128)(2,1)}, u32[]{:S(2)}) copy-start(bf16[1024,384]{1,0:T(8,128)(2,1)} %get-tuple-element.146) | copy-start | bytes 2359300

commit v2 on v0

--- a/solution.py
+++ b/solution.py
@@ -1,6 +1,8 @@
 import jax
 import jax.numpy as jnp
 from jax import lax
+from jax.experimental import pallas as pl
+from jax.experimental.pallas import tpu as pltpu
 from jax.sharding import PartitionSpec as P
 
 
@@ -38,7 +40,7 @@
     return (row_grad, gate_term.astype(jnp.bfloat16), grad_pre_gate, grad_pre_up, scaled_hidden)
 
 
-def per_device(tokens, cotangent, expert_ids, gates, w_gate, w_up, w_down):
+def dispatched(tokens, cotangent, expert_ids, gates, w_gate, w_up, w_down):
     token_count = tokens.shape[0]
     model_width = tokens.shape[1]
     top_count = expert_ids.shape[1]
@@ -113,6 +115,334 @@
         grad_w_down[None],
     )
 
+CORES = 2
+ROW_TILE = 1024
+FACTOR_ROWS = 128
+PRODUCT_TILE = 1024
+LANES = 128
+HBM = pl.BlockSpec(memory_space=pltpu.HBM)
+VMEM = pl.BlockSpec(memory_space=pltpu.VMEM)
+
+
+def wait_for(copies):
+    for copy in copies:
+        copy.wait()
+
+
+def tiles(count, size, body):
+    @pl.loop(0, count // size)
+    def _(i):
+        body(pl.ds(pl.multiple_of(i * size, size), size))
+
+
+def small_cost(rows, width):
+    return pl.CostEstimate(flops=rows * width, bytes_accessed=rows * width, transcendentals=0)
+
+
+def step_kernel(lines, step, token_count, model_width, f, *refs):
+    refs = list(refs)
+    take = lambda n: [refs.pop(0) for _ in range(n)]
+    blocks, (pick_ref,) = take(lines), take(1)
+    gate_w, up_w, down_w = take(CORES), take(CORES), take(CORES)
+    if step:
+        take(8)
+    row_own, row_far = take(2)
+    tok_all, cot_all = take(2)
+    factor_all = take(6)
+    tok, cot, wg, wu, wd, pre_gate, pre_up, back, gg, gu = take(10)
+    factors = take(6)
+    in_sem, out_sem = take(2)
+    rows = lines * token_count
+    room = row_own.shape[1] - model_width
+
+    slot = iter(range(64))
+    copy_in = lambda src, dst: pltpu.make_async_copy(src, dst, in_sem.at[next(slot)])
+    line_rows = [pl.ds(i * token_count, token_count) for i in range(lines)]
+    columns = [pl.ds(e * f, f) for e in range(CORES)]
+    padded = blocks[0].shape[1] - model_width
+    first = [copy_in(blocks[i].at[:, pl.ds(0, model_width)], tok.at[line_rows[i]]) for i in range(lines)]
+    first += [copy_in(gate_w[e], wg.at[:, columns[e]]) for e in range(CORES)]
+    second = [copy_in(up_w[e], wu.at[:, columns[e]]) for e in range(CORES)]
+    third = [copy_in(blocks[i].at[:, pl.ds(model_width, padded)], cot.at[line_rows[i]]) for i in range(lines)]
+    third += [copy_in(down_w[e], wd.at[columns[e]]) for e in range(CORES)]
+    for copy in first + second + third:
+        copy.start()
+
+    def gate_tile(c):
+        pre_gate[:, c] = jnp.dot(tok[...], wg[:, c], preferred_element_type=jnp.float32)
+
+    def up_tile(c):
+        pre_up[:, c] = jnp.dot(tok[...], wu[:, c], preferred_element_type=jnp.float32)
+
+    def back_tile(c):
+        back[:, c] = contract_cols(cot[:, :model_width], wd[c, :])
+
+    def factor_tile(line, r):
+        gate_cols = jnp.dot(cot[r, model_width:], pick_ref[...], preferred_element_type=jnp.float32)
+        sums = []
+        for e in range(CORES):
+            c = columns[e]
+            gate, up, bh = pre_gate[r, c], pre_up[r, c], back[r, c]
+            sigma = jax.nn.sigmoid(gate)
+            active = gate * sigma
+            prod = active * up
+            hidden = prod.astype(jnp.bfloat16)
+            sums.append(jnp.sum(hidden.astype(jnp.float32) * bh, axis=1, keepdims=True))
+            weight = gate_cols[:, e : e + 1]
+            scaled_back = weight * bh
+            grad_gate = (scaled_back * up * sigma * (1.0 + gate * (1.0 - sigma))).astype(jnp.bfloat16)
+            grad_up = (scaled_back * active).astype(jnp.bfloat16)
+            gg[r, c] = grad_gate
+            gu[r, c] = grad_up
+            factors[e][r, :] = grad_gate
+            factors[CORES + e][r, :] = grad_up
+            factors[2 * CORES + e][r, :] = (weight * prod).astype(jnp.bfloat16)
+        lane = lax.broadcasted_iota(jnp.int32, (sums[0].shape[0], room), 1)
+        place = CORES * (step * lines + line)
+        found = jnp.where(lane == place, sums[0], jnp.where(lane == place + 1, sums[1], 0.0))
+        return found
+
+    def own_terms(r):
+        row_own[r, model_width:] = factor_tile(0, r)
+
+    wait_for(first)
+    tiles(CORES * f, CORES * f, gate_tile)
+    wait_for(second)
+    tiles(CORES * f, CORES * f, up_tile)
+    wait_for(third)
+    tiles(CORES * f, CORES * f, back_tile)
+    tiles(token_count, FACTOR_ROWS, own_terms)
+    for i in range(1, lines):
+
+        @pl.loop(0, token_count // FACTOR_ROWS)
+        def _(j):
+            near = pl.ds(pl.multiple_of((i - 1) * token_count + j * FACTOR_ROWS, FACTOR_ROWS), FACTOR_ROWS)
+            r = pl.ds(pl.multiple_of(i * token_count + j * FACTOR_ROWS, FACTOR_ROWS), FACTOR_ROWS)
+            row_far[near, model_width:] = factor_tile(i, r).astype(jnp.bfloat16)
+
+    at = pl.ds(step * rows, rows)
+    outs = [(tok, tok_all), (cot.at[:, pl.ds(0, model_width)], cot_all)] + list(zip(factors, factor_all))
+    out_copies = [pltpu.make_async_copy(a, b.at[at], out_sem.at[i]) for i, (a, b) in enumerate(outs)]
+    for copy in out_copies:
+        copy.start()
+
+    def row_tile(c):
+        grad = contract_cols(gg[...], wg[c, :]) + contract_cols(gu[...], wu[c, :])
+        row_own[:, c] = grad[:token_count]
+        row_far[:, c] = grad[token_count:].astype(jnp.bfloat16)
+
+    tiles(model_width, ROW_TILE, row_tile)
+    wait_for(out_copies)
+
+
+def one_step(step, steps, blocks, pick, weights, held):
+    lines = len(blocks)
+    token_count = blocks[0].shape[0]
+    model_width, f = weights[0].shape
+    padded = blocks[0].shape[1] - model_width
+    rows, wide = lines * token_count, CORES * f
+    bf = jnp.bfloat16
+    ins = [*blocks, pick, *weights, *held]
+    whole = [jax.ShapeDtypeStruct((steps * rows, model_width), bf)] * 2
+    whole += [jax.ShapeDtypeStruct((steps * rows, f), bf)] * 6
+    out_shape = [
+        jax.ShapeDtypeStruct((token_count, padded), jnp.float32),
+        jax.ShapeDtypeStruct(((lines - 1) * token_count, padded), bf),
+        *whole,
+    ]
+    base = len(ins) - len(held)
+    scratch = [pltpu.VMEM((rows, model_width), bf), pltpu.VMEM((rows, padded), bf)]
+    scratch += [pltpu.VMEM((model_width, wide), bf)] * 2 + [pltpu.VMEM((wide, model_width), bf)]
+    scratch += [pltpu.VMEM((rows, wide), jnp.float32)] * 3 + [pltpu.VMEM((rows, wide), bf)] * 2
+    scratch += [pltpu.VMEM((rows, f), bf)] * 6
+    scratch += [pltpu.SemaphoreType.DMA((2 * lines + 3 * CORES,)), pltpu.SemaphoreType.DMA((8,))]
+    outs = pl.pallas_call(
+        lambda *refs: step_kernel(lines, step, token_count, model_width, f, *refs),
+        out_shape=out_shape,
+        in_specs=[HBM] * lines + [VMEM] + [HBM] * (len(ins) - lines - 1),
+        out_specs=[VMEM] * 2 + [HBM] * len(whole),
+        scratch_shapes=scratch,
+        input_output_aliases={base + i: 2 + i for i in range(len(held))},
+        compiler_params=pltpu.CompilerParams(vmem_limit_bytes=60 * 1024 * 1024),
+        cost_estimate=small_cost(rows, wide),
+    )(*ins)
+    return outs[0], outs[1], list(outs[2:])
+
+
+def products_kernel(last, *refs):
+    refs = list(refs)
+    take = lambda n: [refs.pop(0) for _ in range(n)]
+    tok_ref, cot_ref, gate_ref, up_ref, hid_ref = take(5)
+    (got_ref,) = take(1) if last else [None]
+    outs = take(3) if last else take(1)
+    tok, cot, pair, hid = take(4)
+    got = take(1)[0] if last else None
+    (sem,) = take(1)
+    f = hid.shape[1]
+    model_width = tok.shape[1]
+    slot = iter(range(16))
+    copy_in = lambda src, dst: pltpu.make_async_copy(src, dst, sem.at[next(slot)])
+    first = [copy_in(gate_ref, pair.at[:, pl.ds(0, f)]), copy_in(up_ref, pair.at[:, pl.ds(f, f)]), copy_in(tok_ref, tok)]
+    second = [copy_in(hid_ref, hid), copy_in(cot_ref, cot)]
+    if last:
+        first.append(copy_in(got_ref, got))
+    for copy in first + second:
+        copy.start()
+    wait_for(first)
+
+    def pair_tile(c):
+        both = contract_rows(pair[...], tok[:, c])
+        if last:
+            both = (both + got[: 2 * f, c].astype(jnp.float32)).astype(jnp.bfloat16).T
+            outs[0][c, :] = both[:, :f]
+            outs[1][c, :] = both[:, f:]
+        else:
+            outs[0][: 2 * f, c] = both.astype(jnp.bfloat16)
+
+    def down_tile(c):
+        down = contract_rows(hid[...], cot[:, c])
+        if last:
+            outs[2][:, c] = (down + got[2 * f :, c].astype(jnp.float32)).astype(jnp.bfloat16)
+        else:
+            outs[0][2 * f :, c] = down.astype(jnp.bfloat16)
+
+    tiles(model_width, PRODUCT_TILE, pair_tile)
+    wait_for(second)
+    tiles(model_width, PRODUCT_TILE, down_tile)
+
+
+def products(tok, cot, gate, up, hid, got=None):
+    rows, model_width = tok.shape
+    f = gate.shape[1]
+    bf = jnp.bfloat16
+    last = got is not None
+    ins = [tok, cot, gate, up, hid] + ([got] if last else [])
+    if last:
+        out_shape = [jax.ShapeDtypeStruct((model_width, f), bf)] * 2 + [jax.ShapeDtypeStruct((f, model_width), bf)]
+    else:
+        out_shape = [jax.ShapeDtypeStruct((3 * f, model_width), bf)]
+    scratch = [pltpu.VMEM((rows, model_width), bf)] * 2 + [pltpu.VMEM((rows, 2 * f), bf), pltpu.VMEM((rows, f), bf)]
+    if last:
+        scratch.append(pltpu.VMEM((3 * f, model_width), bf))
+    scratch.append(pltpu.SemaphoreType.DMA((7,)))
+    return pl.pallas_call(
+        lambda *refs: products_kernel(last, *refs),
+        out_shape=out_shape,
+        in_specs=[HBM] * len(ins),
+        out_specs=[VMEM] * len(out_shape),
+        scratch_shapes=scratch,
+        compiler_params=pltpu.CompilerParams(vmem_limit_bytes=60 * 1024 * 1024),
+        cost_estimate=small_cost(rows, 2 * f),
+    )(*ins)
+
+
+def gathered(tokens, cotangent, expert_ids, gates, w_gate, w_up, w_down):
+    z_count = lax.axis_size("expert")
+    dp_count = lax.axis_size("dp")
+    x_count = dp_count // CORES
+    expert_count = z_count * dp_count
+    token_count, model_width = tokens.shape
+    z_here = lax.axis_index("expert")
+    dp_here = lax.axis_index("dp")
+
+    def z_shift(value, step):
+        return lax.ppermute(value, "expert", [(i, (i + step) % z_count) for i in range(z_count)])
+
+    def x_shift(value, step):
+        return lax.ppermute(value, "dp", [(i, (i + CORES * step) % dp_count) for i in range(dp_count)])
+
+    def core_swap(value):
+        return lax.ppermute(value, "dp", [(i, i ^ 1) for i in range(dp_count)])
+
+    def after(value, *earlier):
+        return lax.optimization_barrier((value, *earlier))[0]
+
+    def across(block):
+        return [block] + [x_shift(block, s) for s in range(1, x_count)]
+
+    def home(d, carried=None):
+        line = row_own[d]
+        for s in range(1, x_count):
+            line = line + x_shift(row_far[d][s - 1], x_count - s).astype(jnp.float32)
+        if carried is not None:
+            line = line + carried.astype(jnp.float32)
+        return line.astype(jnp.bfloat16) if d else line
+
+    expert_range = jnp.arange(expert_count, dtype=jnp.int32)
+    chosen = expert_ids[:, :, None] == expert_range
+    gate_table = jnp.sum(jnp.where(chosen, gates[:, :, None].astype(jnp.float32), 0.0), axis=1).astype(jnp.bfloat16)
+    table_width = -(-expert_count // LANES) * LANES
+    gate_table = jnp.pad(gate_table, ((0, 0), (0, table_width - expert_count)))
+    block = jnp.concatenate([tokens, cotangent, gate_table], axis=1)
+    own_expert = z_here * dp_count + dp_here
+    mate_expert = z_here * dp_count + (dp_here ^ 1)
+    pick_row = jnp.arange(table_width, dtype=jnp.int32)[:, None]
+    pick_column = jnp.arange(LANES, dtype=jnp.int32)[None, :]
+    wanted = jnp.where(pick_column == 0, own_expert, mate_expert)
+    pick = ((pick_row == wanted) & (pick_column < CORES)).astype(jnp.bfloat16)
+
+    weights = []
+    for own in (w_gate[0], w_up[0], w_down[0]):
+        weights += [own, core_swap(own)]
+    ring = z_shift(block, 1)
+    pairs = [across(block)]
+    ring = after(ring, *weights[1::2])
+
+    row_own, row_far, held, carried = [], [], [], None
+    for d in range(z_count):
+        ready = []
+        if d + 1 < z_count:
+            pairs.append(across(ring))
+            following = z_shift(ring, 1) if d + 2 < z_count else None
+            ready = [ring]
+        elif z_count > 2:
+            row_own[1] = after(row_own[1], row_far[d - 1])
+            carried = home(1)
+            ready = [carried]
+        own, far, held = one_step(d, z_count, pairs[d], after(pick, *ready), weights, held)
+        if d + 1 < z_count:
+            far = after(far, pairs[d + 1][-1])
+        if d + 2 < z_count:
+            ring = after(following, far)
+        row_own.append(own)
+        row_far.append(far.reshape(x_count - 1, token_count, -1))
+
+    tok_all, cot_all, gate_own, gate_mate, up_own, up_mate, hid_own, hid_mate = held
+    row_far[0] = after(row_far[0], row_far[-1])
+    for d in range(2, z_count - 1):
+        row_own[d] = after(row_own[d], row_own[-1])
+        carried = home(d, z_shift(carried, 1))
+    if carried is not None:
+        hid_mate = after(hid_mate, carried)
+    mate = products(tok_all, cot_all, gate_mate, up_mate, hid_mate)[0]
+    got = core_swap(mate)
+    if z_count > 1:
+        row_own[-1] = after(row_own[-1], mate)
+        carried = home(z_count - 1, z_shift(carried, 1) if carried is not None else None)
+        got = after(got, carried)
+        carried = z_shift(carried, 1)
+    grads = products(tok_all, cot_all, gate_own, up_own, hid_own, got)
+
+    row_own[0] = after(row_own[0], grads[0])
+    total = home(0, carried)
+    tokens_grad = total[:, :model_width].astype(jnp.bfloat16)
+    back = total[:, model_width : model_width + expert_count]
+    column_ids = []
+    for d in range(z_count):
+        for s in range(x_count):
+            dp_from = (dp_here + CORES * s) % dp_count
+            first = ((z_here + d) % z_count) * dp_count
+            column_ids += [first + dp_from, first + (dp_from ^ 1)]
+    same = expert_ids[:, :, None] == jnp.stack(column_ids)
+    gates_grad = jnp.sum(jnp.where(same, back[:, None, :], 0.0), axis=2).astype(jnp.bfloat16)
+    return (tokens_grad, gates_grad, *[g[None] for g in grads])
+
+
+def per_device(tokens, cotangent, expert_ids, gates, w_gate, w_up, w_down):
+    expert_count = lax.axis_size("expert") * lax.axis_size("dp")
+    plan = gathered if expert_count <= 4 * expert_ids.shape[1] and lax.axis_size("dp") % CORES == 0 else dispatched
+    return plan(tokens, cotangent, expert_ids, gates, w_gate, w_up, w_down)
+
 
 def solution(mesh):
     placed = (

time: 365 us -> 182 us (0.50)
  the two profiles are of different devices: /device:TPU:11 before, /device:TPU:0 now
where the time goes in v2:
time: 182 us
  waiting for transfers between devices  98.1 us (54%)
  Pallas kernels  62.7 us (34%)
  starting transfers between devices  12.5 us (7%)
  other arithmetic  6.37 us (4%)
    ppermute x8, waiting for transfers between devices, x_shift(): lax.ppermute(value, 'dp', [(i, (i + CORES * step) % dp_count) for i in ra...  62.1 us
    pallas_call x4, Pallas kernels, one_step(): pl.pallas_call(lambda *refs: step_kernel(lines, step, token_count, model_...  40.8 us
    ppermute x6, waiting for transfers between devices, z_shift(): lax.ppermute(value, 'expert', [(i, (i + step) % z_count) for i in range(z...  36 us
    pallas_call x2, Pallas kernels, products(): pl.pallas_call(lambda *refs: products_kernel(last, *refs), out_shape=out_...  21.9 us
    ppermute x8, starting transfers between devices, x_shift(): lax.ppermute(value, 'dp', [(i, (i + CORES * step) % dp_count) for i in ra...  8.67 us
  transfers between devices with their start and end apart: 18, of which 11 were waited for; matrix products, arithmetic and copies ran while one was open for 3% of the time, Pallas kernels for 29%

profile of v2, /device:TPU:0, one launch (start us, length us, event | category | flops | bytes accessed | tf_op | source)
XLA Modules:
  0.0 181.9 jit_solution(18194350433625873877)
XLA Ops:
  0.6 0.5 collective-permute-start.2
  1.1 0.1 collective-permute-start.3
  1.2 0.4 collective-permute-start.4
  1.7 0.7 convert_element_type.46
  2.3 0.7 select_reduce_fusion.1
  3.0 0.1 copy.40
  3.2 2.3 %fusion.1.refs_0_ = bf16[128,4224]{1,0:T(8,128)(2,1)} fusion(bf16[128,16]{1,0:T(8,128)(2,1)S(1)} %copy.40, bf16[128,2048]{1,0:T(8,128)(2,1)} %param.8, bf16[128,2048]{1,0:T(8,128)(2,1)} %param.7), kind=kLoop, calls=%fused_computation.6 | loop fusion | flops 4325376 | bytes 2134016 | tf_op jit(solution)/shard_map/concatenate | solution.py:376
  5.4 2.7 %collective-permute-start.1 = (bf16[128,4224]{1,0:T(8,128)(2,1)}, bf16[128,4224]{1,0:T(8,128)(2,1)}, u32[]{:S(2)}, u32[]{:S(2)}) collective-permute-start(bf16[128,4224]{1,0:T(8,128)(2,1)} %fusion.1.refs_0_), channel_id=1, source_target_pairs={{0,4},{4,8},{8,12},{12,0},{1,5},{5,9},{9,13},{13,1},{2,6},{6,10},{... | collective-permute-start | bytes 3244040 | tf_op jit(solution)/shard_map/ppermute | solution.py:349
  8.1 1.5 collective-permute-start
  9.6 25.3 %collective-permute-done.1.refs_0_ = bf16[128,4224]{1,0:T(8,128)(2,1)} collective-permute-done((bf16[128,4224]{1,0:T(8,128)(2,1)}, bf16[128,4224]{1,0:T(8,128)(2,1)}, u32[]{:S(2)}, u32[]{:S(2)}) %collective-permute-start.1) | collective-permute-done | bytes 1081376 | tf_op jit(solution)/shard_map/ppermute | solution.py:349
  34.9 0.0 collective-permute-done.2.refs_4_
  34.9 0.0 collective-permute-done.3.refs_6_
  34.9 0.0 copy-start.1
  34.9 0.0 collective-permute-done.4.refs_8_
  34.9 1.6 collective-permute-start.6
  36.5 0.0 collective-permute-start.5
  36.5 0.6 fusion.3.refs_2_
  37.1 0.0 collective-permute-done.refs_1_
  37.1 10.2 %shard_map.110 = (f32[128,2176]{1,0:T(8,128)}, bf16[128,2176]{1,0:T(8,128)(2,1)}, bf16[1024,2048]{1,0:T(8,128)(2,1)}, bf16[1024,2048]{1,0:T(8,128)(2,1)}, bf16[1...) custom-call(bf16[128,4224]{1,0:T(8,128)(2,1)} %fusion.1.refs_0_, ...), custom_call_target="tpu_custom_call" | custom-call | flops 196608 | bytes 196608 | tf_op jit(solution)/shard_map/pallas_call | solution.py:259
  47.3 13.6 %collective-permute-done.6.refs_1_ = bf16[128,4224]{1,0:T(8,128)(2,1)} collective-permute-done((bf16[128,4224]{1,0:T(8,128)(2,1)}, bf16[128,4224]{1,0:T(8,128)(2,1)}, u32[]{:S(2)}, u32[]{:S(2)}) %collective-permute-start.6) | collective-permute-done | bytes 1081376 | tf_op jit(solution)/shard_map/ppermute | solution.py:352
  60.9 2.9 %collective-permute-done.5.refs_0_ = bf16[128,4224]{1,0:T(8,128)(2,1)} collective-permute-done((bf16[128,4224]{1,0:T(8,128)(2,1)}, bf16[128,4224]{1,0:T(8,128)(2,1)}, u32[]{:S(2)}, u32[]{:S(2)}) %collective-permute-start.5) | collective-permute-done | bytes 1081376 | tf_op jit(solution)/shard_map/ppermute | solution.py:349
  63.8 0.7 collective-permute-start.8
  64.5 0.0 collective-permute-start.7
  64.5 10.1 %shard_map.111 = (f32[128,2176]{1,0:T(8,128)}, bf16[128,2176]{1,0:T(8,128)(2,1)}, bf16[1024,2048]{1,0:T(8,128)(2,1)}, bf16[1024,2048]{1,0:T(8,128)(2,1)}, bf16[1...) custom-call(bf16[128,4224]{1,0:T(8,128)(2,1)} %collective-permute-do, ...), custom_call_target="tpu_custom_call", output_to_operand_aliasing={{2}: (9, {}), {3}: (10, {}), {4}: (11, {}), {5}: (12, {}), ... | custom-call | flops 196608 | bytes 196608 | tf_op jit(solution)/shard_map/pallas_call | solution.py:259
  74.6 13.7 %collective-permute-done.8.refs_1_ = bf16[128,4224]{1,0:T(8,128)(2,1)S(1)} collective-permute-done((bf16[128,4224]{1,0:T(8,128)(2,1)}, bf16[128,4224]{1,0:T(8,128)(2,1)S(1)}, u32[]{:S(2)}, u32[]{:S(2)}) %collective-permute-start.8) | collective-permute-done | bytes 1081376 | tf_op jit(solution)/shard_map/ppermute | solution.py:352
  88.3 0.8 collective-permute-start.10
  89.1 1.5 collective-permute-done.7.refs_0_
  90.6 1.2 collective-permute-start.9
  91.8 0.0 copy-done.8
  91.8 10.3 %shard_map.112 = (f32[128,2176]{1,0:T(8,128)}, bf16[128,2176]{1,0:T(8,128)(2,1)}, bf16[1024,2048]{1,0:T(8,128)(2,1)}, bf16[1024,2048]{1,0:T(8,128)(2,1)}, bf16[1...) custom-call(bf16[128,4224]{1,0:T(8,128)(2,1)} %collective-permute-do, ...), custom_call_target="tpu_custom_call", output_to_operand_aliasing={{2}: (9, {}), {3}: (10, {}), {4}: (11, {}), {5}: (12, {}), ... | custom-call | flops 196608 | bytes 196608 | tf_op jit(solution)/shard_map/pallas_call | solution.py:259
  102.1 0.0 copy-done.6
  102.1 2.0 %collective-permute-done.10 = bf16[128,2176]{1,0:T(8,128)(2,1)S(1)} collective-permute-done((bf16[128,2176]{1,0:T(8,128)(2,1)}, bf16[128,2176]{1,0:T(8,128)(2,1)S(1)}, u32[]{:S(2)}, u32[]{:S(2)}) %collective-permute-start.10) | collective-permute-done | bytes 557088 | tf_op jit(solution)/shard_map/ppermute | solution.py:352
  104.0 0.0 copy-done.5
  104.0 0.9 add_convert_fusion.2
  104.9 0.0 collective-permute-start.12
  104.9 19.3 %collective-permute-done.9.refs_1_ = bf16[128,4224]{1,0:T(8,128)(2,1)S(1)} collective-permute-done((bf16[128,4224]{1,0:T(8,128)(2,1)S(1)}, bf16[128,4224]{1,0:T(8,128)(2,1)S(1)}, u32[]{:S(2)}, u32[]{:S(2)}) %collective-permute-start.9) | collective-permute-done | bytes 1081376 | tf_op jit(solution)/shard_map/ppermute | solution.py:352
  124.2 0.8 collective-permute-start.11
  125.1 0.2 copy-done.7
  125.2 10.2 %shard_map.113 = (f32[128,2176]{1,0:T(8,128)}, bf16[128,2176]{1,0:T(8,128)(2,1)}, bf16[1024,2048]{1,0:T(8,128)(2,1)}, bf16[1024,2048]{1,0:T(8,128)(2,1)}, bf16[1...) custom-call(bf16[128,4224]{1,0:T(8,128)(2,1)} %copy-done.6, ...), custom_call_target="tpu_custom_call", output_to_operand_aliasing={{2}: (9, {}), {3}: (10, {}), {4}: (11, {}), {5}: (12, {}), ... | custom-call | flops 196608 | bytes 196608 | tf_op jit(solution)/shard_map/pallas_call | solution.py:259
  135.5 0.0 collective-permute-done.12
  135.5 0.2 collective-permute-done.11
  135.7 0.2 add_convert_fusion.1
  135.9 0.0 copy-start.11
  135.9 0.0 copy-start.10
  135.9 0.0 copy-start.4
  135.9 10.7 %shard_map.114 = bf16[1152,2048]{1,0:T(8,128)(2,1)} custom-call(bf16[1024,2048]{1,0:T(8,128)(2,1)} %get-tuple-element.100.refs_0_, bf16[1024,2048]{1,0:T(8,128)(2,1)} %get-tuple-element.101.refs_1_, bf16[1024,384]{1,0:T(8,128)(2,1)} %get-tuple-element.105.refs_2_, bf16[1024,384]{1,0:T(8,128)(2,1)} %get-tuple-element.106.refs_3_, ...), custom_call_target="tpu_custom_call" | custom-call | flops 786432 | bytes 786432 | tf_op jit(solution)/shard_map/pallas_call | solution.py:328
  146.6 0.1 collective-permute-start.13
  146.7 1.1 collective-permute-start.14
  147.8 0.0 collective-permute-start.15
  147.8 1.0 collective-permute-start.16
  148.8 13.4 %collective-permute-done.14 = bf16[128,2176]{1,0:T(8,128)(2,1)S(1)} collective-permute-done((bf16[128,2176]{1,0:T(8,128)(2,1)S(1)}, bf16[128,2176]{1,0:T(8,128)(2,1)S(1)}, u32[]{:S(2)}, u32[]{:S(2)}) %collective-permute-start.14) | collective-permute-done | bytes 557088 | tf_op jit(solution)/shard_map/ppermute | solution.py:352
  162.2 2.0 %collective-permute-done.15 = bf16[128,2176]{1,0:T(8,128)(2,1)S(1)} collective-permute-done((bf16[128,2176]{1,0:T(8,128)(2,1)S(1)}, bf16[128,2176]{1,0:T(8,128)(2,1)S(1)}, u32[]{:S(2)}, u32[]{:S(2)}) %collective-permute-start.15) | collective-permute-done | bytes 557088 | tf_op jit(solution)/shard_map/ppermute | solution.py:349
  164.2 0.0 copy-done.4
  164.2 0.2 add_convert_fusion
  164.4 0.1 collective-permute-start.17
  164.6 0.1 stack.67
  164.7 0.0 collective-permute-done.13.refs_5_
  164.7 11.2 %shard_map.115 = (bf16[2048,384]{1,0:T(8,128)(2,1)}, bf16[2048,384]{1,0:T(8,128)(2,1)}, bf16[384,2048]{1,0:T(8,128)(2,1)}) custom-call(bf16[1024,2048]{1,0:T(8,128)(2,1)} %get-tuple-element.100.refs_0_, bf16[1024,2048]{1,0:T(8,128)(2,1)} %get-tuple-element.101.refs_1_, bf16[1024,384]{1,0:T(8,128)(2,1)} %get-tuple-element.102.refs_2_, ...), custom_call_target="tpu_custom_call" | custom-call | flops 786432 | bytes 786432 | tf_op jit(solution)/shard_map/pallas_call | solution.py:328
  175.9 0.0 collective-permute-done.16
  175.9 4.2 %collective-permute-done.17 = bf16[128,2176]{1,0:T(8,128)(2,1)S(1)} collective-permute-done((bf16[128,2176]{1,0:T(8,128)(2,1)S(1)}, bf16[128,2176]{1,0:T(8,128)(2,1)S(1)}, u32[]{:S(2)}, u32[]{:S(2)}) %collective-permute-start.17) | collective-permute-done | bytes 557088 | tf_op jit(solution)/shard_map/ppermute | solution.py:349
  180.1 0.1 convert_add_fusion
  180.3 0.0 copy-start.9
  180.3 0.9 slice.12
  181.2 0.7 select_reduce_fusion
  (18 shorter events, 0.1 us)
Async XLA Ops:
  0.6 34.2 %collective-permute-start.2 = (bf16[2048,384]{1,0:T(8,128)(2,1)}, bf16[2048,384]{1,0:T(8,128)(2,1)S(1)}, u32[]{:S(2)}, u32[]{:S(2)}) collective-permute-start(bf16[2048,384]{1,0:T(8,128)(2,1)} %bitcast.24), channel_id=1, source_target_pairs={{0,1},{1,0},{2,3},{3,2},{4,5},{5,4},{6,7},{7,6},{8,9},{9,8},{10,11... | collective-permute-start | bytes 4718600 | tf_op jit(solution)/shard_map/ppermute | solution.py:355
  1.1 33.7 %collective-permute-start.3 = (bf16[2048,384]{1,0:T(8,128)(2,1)}, bf16[2048,384]{1,0:T(8,128)(2,1)S(1)}, u32[]{:S(2)}, u32[]{:S(2)}) collective-permute-start(bf16[2048,384]{1,0:T(8,128)(2,1)} %bitcast.29), channel_id=1, source_target_pairs={{0,1},{1,0},{2,3},{3,2},{4,5},{5,4},{6,7},{7,6},{8,9},{9,8},{10,11... | collective-permute-start | bytes 4718600 | tf_op jit(solution)/shard_map/ppermute | solution.py:355
  1.2 33.7 %collective-permute-start.4 = (bf16[384,2048]{1,0:T(8,128)(2,1)}, bf16[384,2048]{1,0:T(8,128)(2,1)}, u32[]{:S(2)}, u32[]{:S(2)}) collective-permute-start(bf16[384,2048]{1,0:T(8,128)(2,1)} %bitcast.34), channel_id=1, source_target_pairs={{0,1},{1,0},{2,3},{3,2},{4,5},{5,4},{6,7},{7,6},{8,9},{9,8},{10,11... | collective-permute-start | bytes 4718600 | tf_op jit(solution)/shard_map/ppermute | solution.py:355
  5.4 29.4 %collective-permute-start.1 = (bf16[128,4224]{1,0:T(8,128)(2,1)}, bf16[128,4224]{1,0:T(8,128)(2,1)}, u32[]{:S(2)}, u32[]{:S(2)}) collective-permute-start(bf16[128,4224]{1,0:T(8,128)(2,1)} %fusion.1.refs_0_), channel_id=1, source_target_pairs={{0,4},{4,8},{8,12},{12,0},{1,5},{5,9},{9,13},{13,1},{2,6},{6,10},{... | collective-permute-start | bytes 3244040 | tf_op jit(solution)/shard_map/ppermute | solution.py:349
  8.1 29.0 %collective-permute-start = (bf16[128,4224]{1,0:T(8,128)(2,1)}, bf16[128,4224]{1,0:T(8,128)(2,1)}, u32[]{:S(2)}, u32[]{:S(2)}) collective-permute-start(bf16[128,4224]{1,0:T(8,128)(2,1)} %fusion.1.refs_0_), channel_id=1, source_target_pairs={{0,2},{1,3},{2,0},{3,1},{4,6},{5,7},{6,4},{7,5},{8,10},{9,11},{10,... | collective-permute-start | bytes 3244040 | tf_op jit(solution)/shard_map/ppermute | solution.py:352
  34.9 2.2 %copy-start = (bf16[2048,384]{1,0:T(8,128)(2,1)}, bf16[2048,384]{1,0:T(8,128)(2,1)S(1)}, u32[]{:S(2)}) copy-start(bf16[2048,384]{1,0:T(8,128)(2,1)S(1)} %collective-permute-done.2.refs_4_) | copy-start | bytes 4718596
  34.9 2.2 %copy-start.1 = (bf16[2048,384]{1,0:T(8,128)(2,1)}, bf16[2048,384]{1,0:T(8,128)(2,1)S(1)}, u32[]{:S(2)}) copy-start(bf16[2048,384]{1,0:T(8,128)(2,1)S(1)} %collective-permute-done.3.refs_6_) | copy-start | bytes 4718596
  34.9 26.0 %collective-permute-start.6 = (bf16[128,4224]{1,0:T(8,128)(2,1)}, bf16[128,4224]{1,0:T(8,128)(2,1)}, u32[]{:S(2)}, u32[]{:S(2)}) collective-permute-start(bf16[128,4224]{1,0:T(8,128)(2,1)} %collective-permute-done.1.refs_0_), channel_id=1, source_target_pairs={{0,2},{1,3},{2,0},{3,1},{4,6},{5,7},{6,4},{7,5},{8,10},{9,11},{10,... | collective-permute-start | bytes 3244040 | tf_op jit(solution)/shard_map/ppermute | solution.py:352
  36.5 27.3 %collective-permute-start.5 = (bf16[128,4224]{1,0:T(8,128)(2,1)}, bf16[128,4224]{1,0:T(8,128)(2,1)}, u32[]{:S(2)}, u32[]{:S(2)}) collective-permute-start(bf16[128,4224]{1,0:T(8,128)(2,1)} %collective-permute-done.1.refs_0_), channel_id=1, source_target_pairs={{0,4},{4,8},{8,12},{12,0},{1,5},{5,9},{9,13},{13,1},{2,6},{6,10},{... | collective-permute-start | bytes 3244040 | tf_op jit(solution)/shard_map/ppermute | solution.py:349
  63.8 24.5 %collective-permute-start.8 = (bf16[128,4224]{1,0:T(8,128)(2,1)}, bf16[128,4224]{1,0:T(8,128)(2,1)S(1)}, u32[]{:S(2)}, u32[]{:S(2)}) collective-permute-start(bf16[128,4224]{1,0:T(8,128)(2,1)} %collective-permute-done.5.refs_0_), channel_id=1, source_target_pairs={{0,2},{1,3},{2,0},{3,1},{4,6},{5,7},{6,4},{7,5},{8,10},{9,11},{10,... | collective-permute-start | bytes 3244040 | tf_op jit(solution)/shard_map/ppermute | solution.py:352
  64.5 26.2 %collective-permute-start.7 = (bf16[128,4224]{1,0:T(8,128)(2,1)}, bf16[128,4224]{1,0:T(8,128)(2,1)S(1)}, u32[]{:S(2)}, u32[]{:S(2)}) collective-permute-start(bf16[128,4224]{1,0:T(8,128)(2,1)} %collective-permute-done.5.refs_0_), channel_id=1, source_target_pairs={{0,4},{4,8},{8,12},{12,0},{1,5},{5,9},{9,13},{13,1},{2,6},{6,10},{... | collective-permute-start | bytes 3244040 | tf_op jit(solution)/shard_map/ppermute | solution.py:349
  88.3 3.5 %copy-start.8 = (bf16[128,4224]{1,0:T(8,128)(2,1)}, bf16[128,4224]{1,0:T(8,128)(2,1)S(1)}, u32[]{:S(2)}) copy-start(bf16[128,4224]{1,0:T(8,128)(2,1)S(1)} %collective-permute-done.8.refs_1_) | copy-start | bytes 3244036
  88.3 15.8 %collective-permute-start.10 = (bf16[128,2176]{1,0:T(8,128)(2,1)}, bf16[128,2176]{1,0:T(8,128)(2,1)S(1)}, u32[]{:S(2)}, u32[]{:S(2)}) collective-permute-start(bf16[128,2176]{1,0:T(8,128)(2,1)} %get-tuple-element.79), channel_id=1, source_target_pairs={{0,2},{1,3},{2,0},{3,1},{4,6},{5,7},{6,4},{7,5},{8,10},{9,11},{10,... | collective-permute-start | bytes 1671176 | tf_op jit(solution)/shard_map/ppermute | solution.py:352
  90.6 11.5 %copy-start.6 = (bf16[128,4224]{1,0:T(8,128)(2,1)}, bf16[128,4224]{1,0:T(8,128)(2,1)S(1)}, u32[]{:S(2)}) copy-start(bf16[128,4224]{1,0:T(8,128)(2,1)S(1)} %collective-permute-done.7.refs_0_) | copy-start | bytes 3244036
  90.6 33.6 %collective-permute-start.9 = (bf16[128,4224]{1,0:T(8,128)(2,1)S(1)}, bf16[128,4224]{1,0:T(8,128)(2,1)S(1)}, u32[]{:S(2)}, u32[]{:S(2)}) collective-permute-start(bf16[128,4224]{1,0:T(8,128)(2,1)S(1)} %collective-permute-done.7.refs_0_), channel_id=1, source_target_pairs={{0,2},{1,3},{2,0},{3,1},{4,6},{5,7},{6,4},{7,5},{8,10},{9,11},{10,... | collective-permute-start | bytes 3244040 | tf_op jit(solution)/shard_map/ppermute | solution.py:352
  91.8 12.2 %copy-start.5 = (f32[128,2176]{1,0:T(8,128)S(1)}, f32[128,2176]{1,0:T(8,128)}, u32[]{:S(2)}) copy-start(f32[128,2176]{1,0:T(8,128)} %get-tuple-element.81) | copy-start | bytes 3342340
  104.9 30.5 %collective-permute-start.12 = (bf16[128,2176]{1,0:T(8,128)(2,1)}, bf16[128,2176]{1,0:T(8,128)(2,1)S(1)}, u32[]{:S(2)}, u32[]{:S(2)}) collective-permute-start(bf16[128,2176]{1,0:T(8,128)(2,1)} %add_convert_fusion.2), channel_id=1, source_target_pairs={{0,4},{4,8},{8,12},{12,0},{1,5},{5,9},{9,13},{13,1},{2,6},{6,10},{... | collective-permute-start | bytes 1671176 | tf_op jit(solution)/shard_map/ppermute | solution.py:349
  124.2 1.0 copy-start.7
  124.2 11.5 %collective-permute-start.11 = (bf16[128,2176]{1,0:T(8,128)(2,1)}, bf16[128,2176]{1,0:T(8,128)(2,1)S(1)}, u32[]{:S(2)}, u32[]{:S(2)}) collective-permute-start(bf16[128,2176]{1,0:T(8,128)(2,1)} %get-tuple-element.112), channel_id=1, source_target_pairs={{0,2},{1,3},{2,0},{3,1},{4,6},{5,7},{6,4},{7,5},{8,10},{9,11},{10,... | collective-permute-start | bytes 1671176 | tf_op jit(solution)/shard_map/ppermute | solution.py:352
  125.2 10.5 %copy-start.3 = (f32[128,2176]{1,0:T(8,128)S(1)}, f32[128,2176]{1,0:T(8,128)}, u32[]{:S(2)}) copy-start(f32[128,2176]{1,0:T(8,128)} %get-tuple-element.110) | copy-start | bytes 3342340
  135.9 10.8 %copy-start.11 = (bf16[128,2176]{1,0:T(8,128)(2,1)S(1)}, bf16[128,2176]{1,0:T(8,128)(2,1)}, u32[]{:S(2)}) copy-start(bf16[128,2176]{1,0:T(8,128)(2,1)} %get-tuple-element.115) | copy-start | bytes 1671172
  135.9 11.9 %copy-start.10 = (bf16[128,2176]{1,0:T(8,128)(2,1)S(1)}, bf16[128,2176]{1,0:T(8,128)(2,1)}, u32[]{:S(2)}) copy-start(bf16[128,2176]{1,0:T(8,128)(2,1)} %get-tuple-element.67) | copy-start | bytes 1671172
  135.9 28.3 %copy-start.4 = (f32[128,2176]{1,0:T(8,128)S(1)}, f32[128,2176]{1,0:T(8,128)}, u32[]{:S(2)}) copy-start(f32[128,2176]{1,0:T(8,128)} %get-tuple-element.114) | copy-start | bytes 3342340
  146.6 18.1 %collective-permute-start.13 = (bf16[1152,2048]{1,0:T(8,128)(2,1)}, bf16[1152,2048]{1,0:T(8,128)(2,1)}, u32[]{:S(2)}, u32[]{:S(2)}) collective-permute-start(bf16[1152,2048]{1,0:T(8,128)(2,1)} %shard_map.114), channel_id=1, source_target_pairs={{0,1},{1,0},{2,3},{3,2},{4,5},{5,4},{6,7},{7,6},{8,9},{9,8},{10,11... | collective-permute-start | bytes 14155784 | tf_op jit(solution)/shard_map/ppermute | solution.py:355
  146.7 15.5 %collective-permute-start.14 = (bf16[128,2176]{1,0:T(8,128)(2,1)S(1)}, bf16[128,2176]{1,0:T(8,128)(2,1)S(1)}, u32[]{:S(2)}, u32[]{:S(2)}) collective-permute-start(bf16[128,2176]{1,0:T(8,128)(2,1)S(1)} %copy-done.11), channel_id=1, source_target_pairs={{0,2},{1,3},{2,0},{3,1},{4,6},{5,7},{6,4},{7,5},{8,10},{9,11},{10,... | collective-permute-start | bytes 1671176 | tf_op jit(solution)/shard_map/ppermute | solution.py:352
  147.8 16.5 %collective-permute-start.15 = (bf16[128,2176]{1,0:T(8,128)(2,1)S(1)}, bf16[128,2176]{1,0:T(8,128)(2,1)S(1)}, u32[]{:S(2)}, u32[]{:S(2)}) collective-permute-start(bf16[128,2176]{1,0:T(8,128)(2,1)S(1)} %add_convert_fusion.1), channel_id=1, source_target_pairs={{0,4},{4,8},{8,12},{12,0},{1,5},{5,9},{9,13},{13,1},{2,6},{6,10},{... | collective-permute-start | bytes 1671176 | tf_op jit(solution)/shard_map/ppermute | solution.py:349
  147.8 28.1 %collective-permute-start.16 = (bf16[128,2176]{1,0:T(8,128)(2,1)S(1)}, bf16[128,2176]{1,0:T(8,128)(2,1)S(1)}, u32[]{:S(2)}, u32[]{:S(2)}) collective-permute-start(bf16[128,2176]{1,0:T(8,128)(2,1)S(1)} %copy-done.10), channel_id=1, source_target_pairs={{0,2},{1,3},{2,0},{3,1},{4,6},{5,7},{6,4},{7,5},{8,10},{9,11},{10,... | collective-permute-start | bytes 1671176 | tf_op jit(solution)/shard_map/ppermute | solution.py:352
  164.4 15.7 %collective-permute-start.17 = (bf16[128,2176]{1,0:T(8,128)(2,1)S(1)}, bf16[128,2176]{1,0:T(8,128)(2,1)S(1)}, u32[]{:S(2)}, u32[]{:S(2)}) collective-permute-start(bf16[128,2176]{1,0:T(8,128)(2,1)S(1)} %add_convert_fusion), channel_id=1, source_target_pairs={{0,4},{4,8},{8,12},{12,0},{1,5},{5,9},{9,13},{13,1},{2,6},{6,10},{... | collective-permute-start | bytes 1671176 | tf_op jit(solution)/shard_map/ppermute | solution.py:349
  164.7 15.5 %copy-start.2 = (f32[128,2176]{1,0:T(8,128)S(1)}, f32[128,2176]{1,0:T(8,128)}, u32[]{:S(2)}) copy-start(f32[128,2176]{1,0:T(8,128)} %get-tuple-element.118) | copy-start | bytes 3342340
  180.3 0.9 copy-start.9

commit v3 on v2

--- a/solution.py
+++ b/solution.py
@@ -135,20 +135,23 @@
         body(pl.ds(pl.multiple_of(i * size, size), size))
 
 
-def small_cost(rows, width):
-    return pl.CostEstimate(flops=rows * width, bytes_accessed=rows * width, transcendentals=0)
-
-
-def step_kernel(lines, step, token_count, model_width, f, *refs):
+def work_cost(rows, depth, width):
+    return pl.CostEstimate(flops=60 * rows * depth * width, bytes_accessed=2 * rows * depth, transcendentals=0)
+
+
+def step_kernel(lines, step, steps, passed, waited, token_count, model_width, f, *refs):
     refs = list(refs)
     take = lambda n: [refs.pop(0) for _ in range(n)]
     blocks, (pick_ref,) = take(lines), take(1)
     gate_w, up_w, down_w = take(CORES), take(CORES), take(CORES)
     if step:
         take(8)
+    take(passed + waited)
     row_own, row_far = take(2)
     tok_all, cot_all = take(2)
     factor_all = take(6)
+    mate_factors = take(1)[0] if step == steps - 1 else None
+    take(passed)
     tok, cot, wg, wu, wd, pre_gate, pre_up, back, gg, gu = take(10)
     factors = take(6)
     in_sem, out_sem = take(2)
@@ -222,7 +225,10 @@
 
     at = pl.ds(step * rows, rows)
     outs = [(tok, tok_all), (cot.at[:, pl.ds(0, model_width)], cot_all)] + list(zip(factors, factor_all))
-    out_copies = [pltpu.make_async_copy(a, b.at[at], out_sem.at[i]) for i, (a, b) in enumerate(outs)]
+    pairs = [(a, b.at[at]) for a, b in outs]
+    if mate_factors is not None:
+        pairs += [(factors[CORES * i + 1], mate_factors.at[:, pl.ds(i * f, f)]) for i in range(3)]
+    out_copies = [pltpu.make_async_copy(a, b, out_sem.at[i]) for i, (a, b) in enumerate(pairs)]
     for copy in out_copies:
         copy.start()
 
@@ -235,14 +241,14 @@
     wait_for(out_copies)
 
 
-def one_step(step, steps, blocks, pick, weights, held):
+def one_step(step, steps, blocks, pick, weights, held, passed=(), waited=()):
     lines = len(blocks)
     token_count = blocks[0].shape[0]
     model_width, f = weights[0].shape
     padded = blocks[0].shape[1] - model_width
     rows, wide = lines * token_count, CORES * f
     bf = jnp.bfloat16
-    ins = [*blocks, pick, *weights, *held]
+    ins = [*blocks, pick, *weights, *held, *passed, *waited]
     whole = [jax.ShapeDtypeStruct((steps * rows, model_width), bf)] * 2
     whole += [jax.ShapeDtypeStruct((steps * rows, f), bf)] * 6
     out_shape = [
@@ -250,89 +256,127 @@
         jax.ShapeDtypeStruct(((lines - 1) * token_count, padded), bf),
         *whole,
     ]
-    base = len(ins) - len(held)
+    if step == steps - 1:
+        out_shape.append(jax.ShapeDtypeStruct((rows, 3 * f), bf))
+    base = lines + 1 + len(weights)
+    aliases = {base + i: 2 + i for i in range(len(held))}
+    base += len(held)
+    aliases |= {base + i: len(out_shape) + i for i in range(len(passed))}
+    out_shape += [jax.ShapeDtypeStruct(value.shape, value.dtype) for value in passed]
     scratch = [pltpu.VMEM((rows, model_width), bf), pltpu.VMEM((rows, padded), bf)]
     scratch += [pltpu.VMEM((model_width, wide), bf)] * 2 + [pltpu.VMEM((wide, model_width), bf)]
     scratch += [pltpu.VMEM((rows, wide), jnp.float32)] * 3 + [pltpu.VMEM((rows, wide), bf)] * 2
     scratch += [pltpu.VMEM((rows, f), bf)] * 6
-    scratch += [pltpu.SemaphoreType.DMA((2 * lines + 3 * CORES,)), pltpu.SemaphoreType.DMA((8,))]
+    scratch += [pltpu.SemaphoreType.DMA((2 * lines + 3 * CORES,)), pltpu.SemaphoreType.DMA((11,))]
     outs = pl.pallas_call(
-        lambda *refs: step_kernel(lines, step, token_count, model_width, f, *refs),
+        lambda *refs: step_kernel(lines, step, steps, len(passed), len(waited), token_count, model_width, f, *refs),
         out_shape=out_shape,
         in_specs=[HBM] * lines + [VMEM] + [HBM] * (len(ins) - lines - 1),
-        out_specs=[VMEM] * 2 + [HBM] * len(whole),
+        out_specs=[VMEM] * 2 + [HBM] * (len(out_shape) - 2),
         scratch_shapes=scratch,
-        input_output_aliases={base + i: 2 + i for i in range(len(held))},
+        input_output_aliases=aliases,
         compiler_params=pltpu.CompilerParams(vmem_limit_bytes=60 * 1024 * 1024),
-        cost_estimate=small_cost(rows, wide),
+        cost_estimate=work_cost(rows, model_width, 5 * wide),
     )(*ins)
-    return outs[0], outs[1], list(outs[2:])
-
-
-def products_kernel(last, *refs):
-    refs = list(refs)
-    take = lambda n: [refs.pop(0) for _ in range(n)]
-    tok_ref, cot_ref, gate_ref, up_ref, hid_ref = take(5)
-    (got_ref,) = take(1) if last else [None]
-    outs = take(3) if last else take(1)
-    tok, cot, pair, hid = take(4)
-    got = take(1)[0] if last else None
-    (sem,) = take(1)
+    return outs[0], outs[1], list(outs[2:10]), outs[10:]
+
+
+def mate_kernel(count, tok_ref, cot_ref, gate_ref, up_ref, hid_ref, out, tok, cot, pair, hid, sem):
     f = hid.shape[1]
-    model_width = tok.shape[1]
-    slot = iter(range(16))
-    copy_in = lambda src, dst: pltpu.make_async_copy(src, dst, sem.at[next(slot)])
-    first = [copy_in(gate_ref, pair.at[:, pl.ds(0, f)]), copy_in(up_ref, pair.at[:, pl.ds(f, f)]), copy_in(tok_ref, tok)]
-    second = [copy_in(hid_ref, hid), copy_in(cot_ref, cot)]
-    if last:
-        first.append(copy_in(got_ref, got))
-    for copy in first + second:
+    top = pl.ds(0, count)
+    first = [(gate_ref, pair.at[:, pl.ds(0, f)]), (up_ref, pair.at[:, pl.ds(f, f)]), (tok_ref, tok)]
+    moves = first + [(hid_ref, hid), (cot_ref, cot)]
+    copies = [pltpu.make_async_copy(src.at[top], dst, sem.at[i]) for i, (src, dst) in enumerate(moves)]
+    for copy in copies:
         copy.start()
-    wait_for(first)
+
+    def pair_tile(c):
+        out[: 2 * f, c] = contract_rows(pair[...], tok[:, c]).astype(jnp.bfloat16)
+
+    def down_tile(c):
+        out[2 * f :, c] = contract_rows(hid[...], cot[:, c]).astype(jnp.bfloat16)
+
+    wait_for(copies[:3])
+    tiles(tok.shape[1], PRODUCT_TILE, pair_tile)
+    wait_for(copies[3:])
+    tiles(tok.shape[1], PRODUCT_TILE, down_tile)
+
+
+def mate_products(count, tok, cot, gate, up, hid):
+    model_width, f = tok.shape[1], gate.shape[1]
+    bf = jnp.bfloat16
+    return pl.pallas_call(
+        lambda *refs: mate_kernel(count, *refs),
+        out_shape=jax.ShapeDtypeStruct((3 * f, model_width), bf),
+        in_specs=[HBM] * 5,
+        out_specs=VMEM,
+        scratch_shapes=[
+            pltpu.VMEM((count, model_width), bf),
+            pltpu.VMEM((count, model_width), bf),
+            pltpu.VMEM((count, 2 * f), bf),
+            pltpu.VMEM((count, f), bf),
+            pltpu.SemaphoreType.DMA((5,)),
+        ],
+        compiler_params=pltpu.CompilerParams(vmem_limit_bytes=60 * 1024 * 1024),
+        cost_estimate=work_cost(count, model_width, 3 * f),
+    )(tok, cot, gate, up, hid)
+
+
+def finish_kernel(lines, tok_ref, cot_ref, gate_ref, up_ref, hid_ref, got_ref, factor_ref, *refs):
+    far_blocks = refs[:lines]
+    gate_out, up_out, down_out, tok, cot, pair, hid, got, sem = refs[lines + 1 :]
+    rows, model_width = tok_ref.shape
+    f = gate_ref.shape[1]
+    token_count = far_blocks[0].shape[0]
+    near, far = pl.ds(0, rows), pl.ds(rows, lines * token_count)
+    line = [pl.ds(rows + i * token_count, token_count) for i in range(lines)]
+    first = [(gate_ref, pair.at[near, pl.ds(0, f)]), (up_ref, pair.at[near, pl.ds(f, f)]), (tok_ref, tok.at[near])]
+    first += [(factor_ref.at[:, pl.ds(0, 2 * f)], pair.at[far]), (got_ref, got)]
+    first += [(far_blocks[i].at[:, pl.ds(0, model_width)], tok.at[line[i]]) for i in range(lines)]
+    second = [(hid_ref, hid.at[near]), (factor_ref.at[:, pl.ds(2 * f, f)], hid.at[far]), (cot_ref, cot.at[near])]
+    second += [(far_blocks[i].at[:, pl.ds(model_width, model_width)], cot.at[line[i]]) for i in range(lines)]
+    copies = [pltpu.make_async_copy(src, dst, sem.at[i]) for i, (src, dst) in enumerate(first + second)]
+    for copy in copies:
+        copy.start()
 
     def pair_tile(c):
         both = contract_rows(pair[...], tok[:, c])
-        if last:
-            both = (both + got[: 2 * f, c].astype(jnp.float32)).astype(jnp.bfloat16).T
-            outs[0][c, :] = both[:, :f]
-            outs[1][c, :] = both[:, f:]
-        else:
-            outs[0][: 2 * f, c] = both.astype(jnp.bfloat16)
+        both = (both + got[: 2 * f, c].astype(jnp.float32)).astype(jnp.bfloat16).T
+        gate_out[c, :] = both[:, :f]
+        up_out[c, :] = both[:, f:]
 
     def down_tile(c):
         down = contract_rows(hid[...], cot[:, c])
-        if last:
-            outs[2][:, c] = (down + got[2 * f :, c].astype(jnp.float32)).astype(jnp.bfloat16)
-        else:
-            outs[0][2 * f :, c] = down.astype(jnp.bfloat16)
-
+        down_out[:, c] = (down + got[2 * f :, c].astype(jnp.float32)).astype(jnp.bfloat16)
+
+    wait_for(copies[: len(first)])
     tiles(model_width, PRODUCT_TILE, pair_tile)
-    wait_for(second)
+    wait_for(copies[len(first) :])
     tiles(model_width, PRODUCT_TILE, down_tile)
 
 
-def products(tok, cot, gate, up, hid, got=None):
+def finish(tok, cot, gate, up, hid, got, far_factors, far_blocks, waited):
     rows, model_width = tok.shape
     f = gate.shape[1]
+    lines = len(far_blocks)
+    more = rows + lines * far_blocks[0].shape[0]
     bf = jnp.bfloat16
-    last = got is not None
-    ins = [tok, cot, gate, up, hid] + ([got] if last else [])
-    if last:
-        out_shape = [jax.ShapeDtypeStruct((model_width, f), bf)] * 2 + [jax.ShapeDtypeStruct((f, model_width), bf)]
-    else:
-        out_shape = [jax.ShapeDtypeStruct((3 * f, model_width), bf)]
-    scratch = [pltpu.VMEM((rows, model_width), bf)] * 2 + [pltpu.VMEM((rows, 2 * f), bf), pltpu.VMEM((rows, f), bf)]
-    if last:
-        scratch.append(pltpu.VMEM((3 * f, model_width), bf))
-    scratch.append(pltpu.SemaphoreType.DMA((7,)))
+    ins = [tok, cot, gate, up, hid, got, far_factors, *far_blocks, waited]
     return pl.pallas_call(
-        lambda *refs: products_kernel(last, *refs),
-        out_shape=out_shape,
+        lambda *refs: finish_kernel(lines, *refs),
+        out_shape=[jax.ShapeDtypeStruct((model_width, f), bf)] * 2 + [jax.ShapeDtypeStruct((f, model_width), bf)],
         in_specs=[HBM] * len(ins),
-        out_specs=[VMEM] * len(out_shape),
-        scratch_shapes=scratch,
+        out_specs=[VMEM] * 3,
+        scratch_shapes=[
+            pltpu.VMEM((more, model_width), bf),
+            pltpu.VMEM((more, model_width), bf),
+            pltpu.VMEM((more, 2 * f), bf),
+            pltpu.VMEM((more, f), bf),
+            pltpu.VMEM((3 * f, model_width), bf),
+            pltpu.SemaphoreType.DMA((8 + 2 * lines,)),
+        ],
         compiler_params=pltpu.CompilerParams(vmem_limit_bytes=60 * 1024 * 1024),
-        cost_estimate=small_cost(rows, 2 * f),
+        cost_estimate=work_cost(more, model_width, 3 * f),
     )(*ins)
 
 
@@ -388,18 +432,25 @@
     pairs = [across(block)]
     ring = after(ring, *weights[1::2])
 
-    row_own, row_far, held, carried = [], [], [], None
+    row_own, row_far, held, line = [], [], [], tokens
+    mate = jnp.zeros((3 * w_gate.shape[2], model_width), jnp.bfloat16)
     for d in range(z_count):
         ready = []
         if d + 1 < z_count:
             pairs.append(across(ring))
             following = z_shift(ring, 1) if d + 2 < z_count else None
             ready = [ring]
-        elif z_count > 2:
-            row_own[1] = after(row_own[1], row_far[d - 1])
-            carried = home(1)
-            ready = [carried]
-        own, far, held = one_step(d, z_count, pairs[d], after(pick, *ready), weights, held)
+        passed, waited = [], []
+        if d and d + 1 == z_count:
+            count = d * x_count * token_count
+            mate = mate_products(count, held[0], held[1], held[3], held[5], held[7])
+            passed, waited = ([row_far[0][0], row_own[1]] if d > 1 else [row_far[0][0]]), [mate]
+        outs = one_step(d, z_count, pairs[d], after(pick, *ready), weights, held, passed, waited)
+        own, far, held, mate_factors = outs
+        if len(mate_factors) > 1:
+            row_far[0] = mate_factors[1][None]
+        if len(mate_factors) > 2:
+            row_own[1] = mate_factors[2]
         if d + 1 < z_count:
             far = after(far, pairs[d + 1][-1])
         if d + 2 < z_count:
@@ -407,21 +458,14 @@
         row_own.append(own)
         row_far.append(far.reshape(x_count - 1, token_count, -1))
 
-    tok_all, cot_all, gate_own, gate_mate, up_own, up_mate, hid_own, hid_mate = held
-    row_far[0] = after(row_far[0], row_far[-1])
-    for d in range(2, z_count - 1):
-        row_own[d] = after(row_own[d], row_own[-1])
-        carried = home(d, z_shift(carried, 1))
-    if carried is not None:
-        hid_mate = after(hid_mate, carried)
-    mate = products(tok_all, cot_all, gate_mate, up_mate, hid_mate)[0]
+    carried = None
+    for d in range(1, z_count):
+        line = home(d, carried)
+        carried = z_shift(line, 1)
     got = core_swap(mate)
-    if z_count > 1:
-        row_own[-1] = after(row_own[-1], mate)
-        carried = home(z_count - 1, z_shift(carried, 1) if carried is not None else None)
-        got = after(got, carried)
-        carried = z_shift(carried, 1)
-    grads = products(tok_all, cot_all, gate_own, up_own, hid_own, got)
+    far_blocks = [core_swap(block) for block in pairs[-1]]
+    far_factors = core_swap(mate_factors[0])
+    grads = finish(held[0], held[1], held[2], held[4], held[6], got, far_factors, far_blocks, line)
 
     row_own[0] = after(row_own[0], grads[0])
     total = home(0, carried)

time: 182 us -> 175 us (0.962)
  waiting for transfers between devices: 98.1 us -> 86 us
  starting transfers between devices: 12.5 us -> 14.8 us
    ppermute x8, waiting for transfers between devices: 62.1 us -> 45.7 us  [x_shift(): lax.ppermute(value, 'dp', [(i, (i + CORES * step) % dp_count) for i in ra...]
    ppermute x6, waiting for transfers between devices: 36 us -> 40.3 us  [z_shift(): lax.ppermute(value, 'expert', [(i, (i + step) % z_count) for i in range(z...]
  transfers between devices with their start and end apart: 18 -> 21, of which waited for: 11 -> 11; matrix products, arithmetic and copies ran while one was open for 3% -> 4% of each run, Pallas kernels for 29% -> 36%
where the time goes in v3:
time: 175 us
  waiting for transfers between devices  86 us (49%)
  Pallas kernels  62.5 us (36%)
  starting transfers between devices  14.8 us (8%)
  other arithmetic  8.09 us (5%)
  local copies, waits for them, and re-layouts  2.53 us (1%)
    ppermute x8, waiting for transfers between devices, x_shift(): lax.ppermute(value, 'dp', [(i, (i + CORES * step) % dp_count) for i in ra...  45.7 us
    pallas_call x4, Pallas kernels, one_step(): pl.pallas_call(lambda *refs: step_kernel(lines, step, steps, len(passed),...  40.9 us
    ppermute x6, waiting for transfers between devices, z_shift(): lax.ppermute(value, 'expert', [(i, (i + step) % z_count) for i in range(z...  40.3 us
    pallas_call x1, Pallas kernels, finish(): pl.pallas_call(lambda *refs: finish_kernel(lines, *refs), out_shape=[jax....  12.7 us
    ppermute x8, starting transfers between devices, x_shift(): lax.ppermute(value, 'dp', [(i, (i + CORES * step) % dp_count) for i in ra...  10.3 us
    pallas_call x1, Pallas kernels, mate_products(): pl.pallas_call(lambda *refs: mate_kernel(count, *refs), out_shape=jax.Sha...  8.94 us
  transfers between devices with their start and end apart: 21, of which 11 were waited for; matrix products, arithmetic and copies ran while one was open for 4% of the time, Pallas kernels for 36%

profile of v3, /device:TPU:0, one launch (start us, length us, event | category | flops | bytes accessed | tf_op | source)
XLA Modules:
  0.0 174.9 jit_solution(2381374798365169640)
XLA Ops:
  0.6 0.5 collective-permute-start.2
  1.1 0.1 collective-permute-start.3
  1.2 0.4 collective-permute-start.4
  1.7 0.7 convert_element_type.46
  2.3 0.7 select_reduce_fusion.1
  3.0 0.1 copy.42
  3.2 1.3 fusion.1.refs_0_
  4.5 0.0 copy-start.3
  4.5 2.7 %collective-permute-start.1 = (bf16[128,4224]{1,0:T(8,128)(2,1)S(1)}, bf16[128,4224]{1,0:T(8,128)(2,1)S(1)}, u32[]{:S(2)}, u32[]{:S(2)}) collective-permute-start(bf16[128,4224]{1,0:T(8,128)(2,1)S(1)} %fusion.1.refs_0_), channel_id=1, source_target_pairs={{0,4},{4,8},{8,12},{12,0},{1,5},{5,9},{9,13},{13,1},{2,6},{6,10},{... | collective-permute-start | bytes 3244040 | tf_op jit(solution)/shard_map/ppermute | solution.py:393
  7.2 1.5 collective-permute-start
  8.7 0.6 fusion.3.refs_2_
  9.3 24.3 %collective-permute-done.1.refs_0_ = bf16[128,4224]{1,0:T(8,128)(2,1)S(1)} collective-permute-done((bf16[128,4224]{1,0:T(8,128)(2,1)S(1)}, bf16[128,4224]{1,0:T(8,128)(2,1)S(1)}, u32[]{:S(2)}, u32[]{:S(2)}) %collective-permute-start.1) | collective-permute-done | bytes 1081376 | tf_op jit(solution)/shard_map/ppermute | solution.py:393
  33.7 0.0 collective-permute-done.2.refs_4_
  33.7 0.0 collective-permute-done.3.refs_6_
  33.7 0.0 collective-permute-done.4.refs_8_
  33.7 1.6 collective-permute-start.6
  35.2 0.0 collective-permute-start.5
  35.2 0.0 collective-permute-done.refs_1_
  35.2 10.2 %shard_map.110 = (f32[128,2176]{1,0:T(8,128)}, bf16[128,2176]{1,0:T(8,128)(2,1)}, bf16[1024,2048]{1,0:T(8,128)(2,1)}, bf16[1024,2048]{1,0:T(8,128)(2,1)}, bf16[1...) custom-call(bf16[128,4224]{1,0:T(8,128)(2,1)} %copy-done.3, ...), custom_call_target="tpu_custom_call" | custom-call | flops 120795955200 | bytes 1048576 | tf_op jit(solution)/shard_map/pallas_call | solution.py:271
  45.5 14.0 %collective-permute-done.6.refs_1_ = bf16[128,4224]{1,0:T(8,128)(2,1)} collective-permute-done((bf16[128,4224]{1,0:T(8,128)(2,1)S(1)}, bf16[128,4224]{1,0:T(8,128)(2,1)}, u32[]{:S(2)}, u32[]{:S(2)}) %collective-permute-start.6) | collective-permute-done | bytes 1081376 | tf_op jit(solution)/shard_map/ppermute | solution.py:396
  59.5 2.8 %collective-permute-done.5.refs_0_ = bf16[128,4224]{1,0:T(8,128)(2,1)S(1)} collective-permute-done((bf16[128,4224]{1,0:T(8,128)(2,1)S(1)}, bf16[128,4224]{1,0:T(8,128)(2,1)S(1)}, u32[]{:S(2)}, u32[]{:S(2)}) %collective-permute-start.5) | collective-permute-done | bytes 1081376 | tf_op jit(solution)/shard_map/ppermute | solution.py:393
  62.2 0.7 collective-permute-start.8
  62.9 0.0 collective-permute-start.7
  62.9 10.3 %shard_map.111 = (f32[128,2176]{1,0:T(8,128)}, bf16[128,2176]{1,0:T(8,128)(2,1)}, bf16[1024,2048]{1,0:T(8,128)(2,1)}, bf16[1024,2048]{1,0:T(8,128)(2,1)}, bf16[1...) custom-call(bf16[128,4224]{1,0:T(8,128)(2,1)} %copy-done.6, ...), custom_call_target="tpu_custom_call", output_to_operand_aliasing={{2}: (9, {}), {3}: (10, {}), {4}: (11, {}), {5}: (12, {}), ... | custom-call | flops 120795955200 | bytes 1048576 | tf_op jit(solution)/shard_map/pallas_call | solution.py:271
  73.3 0.0 copy-done.7
  73.3 13.2 %collective-permute-done.8.refs_1_ = bf16[128,4224]{1,0:T(8,128)(2,1)S(1)} collective-permute-done((bf16[128,4224]{1,0:T(8,128)(2,1)S(1)}, bf16[128,4224]{1,0:T(8,128)(2,1)S(1)}, u32[]{:S(2)}, u32[]{:S(2)}) %collective-permute-start.8) | collective-permute-done | bytes 1081376 | tf_op jit(solution)/shard_map/ppermute | solution.py:396
  86.5 2.5 %collective-permute-done.7.refs_0_ = bf16[128,4224]{1,0:T(8,128)(2,1)} collective-permute-done((bf16[128,4224]{1,0:T(8,128)(2,1)S(1)}, bf16[128,4224]{1,0:T(8,128)(2,1)}, u32[]{:S(2)}, u32[]{:S(2)}) %collective-permute-start.7) | collective-permute-done | bytes 1081376 | tf_op jit(solution)/shard_map/ppermute | solution.py:393
  89.0 1.2 collective-permute-start.9
  90.1 0.8 collective-permute-start.16
  91.0 10.2 %shard_map.112 = (f32[128,2176]{1,0:T(8,128)}, bf16[128,2176]{1,0:T(8,128)(2,1)}, bf16[1024,2048]{1,0:T(8,128)(2,1)}, bf16[1024,2048]{1,0:T(8,128)(2,1)}, bf16[1...) custom-call(bf16[128,4224]{1,0:T(8,128)(2,1)} %copy-done.7, ...), custom_call_target="tpu_custom_call", output_to_operand_aliasing={{2}: (9, {}), {3}: (10, {}), {4}: (11, {}), {5}: (12, {}), ... | custom-call | flops 120795955200 | bytes 1048576 | tf_op jit(solution)/shard_map/pallas_call | solution.py:271
  101.2 8.9 %shard_map.113.refs_19_ = bf16[1152,2048]{1,0:T(8,128)(2,1)} custom-call(bf16[1024,2048]{1,0:T(8,128)(2,1)} %get-tuple-element.85.refs_0_.refs_9_, bf16[1024,2048]{1,0:T(8,128)(2,1)} %get-tuple-element.86.refs_1_.refs_10_, bf16[1024,384]{1,0:T(8,128)(2,1)} %get-tuple-element.88.refs_2_.refs_12_, bf16[1024,384]{1,0:T(8,128)(2,1)} %get-tuple-element.90.refs_3_.refs_14_, ...), custom_call_target="tpu_custom_call" | custom-call | flops 108716359680 | bytes 3145728 | tf_op jit(solution)/shard_map/pallas_call | solution.py:308
  110.1 0.1 collective-permute-start.10
  110.2 5.9 %collective-permute-done.9.refs_1_ = bf16[128,4224]{1,0:T(8,128)(2,1)} collective-permute-done((bf16[128,4224]{1,0:T(8,128)(2,1)}, bf16[128,4224]{1,0:T(8,128)(2,1)}, u32[]{:S(2)}, u32[]{:S(2)}) %collective-permute-start.9) | collective-permute-done | bytes 1081376 | tf_op jit(solution)/shard_map/ppermute | solution.py:396
  116.1 1.2 collective-permute-start.15
  117.3 10.2 %shard_map.114 = (f32[128,2176]{1,0:T(8,128)}, bf16[128,2176]{1,0:T(8,128)(2,1)}, bf16[1024,2048]{1,0:T(8,128)(2,1)}, bf16[1024,2048]{1,0:T(8,128)(2,1)}, bf16[1...) custom-call(bf16[128,4224]{1,0:T(8,128)(2,1)} %collective-permute-do, ...), custom_call_target="tpu_custom_call", output_to_operand_aliasing={{2}: (9, {}), {3}: (10, {}), {4}: (11, {}), {5}: (12, {}), ... | custom-call | flops 120795955200 | bytes 1048576 | tf_op jit(solution)/shard_map/pallas_call | solution.py:271
  127.5 0.6 collective-permute-done.16
  128.0 1.6 add_convert_fusion.2
  129.6 0.1 collective-permute-start.17
  129.7 1.3 collective-permute-start.14
  130.9 8.9 %collective-permute-done.15 = bf16[128,2176]{1,0:T(8,128)(2,1)S(1)} collective-permute-done((bf16[128,2176]{1,0:T(8,128)(2,1)S(1)}, bf16[128,2176]{1,0:T(8,128)(2,1)S(1)}, u32[]{:S(2)}, u32[]{:S(2)}) %collective-permute-start.15) | collective-permute-done | bytes 557088 | tf_op jit(solution)/shard_map/ppermute | solution.py:396
  139.8 3.7 %collective-permute-done.17 = bf16[128,2176]{1,0:T(8,128)(2,1)S(1)} collective-permute-done((bf16[128,2176]{1,0:T(8,128)(2,1)S(1)}, bf16[128,2176]{1,0:T(8,128)(2,1)S(1)}, u32[]{:S(2)}, u32[]{:S(2)}) %collective-permute-start.17) | collective-permute-done | bytes 557088 | tf_op jit(solution)/shard_map/ppermute | solution.py:393
  143.6 0.2 add_convert_fusion.1
  143.8 0.1 collective-permute-start.18
  143.8 0.1 collective-permute-start.12
  143.9 0.5 collective-permute-start.13
  144.4 0.6 stack.67
  145.0 3.2 %collective-permute-done.14 = bf16[128,2176]{1,0:T(8,128)(2,1)S(1)} collective-permute-done((bf16[128,2176]{1,0:T(8,128)(2,1)}, bf16[128,2176]{1,0:T(8,128)(2,1)S(1)}, u32[]{:S(2)}, u32[]{:S(2)}) %collective-permute-start.14) | collective-permute-done | bytes 557088 | tf_op jit(solution)/shard_map/ppermute | solution.py:396
  148.2 0.0 collective-permute-start.11
  148.2 7.0 %collective-permute-done.18 = bf16[128,2176]{1,0:T(8,128)(2,1)S(1)} collective-permute-done((bf16[128,2176]{1,0:T(8,128)(2,1)S(1)}, bf16[128,2176]{1,0:T(8,128)(2,1)S(1)}, u32[]{:S(2)}, u32[]{:S(2)}) %collective-permute-start.18) | collective-permute-done | bytes 557088 | tf_op jit(solution)/shard_map/ppermute | solution.py:393
  155.2 2.1 %collective-permute-start.19 = (bf16[128,2176]{1,0:T(8,128)(2,1)}, bf16[128,2176]{1,0:T(8,128)(2,1)}, u32[]{:S(2)}, u32[]{:S(2)}) collective-permute-start(bf16[128,2176]{1,0:T(8,128)(2,1)} %get-tuple-element.108), channel_id=1, source_target_pairs={{0,2},{1,3},{2,0},{3,1},{4,6},{5,7},{6,4},{7,5},{8,10},{9,11},{10,... | collective-permute-start | bytes 1671176 | tf_op jit(solution)/shard_map/ppermute | solution.py:396
  157.3 1.0 add_convert_fusion.refs_9_
  158.3 0.0 collective-permute-done.12.refs_7_
  158.3 0.0 collective-permute-start.20
  158.3 0.0 collective-permute-done.11.refs_6_
  158.3 0.0 collective-permute-done.13.refs_8_
  158.3 0.0 collective-permute-done.10.refs_5_
  158.3 0.8 copy-done.10
  159.2 12.7 %shard_map.115 = (bf16[2048,384]{1,0:T(8,128)(2,1)}, bf16[2048,384]{1,0:T(8,128)(2,1)}, bf16[384,2048]{1,0:T(8,128)(2,1)}) custom-call(bf16[1024,2048]{1,0:T(8,128)(2,1)} %get-tuple-element.94.refs_0_, bf16[1024,2048]{1,0:T(8,128)(2,1)} %get-tuple-element.95.refs_1_, bf16[1024,384]{1,0:T(8,128)(2,1)} %get-tuple-element.96.refs_2_, ...), custom_call_target="tpu_custom_call" | custom-call | flops 181193932800 | bytes 5242880 | tf_op jit(solution)/shard_map/pallas_call | solution.py:365
  171.9 0.0 collective-permute-done.19
  171.9 0.0 collective-permute-done.20
  171.9 1.4 convert_add_fusion
  173.3 0.0 copy-start.4
  173.3 0.9 slice.12
  174.2 0.7 select_reduce_fusion
  (24 shorter events, 0.1 us)
Async XLA Ops:
  0.6 33.0 %collective-permute-start.2 = (bf16[2048,384]{1,0:T(8,128)(2,1)}, bf16[2048,384]{1,0:T(8,128)(2,1)}, u32[]{:S(2)}, u32[]{:S(2)}) collective-permute-start(bf16[2048,384]{1,0:T(8,128)(2,1)} %bitcast.22), channel_id=1, source_target_pairs={{0,1},{1,0},{2,3},{3,2},{4,5},{5,4},{6,7},{7,6},{8,9},{9,8},{10,11... | collective-permute-start | bytes 4718600 | tf_op jit(solution)/shard_map/ppermute | solution.py:399
  1.1 32.5 %collective-permute-start.3 = (bf16[2048,384]{1,0:T(8,128)(2,1)}, bf16[2048,384]{1,0:T(8,128)(2,1)}, u32[]{:S(2)}, u32[]{:S(2)}) collective-permute-start(bf16[2048,384]{1,0:T(8,128)(2,1)} %bitcast.27), channel_id=1, source_target_pairs={{0,1},{1,0},{2,3},{3,2},{4,5},{5,4},{6,7},{7,6},{8,9},{9,8},{10,11... | collective-permute-start | bytes 4718600 | tf_op jit(solution)/shard_map/ppermute | solution.py:399
  1.2 32.4 %collective-permute-start.4 = (bf16[384,2048]{1,0:T(8,128)(2,1)}, bf16[384,2048]{1,0:T(8,128)(2,1)}, u32[]{:S(2)}, u32[]{:S(2)}) collective-permute-start(bf16[384,2048]{1,0:T(8,128)(2,1)} %bitcast.32), channel_id=1, source_target_pairs={{0,1},{1,0},{2,3},{3,2},{4,5},{5,4},{6,7},{7,6},{8,9},{9,8},{10,11... | collective-permute-start | bytes 4718600 | tf_op jit(solution)/shard_map/ppermute | solution.py:399
  4.5 30.8 %copy-start.3 = (bf16[128,4224]{1,0:T(8,128)(2,1)}, bf16[128,4224]{1,0:T(8,128)(2,1)S(1)}, u32[]{:S(2)}) copy-start(bf16[128,4224]{1,0:T(8,128)(2,1)S(1)} %fusion.1.refs_0_) | copy-start | bytes 3244036
  4.5 29.2 %collective-permute-start.1 = (bf16[128,4224]{1,0:T(8,128)(2,1)S(1)}, bf16[128,4224]{1,0:T(8,128)(2,1)S(1)}, u32[]{:S(2)}, u32[]{:S(2)}) collective-permute-start(bf16[128,4224]{1,0:T(8,128)(2,1)S(1)} %fusion.1.refs_0_), channel_id=1, source_target_pairs={{0,4},{4,8},{8,12},{12,0},{1,5},{5,9},{9,13},{13,1},{2,6},{6,10},{... | collective-permute-start | bytes 3244040 | tf_op jit(solution)/shard_map/ppermute | solution.py:393
  7.2 28.1 %collective-permute-start = (bf16[128,4224]{1,0:T(8,128)(2,1)S(1)}, bf16[128,4224]{1,0:T(8,128)(2,1)}, u32[]{:S(2)}, u32[]{:S(2)}) collective-permute-start(bf16[128,4224]{1,0:T(8,128)(2,1)S(1)} %fusion.1.refs_0_), channel_id=1, source_target_pairs={{0,2},{1,3},{2,0},{3,1},{4,6},{5,7},{6,4},{7,5},{8,10},{9,11},{10,... | collective-permute-start | bytes 3244040 | tf_op jit(solution)/shard_map/ppermute | solution.py:396
  33.6 11.8 %copy-start.6 = (bf16[128,4224]{1,0:T(8,128)(2,1)}, bf16[128,4224]{1,0:T(8,128)(2,1)S(1)}, u32[]{:S(2)}) copy-start(bf16[128,4224]{1,0:T(8,128)(2,1)S(1)} %collective-permute-done.1.refs_0_) | copy-start | bytes 3244036
  33.7 25.8 %collective-permute-start.6 = (bf16[128,4224]{1,0:T(8,128)(2,1)S(1)}, bf16[128,4224]{1,0:T(8,128)(2,1)}, u32[]{:S(2)}, u32[]{:S(2)}) collective-permute-start(bf16[128,4224]{1,0:T(8,128)(2,1)S(1)} %collective-permute-done.1.refs_0_), channel_id=1, source_target_pairs={{0,2},{1,3},{2,0},{3,1},{4,6},{5,7},{6,4},{7,5},{8,10},{9,11},{10,... | collective-permute-start | bytes 3244040 | tf_op jit(solution)/shard_map/ppermute | solution.py:396
  35.2 27.0 %collective-permute-start.5 = (bf16[128,4224]{1,0:T(8,128)(2,1)S(1)}, bf16[128,4224]{1,0:T(8,128)(2,1)S(1)}, u32[]{:S(2)}, u32[]{:S(2)}) collective-permute-start(bf16[128,4224]{1,0:T(8,128)(2,1)S(1)} %collective-permute-done.1.refs_0_), channel_id=1, source_target_pairs={{0,4},{4,8},{8,12},{12,0},{1,5},{5,9},{9,13},{13,1},{2,6},{6,10},{... | collective-permute-start | bytes 3244040 | tf_op jit(solution)/shard_map/ppermute | solution.py:393
  62.2 11.0 %copy-start.7 = (bf16[128,4224]{1,0:T(8,128)(2,1)}, bf16[128,4224]{1,0:T(8,128)(2,1)S(1)}, u32[]{:S(2)}) copy-start(bf16[128,4224]{1,0:T(8,128)(2,1)S(1)} %collective-permute-done.5.refs_0_) | copy-start | bytes 3244036
  62.2 24.3 %collective-permute-start.8 = (bf16[128,4224]{1,0:T(8,128)(2,1)S(1)}, bf16[128,4224]{1,0:T(8,128)(2,1)S(1)}, u32[]{:S(2)}, u32[]{:S(2)}) collective-permute-start(bf16[128,4224]{1,0:T(8,128)(2,1)S(1)} %collective-permute-done.5.refs_0_), channel_id=1, source_target_pairs={{0,2},{1,3},{2,0},{3,1},{4,6},{5,7},{6,4},{7,5},{8,10},{9,11},{10,... | collective-permute-start | bytes 3244040 | tf_op jit(solution)/shard_map/ppermute | solution.py:396
  62.9 26.1 %collective-permute-start.7 = (bf16[128,4224]{1,0:T(8,128)(2,1)S(1)}, bf16[128,4224]{1,0:T(8,128)(2,1)}, u32[]{:S(2)}, u32[]{:S(2)}) collective-permute-start(bf16[128,4224]{1,0:T(8,128)(2,1)S(1)} %collective-permute-done.5.refs_0_), channel_id=1, source_target_pairs={{0,4},{4,8},{8,12},{12,0},{1,5},{5,9},{9,13},{13,1},{2,6},{6,10},{... | collective-permute-start | bytes 3244040 | tf_op jit(solution)/shard_map/ppermute | solution.py:393
  86.5 4.5 %copy-start.8 = (bf16[128,4224]{1,0:T(8,128)(2,1)}, bf16[128,4224]{1,0:T(8,128)(2,1)S(1)}, u32[]{:S(2)}) copy-start(bf16[128,4224]{1,0:T(8,128)(2,1)S(1)} %collective-permute-done.8.refs_1_) | copy-start | bytes 3244036
  89.0 27.1 %collective-permute-start.9 = (bf16[128,4224]{1,0:T(8,128)(2,1)}, bf16[128,4224]{1,0:T(8,128)(2,1)}, u32[]{:S(2)}, u32[]{:S(2)}) collective-permute-start(bf16[128,4224]{1,0:T(8,128)(2,1)} %collective-permute-done.7.refs_0_), channel_id=1, source_target_pairs={{0,2},{1,3},{2,0},{3,1},{4,6},{5,7},{6,4},{7,5},{8,10},{9,11},{10,... | collective-permute-start | bytes 3244040 | tf_op jit(solution)/shard_map/ppermute | solution.py:396
  90.1 37.9 %collective-permute-start.16 = (bf16[128,2176]{1,0:T(8,128)(2,1)}, bf16[128,2176]{1,0:T(8,128)(2,1)}, u32[]{:S(2)}, u32[]{:S(2)}) collective-permute-start(bf16[128,2176]{1,0:T(8,128)(2,1)} %get-tuple-element.74), channel_id=1, source_target_pairs={{0,2},{1,3},{2,0},{3,1},{4,6},{5,7},{6,4},{7,5},{8,10},{9,11},{10,... | collective-permute-start | bytes 1671176 | tf_op jit(solution)/shard_map/ppermute | solution.py:396
  101.2 14.9 %copy-start.11 = (bf16[128,2176]{1,0:T(8,128)(2,1)S(1)}, bf16[128,2176]{1,0:T(8,128)(2,1)}, u32[]{:S(2)}) copy-start(bf16[128,2176]{1,0:T(8,128)(2,1)} %get-tuple-element.104) | copy-start | bytes 1671172
  110.1 48.2 %collective-permute-start.10 = (bf16[1152,2048]{1,0:T(8,128)(2,1)}, bf16[1152,2048]{1,0:T(8,128)(2,1)}, u32[]{:S(2)}, u32[]{:S(2)}) collective-permute-start(bf16[1152,2048]{1,0:T(8,128)(2,1)} %shard_map.113.refs_19_), channel_id=1, source_target_pairs={{0,1},{1,0},{2,3},{3,2},{4,5},{5,4},{6,7},{7,6},{8,9},{9,8},{10,11... | collective-permute-start | bytes 14155784 | tf_op jit(solution)/shard_map/ppermute | solution.py:399
  116.1 23.8 %collective-permute-start.15 = (bf16[128,2176]{1,0:T(8,128)(2,1)S(1)}, bf16[128,2176]{1,0:T(8,128)(2,1)S(1)}, u32[]{:S(2)}, u32[]{:S(2)}) collective-permute-start(bf16[128,2176]{1,0:T(8,128)(2,1)S(1)} %copy-done.11), channel_id=1, source_target_pairs={{0,2},{1,3},{2,0},{3,1},{4,6},{5,7},{6,4},{7,5},{8,10},{9,11},{10,... | collective-permute-start | bytes 1671176 | tf_op jit(solution)/shard_map/ppermute | solution.py:396
  128.0 15.6 %copy-start.2 = (f32[128,2176]{1,0:T(8,128)S(1)}, f32[128,2176]{1,0:T(8,128)}, u32[]{:S(2)}) copy-start(f32[128,2176]{1,0:T(8,128)} %get-tuple-element.102) | copy-start | bytes 3342340
  129.6 14.0 %collective-permute-start.17 = (bf16[128,2176]{1,0:T(8,128)(2,1)S(1)}, bf16[128,2176]{1,0:T(8,128)(2,1)S(1)}, u32[]{:S(2)}, u32[]{:S(2)}) collective-permute-start(bf16[128,2176]{1,0:T(8,128)(2,1)S(1)} %add_convert_fusion.2), channel_id=1, source_target_pairs={{0,4},{4,8},{8,12},{12,0},{1,5},{5,9},{9,13},{13,1},{2,6},{6,10},{... | collective-permute-start | bytes 1671176 | tf_op jit(solution)/shard_map/ppermute | solution.py:393
  129.7 18.6 %collective-permute-start.14 = (bf16[128,2176]{1,0:T(8,128)(2,1)}, bf16[128,2176]{1,0:T(8,128)(2,1)S(1)}, u32[]{:S(2)}, u32[]{:S(2)}) collective-permute-start(bf16[128,2176]{1,0:T(8,128)(2,1)} %get-tuple-element.101), channel_id=1, source_target_pairs={{0,2},{1,3},{2,0},{3,1},{4,6},{5,7},{6,4},{7,5},{8,10},{9,11},{10,... | collective-permute-start | bytes 1671176 | tf_op jit(solution)/shard_map/ppermute | solution.py:396
  143.6 4.6 %copy-start.9 = (bf16[256,1152]{1,0:T(8,128)(2,1)S(1)}, bf16[256,1152]{1,0:T(8,128)(2,1)}, u32[]{:S(2)}) copy-start(bf16[256,1152]{1,0:T(8,128)(2,1)} %get-tuple-element.99) | copy-start | bytes 1769476
  143.6 13.7 %copy-start.1 = (f32[128,2176]{1,0:T(8,128)S(1)}, f32[128,2176]{1,0:T(8,128)}, u32[]{:S(2)}) copy-start(f32[128,2176]{1,0:T(8,128)} %get-tuple-element.100) | copy-start | bytes 3342340
  143.8 11.4 %collective-permute-start.18 = (bf16[128,2176]{1,0:T(8,128)(2,1)S(1)}, bf16[128,2176]{1,0:T(8,128)(2,1)S(1)}, u32[]{:S(2)}, u32[]{:S(2)}) collective-permute-start(bf16[128,2176]{1,0:T(8,128)(2,1)S(1)} %add_convert_fusion.1), channel_id=1, source_target_pairs={{0,4},{4,8},{8,12},{12,0},{1,5},{5,9},{9,13},{13,1},{2,6},{6,10},{... | collective-permute-start | bytes 1671176 | tf_op jit(solution)/shard_map/ppermute | solution.py:393
  143.8 14.5 %collective-permute-start.12 = (bf16[128,4224]{1,0:T(8,128)(2,1)}, bf16[128,4224]{1,0:T(8,128)(2,1)}, u32[]{:S(2)}, u32[]{:S(2)}) collective-permute-start(bf16[128,4224]{1,0:T(8,128)(2,1)} %collective-permute-done.7.refs_0_), channel_id=1, source_target_pairs={{0,1},{1,0},{2,3},{3,2},{4,5},{5,4},{6,7},{7,6},{8,9},{9,8},{10,11... | collective-permute-start | bytes 3244040 | tf_op jit(solution)/shard_map/ppermute | solution.py:399
  143.9 14.4 %collective-permute-start.13 = (bf16[128,4224]{1,0:T(8,128)(2,1)}, bf16[128,4224]{1,0:T(8,128)(2,1)}, u32[]{:S(2)}, u32[]{:S(2)}) collective-permute-start(bf16[128,4224]{1,0:T(8,128)(2,1)} %collective-permute-done.9.refs_1_), channel_id=1, source_target_pairs={{0,1},{1,0},{2,3},{3,2},{4,5},{5,4},{6,7},{7,6},{8,9},{9,8},{10,11... | collective-permute-start | bytes 3244040 | tf_op jit(solution)/shard_map/ppermute | solution.py:399
  148.2 10.1 %collective-permute-start.11 = (bf16[256,1152]{1,0:T(8,128)(2,1)S(1)}, bf16[256,1152]{1,0:T(8,128)(2,1)S(1)}, u32[]{:S(2)}, u32[]{:S(2)}) collective-permute-start(bf16[256,1152]{1,0:T(8,128)(2,1)S(1)} %copy-done.9), channel_id=1, source_target_pairs={{0,1},{1,0},{2,3},{3,2},{4,5},{5,4},{6,7},{7,6},{8,9},{9,8},{10,11... | collective-permute-start | bytes 1769480 | tf_op jit(solution)/shard_map/ppermute | solution.py:399
  155.2 16.7 %collective-permute-start.19 = (bf16[128,2176]{1,0:T(8,128)(2,1)}, bf16[128,2176]{1,0:T(8,128)(2,1)}, u32[]{:S(2)}, u32[]{:S(2)}) collective-permute-start(bf16[128,2176]{1,0:T(8,128)(2,1)} %get-tuple-element.108), channel_id=1, source_target_pairs={{0,2},{1,3},{2,0},{3,1},{4,6},{5,7},{6,4},{7,5},{8,10},{9,11},{10,... | collective-permute-start | bytes 1671176 | tf_op jit(solution)/shard_map/ppermute | solution.py:396
  158.3 13.6 %collective-permute-start.20 = (bf16[128,2176]{1,0:T(8,128)(2,1)}, bf16[128,2176]{1,0:T(8,128)(2,1)}, u32[]{:S(2)}, u32[]{:S(2)}) collective-permute-start(bf16[128,2176]{1,0:T(8,128)(2,1)} %add_convert_fusion.refs_9_), channel_id=1, source_target_pairs={{0,4},{4,8},{8,12},{12,0},{1,5},{5,9},{9,13},{13,1},{2,6},{6,10},{... | collective-permute-start | bytes 1671176 | tf_op jit(solution)/shard_map/ppermute | solution.py:393
  158.3 0.8 copy-start.10
  159.2 12.7 %copy-start = (f32[128,2176]{1,0:T(8,128)S(1)}, f32[128,2176]{1,0:T(8,128)}, u32[]{:S(2)}) copy-start(f32[128,2176]{1,0:T(8,128)} %get-tuple-element.107) | copy-start | bytes 3342340
  173.3 1.0 copy-start.4
  173.3 0.9 copy-start.5

commit v4 on v3

--- a/solution.py
+++ b/solution.py
@@ -380,6 +380,37 @@
     )(*ins)
 
 
+def pack_kernel(tok_ref, cot_ref, ids_ref, gates_ref, out, table, sem):
+    model_width = tok_ref.shape[1]
+    token_count, room = table.shape
+    moves = [(tok_ref, 0, model_width), (cot_ref, model_width, model_width), (table, 2 * model_width, room)]
+    copies = [
+        pltpu.make_async_copy(src, out.at[:, pl.ds(start, width)], sem.at[i])
+        for i, (src, start, width) in enumerate(moves)
+    ]
+    copies[0].start()
+    copies[1].start()
+    expert = lax.broadcasted_iota(jnp.int32, (room, token_count), 0)
+    found = jnp.zeros((room, token_count), jnp.float32)
+    for k in range(ids_ref.shape[0]):
+        found = found + jnp.where(expert == ids_ref[k : k + 1, :], gates_ref[k : k + 1, :].astype(jnp.float32), 0.0)
+    table[...] = found.T.astype(jnp.bfloat16)
+    copies[2].start()
+    wait_for(copies)
+
+
+def pack(tokens, cotangent, expert_ids, gates, room):
+    token_count, model_width = tokens.shape
+    return pl.pallas_call(
+        pack_kernel,
+        out_shape=jax.ShapeDtypeStruct((token_count, 2 * model_width + room), jnp.bfloat16),
+        in_specs=[VMEM, VMEM, VMEM, VMEM],
+        out_specs=HBM,
+        scratch_shapes=[pltpu.VMEM((token_count, room), jnp.bfloat16), pltpu.SemaphoreType.DMA((3,))],
+        compiler_params=pltpu.CompilerParams(vmem_limit_bytes=60 * 1024 * 1024),
+    )(tokens, cotangent, expert_ids.T, gates.T)
+
+
 def gathered(tokens, cotangent, expert_ids, gates, w_gate, w_up, w_down):
     z_count = lax.axis_size("expert")
     dp_count = lax.axis_size("dp")
@@ -412,12 +443,8 @@
             line = line + carried.astype(jnp.float32)
         return line.astype(jnp.bfloat16) if d else line
 
-    expert_range = jnp.arange(expert_count, dtype=jnp.int32)
-    chosen = expert_ids[:, :, None] == expert_range
-    gate_table = jnp.sum(jnp.where(chosen, gates[:, :, None].astype(jnp.float32), 0.0), axis=1).astype(jnp.bfloat16)
     table_width = -(-expert_count // LANES) * LANES
-    gate_table = jnp.pad(gate_table, ((0, 0), (0, table_width - expert_count)))
-    block = jnp.concatenate([tokens, cotangent, gate_table], axis=1)
+    block = pack(tokens, cotangent, expert_ids, gates, table_width)
     own_expert = z_here * dp_count + dp_here
     mate_expert = z_here * dp_count + (dp_here ^ 1)
     pick_row = jnp.arange(table_width, dtype=jnp.int32)[:, None]
@@ -432,25 +459,30 @@
     pairs = [across(block)]
     ring = after(ring, *weights[1::2])
 
-    row_own, row_far, held, line = [], [], [], tokens
+    row_own, row_far, held, line, carried = [], [], [], tokens, None
     mate = jnp.zeros((3 * w_gate.shape[2], model_width), jnp.bfloat16)
     for d in range(z_count):
         ready = []
         if d + 1 < z_count:
-            pairs.append(across(ring))
+            if d > 1 and d + 2 == z_count:
+                pairs.append([ring] + [z_shift(block, 1) for block in pairs[d][1:]])
+            else:
+                pairs.append(across(ring))
             following = z_shift(ring, 1) if d + 2 < z_count else None
             ready = [ring]
         passed, waited = [], []
         if d and d + 1 == z_count:
             count = d * x_count * token_count
             mate = mate_products(count, held[0], held[1], held[3], held[5], held[7])
-            passed, waited = ([row_far[0][0], row_own[1]] if d > 1 else [row_far[0][0]]), [mate]
+            passed, waited = [row_far[0][0]], [mate]
+            if d > 1:
+                carried = home(1)
+                waited.append(carried)
+                carried = z_shift(carried, 1)
         outs = one_step(d, z_count, pairs[d], after(pick, *ready), weights, held, passed, waited)
         own, far, held, mate_factors = outs
         if len(mate_factors) > 1:
             row_far[0] = mate_factors[1][None]
-        if len(mate_factors) > 2:
-            row_own[1] = mate_factors[2]
         if d + 1 < z_count:
             far = after(far, pairs[d + 1][-1])
         if d + 2 < z_count:
@@ -458,8 +490,7 @@
         row_own.append(own)
         row_far.append(far.reshape(x_count - 1, token_count, -1))
 
-    carried = None
-    for d in range(1, z_count):
+    for d in range(1 if carried is None else 2, z_count):
         line = home(d, carried)
         carried = z_shift(line, 1)
     got = core_swap(mate)

time: 175 us -> 166 us (0.949)
  waiting for transfers between devices: 86 us -> 78 us
  starting transfers between devices: 14.8 us -> 12.3 us
  Pallas kernels: 62.5 us -> 64.6 us
  other arithmetic: 8.09 us -> 6.18 us
    ppermute x8 -> x7, waiting for transfers between devices: 45.7 us -> 34.8 us  [x_shift(): lax.ppermute(value, 'dp', [(i, (i + CORES * step) % dp_count) for i in ra...]
    ppermute x6 -> x7, waiting for transfers between devices: 40.3 us -> 43.2 us  [z_shift(): lax.ppermute(value, 'expert', [(i, (i + step) % z_count) for i in range(z...]
    ppermute x8 -> x7, starting transfers between devices: 10.3 us -> 7.84 us  [x_shift(): lax.ppermute(value, 'dp', [(i, (i + CORES * step) % dp_count) for i in ra...]
    pallas_call x0 -> x1, Pallas kernels: none -> 2.2 us  [pack(): pl.pallas_call(pack_kernel, out_shape=jax.ShapeDtypeStruct((token_count,...]
  transfers between devices with their start and end apart: 21 -> 21, of which waited for: 11 -> 9; matrix products, arithmetic and copies ran while one was open for 4% -> 3% of each run, Pallas kernels for 36% -> 39%
where the time goes in v4:
time: 166 us; the launch traced here: 165 us
  waiting for transfers between devices  78 us (47%)
  Pallas kernels  64.6 us (39%)
  starting transfers between devices  12.3 us (7%)
  other arithmetic  6.18 us (4%)
  local copies, waits for them, and re-layouts  3.22 us (2%)
    ppermute x7, waiting for transfers between devices, z_shift(): lax.ppermute(value, 'expert', [(i, (i + step) % z_count) for i in range(z...  43.2 us
    pallas_call x4, Pallas kernels, one_step(): pl.pallas_call(lambda *refs: step_kernel(lines, step, steps, len(passed),...  40.7 us
    ppermute x7, waiting for transfers between devices, x_shift(): lax.ppermute(value, 'dp', [(i, (i + CORES * step) % dp_count) for i in ra...  34.8 us
    pallas_call x1, Pallas kernels, finish(): pl.pallas_call(lambda *refs: finish_kernel(lines, *refs), out_shape=[jax....  12.7 us
    pallas_call x1, Pallas kernels, mate_products(): pl.pallas_call(lambda *refs: mate_kernel(count, *refs), out_shape=jax.Sha...  8.96 us
    ppermute x7, starting transfers between devices, x_shift(): lax.ppermute(value, 'dp', [(i, (i + CORES * step) % dp_count) for i in ra...  7.84 us
    convert_element_type x3, other arithmetic, home(): return line.astype(jnp.bfloat16) if d else line  3.48 us
  transfers between devices with their start and end apart: 21, of which 9 were waited for; matrix products, arithmetic and copies ran while one was open for 3% of the time, Pallas kernels for 39%

profile of v4, /device:TPU:0, one launch (start us, length us, event | category | flops | bytes accessed | tf_op | source)
XLA Modules:
  0.0 165.2 jit_solution(5739190661168122547)
XLA Ops:
  0.6 0.5 collective-permute-start.2
  1.1 0.1 collective-permute-start.3
  1.2 0.4 collective-permute-start.4
  1.7 2.2 %shard_map.110.refs_0_ = bf16[128,4224]{1,0:T(8,128)(2,1)} custom-call(bf16[128,2048]{1,0:T(8,128)(2,1)} %tok_ref.1, bf16[128,2048]{1,0:T(8,128)(2,1)} %cot_ref.1, s32[8,128]{1,0:T(8,128)} %bitcast.24, bf16[8,128]{1,0:T(8,128)(2,1)} %bitcast.25), custom_call_target="tpu_custom_call" | custom-call | tf_op jit(solution)/shard_map/pallas_call | solution.py:404
  3.9 2.7 %collective-permute-start.1 = (bf16[128,4224]{1,0:T(8,128)(2,1)}, bf16[128,4224]{1,0:T(8,128)(2,1)S(1)}, u32[]{:S(2)}, u32[]{:S(2)}) collective-permute-start(bf16[128,4224]{1,0:T(8,128)(2,1)} %shard_map.110.refs_0_), channel_id=1, source_target_pairs={{0,4},{4,8},{8,12},{12,0},{1,5},{5,9},{9,13},{13,1},{2,6},{6,10},{... | collective-permute-start | bytes 3244040 | tf_op jit(solution)/shard_map/ppermute | solution.py:424
  6.6 1.5 collective-permute-start
  8.1 0.6 fusion.1.refs_2_
  8.7 24.6 %collective-permute-done.1.refs_0_ = bf16[128,4224]{1,0:T(8,128)(2,1)S(1)} collective-permute-done((bf16[128,4224]{1,0:T(8,128)(2,1)}, bf16[128,4224]{1,0:T(8,128)(2,1)S(1)}, u32[]{:S(2)}, u32[]{:S(2)}) %collective-permute-start.1) | collective-permute-done | bytes 1081376 | tf_op jit(solution)/shard_map/ppermute | solution.py:424
  33.3 0.0 collective-permute-done.2.refs_4_
  33.3 0.0 collective-permute-done.3.refs_6_
  33.3 0.0 collective-permute-done.4.refs_8_
  33.3 1.6 collective-permute-start.6
  34.8 0.0 collective-permute-start.5
  34.8 0.0 collective-permute-done.refs_1_
  34.9 10.2 %shard_map.111 = (f32[128,2176]{1,0:T(8,128)}, bf16[128,2176]{1,0:T(8,128)(2,1)}, bf16[1024,2048]{1,0:T(8,128)(2,1)}, bf16[1024,2048]{1,0:T(8,128)(2,1)}, bf16[1...) custom-call(bf16[128,4224]{1,0:T(8,128)(2,1)} %shard_map.110.refs_0_, ...), custom_call_target="tpu_custom_call" | custom-call | flops 120795955200 | bytes 1048576 | tf_op jit(solution)/shard_map/pallas_call | solution.py:271
  45.0 14.0 %collective-permute-done.6.refs_1_ = bf16[128,4224]{1,0:T(8,128)(2,1)} collective-permute-done((bf16[128,4224]{1,0:T(8,128)(2,1)S(1)}, bf16[128,4224]{1,0:T(8,128)(2,1)}, u32[]{:S(2)}, u32[]{:S(2)}) %collective-permute-start.6) | collective-permute-done | bytes 1081376 | tf_op jit(solution)/shard_map/ppermute | solution.py:427
  59.1 2.8 %collective-permute-done.5.refs_0_ = bf16[128,4224]{1,0:T(8,128)(2,1)S(1)} collective-permute-done((bf16[128,4224]{1,0:T(8,128)(2,1)S(1)}, bf16[128,4224]{1,0:T(8,128)(2,1)S(1)}, u32[]{:S(2)}, u32[]{:S(2)}) %collective-permute-start.5) | collective-permute-done | bytes 1081376 | tf_op jit(solution)/shard_map/ppermute | solution.py:424
  61.8 0.7 collective-permute-start.8
  62.5 0.0 collective-permute-start.7
  62.5 10.1 %shard_map.112 = (f32[128,2176]{1,0:T(8,128)}, bf16[128,2176]{1,0:T(8,128)(2,1)}, bf16[1024,2048]{1,0:T(8,128)(2,1)}, bf16[1024,2048]{1,0:T(8,128)(2,1)}, bf16[1...) custom-call(bf16[128,4224]{1,0:T(8,128)(2,1)} %copy-done.9, ...), custom_call_target="tpu_custom_call", output_to_operand_aliasing={{2}: (9, {}), {3}: (10, {}), {4}: (11, {}), {5}: (12, {}), ... | custom-call | flops 120795955200 | bytes 1048576 | tf_op jit(solution)/shard_map/pallas_call | solution.py:271
  72.7 13.5 %collective-permute-done.8.refs_1_ = bf16[128,4224]{1,0:T(8,128)(2,1)} collective-permute-done((bf16[128,4224]{1,0:T(8,128)(2,1)S(1)}, bf16[128,4224]{1,0:T(8,128)(2,1)}, u32[]{:S(2)}, u32[]{:S(2)}) %collective-permute-start.8) | collective-permute-done | bytes 1081376 | tf_op jit(solution)/shard_map/ppermute | solution.py:427
  86.2 0.8 collective-permute-start.10
  87.1 1.5 collective-permute-done.7.refs_0_
  88.6 0.0 collective-permute-start.9
  88.6 10.2 %shard_map.113 = (f32[128,2176]{1,0:T(8,128)}, bf16[128,2176]{1,0:T(8,128)(2,1)}, bf16[1024,2048]{1,0:T(8,128)(2,1)}, bf16[1024,2048]{1,0:T(8,128)(2,1)}, bf16[1...) custom-call(bf16[128,4224]{1,0:T(8,128)(2,1)} %copy-done.10, ...), custom_call_target="tpu_custom_call", output_to_operand_aliasing={{2}: (9, {}), {3}: (10, {}), {4}: (11, {}), {5}: (12, {}), ... | custom-call | flops 120795955200 | bytes 1048576 | tf_op jit(solution)/shard_map/pallas_call | solution.py:271
  98.7 0.0 copy-start.3
  98.8 9.0 %shard_map.114.refs_18_ = bf16[1152,2048]{1,0:T(8,128)(2,1)} custom-call(bf16[1024,2048]{1,0:T(8,128)(2,1)} %get-tuple-element.84.refs_0_.refs_9_, bf16[1024,2048]{1,0:T(8,128)(2,1)} %get-tuple-element.85.refs_1_.refs_10_, bf16[1024,384]{1,0:T(8,128)(2,1)} %get-tuple-element.87.refs_2_.refs_12_, bf16[1024,384]{1,0:T(8,128)(2,1)} %get-tuple-element.89.refs_3_.refs_14_, ...), custom_call_target="tpu_custom_call" | custom-call | flops 108716359680 | bytes 3145728 | tf_op jit(solution)/shard_map/pallas_call | solution.py:308
  107.7 0.1 collective-permute-start.11
  107.8 0.0 collective-permute-done.10
  107.8 1.2 add_convert_fusion.2.refs_19_
  109.1 0.1 collective-permute-start.17
  109.1 4.8 %collective-permute-done.9.refs_1_ = bf16[128,4224]{1,0:T(8,128)(2,1)} collective-permute-done((bf16[128,4224]{1,0:T(8,128)(2,1)}, bf16[128,4224]{1,0:T(8,128)(2,1)}, u32[]{:S(2)}, u32[]{:S(2)}) %collective-permute-start.9) | collective-permute-done | bytes 1081376 | tf_op jit(solution)/shard_map/ppermute | solution.py:424
  113.9 1.0 collective-permute-start.16
  115.0 10.2 %shard_map.115 = (f32[128,2176]{1,0:T(8,128)}, bf16[128,2176]{1,0:T(8,128)(2,1)}, bf16[1024,2048]{1,0:T(8,128)(2,1)}, bf16[1024,2048]{1,0:T(8,128)(2,1)}, bf16[1...) custom-call(bf16[128,4224]{1,0:T(8,128)(2,1)} %collective-permute-do, ...), custom_call_target="tpu_custom_call", output_to_operand_aliasing={{2}: (9, {}), {3}: (10, {}), {4}: (11, {}), {5}: (12, {}), ... | custom-call | flops 120795955200 | bytes 1048576 | tf_op jit(solution)/shard_map/pallas_call | solution.py:271
  125.2 1.0 collective-permute-start.15
  126.3 0.0 collective-permute-done.17
  126.3 0.0 collective-permute-done.16
  126.3 0.8 copy-done.5
  127.1 0.0 copy-done.2
  127.1 1.3 add_convert_fusion.1
  128.4 0.1 collective-permute-start.18
  128.5 0.1 collective-permute-start.13
  128.5 0.5 collective-permute-start.14
  129.0 0.7 stack.67
  129.7 7.2 %collective-permute-done.15 = bf16[128,2176]{1,0:T(8,128)(2,1)S(1)} collective-permute-done((bf16[128,2176]{1,0:T(8,128)(2,1)}, bf16[128,2176]{1,0:T(8,128)(2,1)S(1)}, u32[]{:S(2)}, u32[]{:S(2)}) %collective-permute-start.15) | collective-permute-done | bytes 557088 | tf_op jit(solution)/shard_map/ppermute | solution.py:427
  136.9 0.0 collective-permute-start.12
  136.9 7.7 %collective-permute-done.18 = bf16[128,2176]{1,0:T(8,128)(2,1)S(1)} collective-permute-done((bf16[128,2176]{1,0:T(8,128)(2,1)S(1)}, bf16[128,2176]{1,0:T(8,128)(2,1)S(1)}, u32[]{:S(2)}, u32[]{:S(2)}) %collective-permute-start.18) | collective-permute-done | bytes 557088 | tf_op jit(solution)/shard_map/ppermute | solution.py:424
  144.6 1.2 collective-permute-start.19
  145.8 1.0 add_convert_fusion.refs_9_
  146.8 0.0 collective-permute-done.13.refs_7_
  146.8 0.0 collective-permute-start.20
  146.8 0.0 collective-permute-done.12.refs_6_
  146.8 0.0 copy-start.11
  146.8 0.0 collective-permute-done.14.refs_8_
  146.8 0.0 collective-permute-done.11.refs_5_
  146.8 0.8 copy-done.11
  147.6 12.7 %shard_map.116 = (bf16[2048,384]{1,0:T(8,128)(2,1)}, bf16[2048,384]{1,0:T(8,128)(2,1)}, bf16[384,2048]{1,0:T(8,128)(2,1)}) custom-call(bf16[1024,2048]{1,0:T(8,128)(2,1)} %get-tuple-element.93.refs_0_, bf16[1024,2048]{1,0:T(8,128)(2,1)} %get-tuple-element.94.refs_1_, bf16[1024,384]{1,0:T(8,128)(2,1)} %get-tuple-element.95.refs_2_, ...), custom_call_target="tpu_custom_call" | custom-call | flops 181193932800 | bytes 5242880 | tf_op jit(solution)/shard_map/pallas_call | solution.py:365
  160.3 0.0 collective-permute-done.19
  160.3 1.9 %collective-permute-done.20 = bf16[128,2176]{1,0:T(8,128)(2,1)} collective-permute-done((bf16[128,2176]{1,0:T(8,128)(2,1)}, bf16[128,2176]{1,0:T(8,128)(2,1)}, u32[]{:S(2)}, u32[]{:S(2)}) %collective-permute-start.20) | collective-permute-done | bytes 557088 | tf_op jit(solution)/shard_map/ppermute | solution.py:424
  162.2 1.4 convert_add_fusion
  163.5 0.0 copy-start.6
  163.6 0.9 slice.12
  164.4 0.1 copy.38
  164.5 0.7 select_reduce_fusion
  (23 shorter events, 0.1 us)
Async XLA Ops:
  0.6 32.6 %collective-permute-start.2 = (bf16[2048,384]{1,0:T(8,128)(2,1)}, bf16[2048,384]{1,0:T(8,128)(2,1)S(1)}, u32[]{:S(2)}, u32[]{:S(2)}) collective-permute-start(bf16[2048,384]{1,0:T(8,128)(2,1)} %bitcast.26), channel_id=1, source_target_pairs={{0,1},{1,0},{2,3},{3,2},{4,5},{5,4},{6,7},{7,6},{8,9},{9,8},{10,11... | collective-permute-start | bytes 4718600 | tf_op jit(solution)/shard_map/ppermute | solution.py:430
  1.1 32.1 %collective-permute-start.3 = (bf16[2048,384]{1,0:T(8,128)(2,1)}, bf16[2048,384]{1,0:T(8,128)(2,1)}, u32[]{:S(2)}, u32[]{:S(2)}) collective-permute-start(bf16[2048,384]{1,0:T(8,128)(2,1)} %bitcast.31), channel_id=1, source_target_pairs={{0,1},{1,0},{2,3},{3,2},{4,5},{5,4},{6,7},{7,6},{8,9},{9,8},{10,11... | collective-permute-start | bytes 4718600 | tf_op jit(solution)/shard_map/ppermute | solution.py:430
  1.2 32.0 %collective-permute-start.4 = (bf16[384,2048]{1,0:T(8,128)(2,1)}, bf16[384,2048]{1,0:T(8,128)(2,1)}, u32[]{:S(2)}, u32[]{:S(2)}) collective-permute-start(bf16[384,2048]{1,0:T(8,128)(2,1)} %bitcast.36), channel_id=1, source_target_pairs={{0,1},{1,0},{2,3},{3,2},{4,5},{5,4},{6,7},{7,6},{8,9},{9,8},{10,11... | collective-permute-start | bytes 4718600 | tf_op jit(solution)/shard_map/ppermute | solution.py:430
  3.9 29.4 %collective-permute-start.1 = (bf16[128,4224]{1,0:T(8,128)(2,1)}, bf16[128,4224]{1,0:T(8,128)(2,1)S(1)}, u32[]{:S(2)}, u32[]{:S(2)}) collective-permute-start(bf16[128,4224]{1,0:T(8,128)(2,1)} %shard_map.110.refs_0_), channel_id=1, source_target_pairs={{0,4},{4,8},{8,12},{12,0},{1,5},{5,9},{9,13},{13,1},{2,6},{6,10},{... | collective-permute-start | bytes 3244040 | tf_op jit(solution)/shard_map/ppermute | solution.py:424
  6.6 28.3 %collective-permute-start = (bf16[128,4224]{1,0:T(8,128)(2,1)}, bf16[128,4224]{1,0:T(8,128)(2,1)}, u32[]{:S(2)}, u32[]{:S(2)}) collective-permute-start(bf16[128,4224]{1,0:T(8,128)(2,1)} %shard_map.110.refs_0_), channel_id=1, source_target_pairs={{0,2},{1,3},{2,0},{3,1},{4,6},{5,7},{6,4},{7,5},{8,10},{9,11},{10,... | collective-permute-start | bytes 3244040 | tf_op jit(solution)/shard_map/ppermute | solution.py:427
  33.3 11.8 %copy-start.9 = (bf16[128,4224]{1,0:T(8,128)(2,1)}, bf16[128,4224]{1,0:T(8,128)(2,1)S(1)}, u32[]{:S(2)}) copy-start(bf16[128,4224]{1,0:T(8,128)(2,1)S(1)} %collective-permute-done.1.refs_0_) | copy-start | bytes 3244036
  33.3 1.6 copy-start.8
  33.3 25.8 %collective-permute-start.6 = (bf16[128,4224]{1,0:T(8,128)(2,1)S(1)}, bf16[128,4224]{1,0:T(8,128)(2,1)}, u32[]{:S(2)}, u32[]{:S(2)}) collective-permute-start(bf16[128,4224]{1,0:T(8,128)(2,1)S(1)} %collective-permute-done.1.refs_0_), channel_id=1, source_target_pairs={{0,2},{1,3},{2,0},{3,1},{4,6},{5,7},{6,4},{7,5},{8,10},{9,11},{10,... | collective-permute-start | bytes 3244040 | tf_op jit(solution)/shard_map/ppermute | solution.py:427
  34.8 27.0 %collective-permute-start.5 = (bf16[128,4224]{1,0:T(8,128)(2,1)S(1)}, bf16[128,4224]{1,0:T(8,128)(2,1)S(1)}, u32[]{:S(2)}, u32[]{:S(2)}) collective-permute-start(bf16[128,4224]{1,0:T(8,128)(2,1)S(1)} %collective-permute-done.1.refs_0_), channel_id=1, source_target_pairs={{0,4},{4,8},{8,12},{12,0},{1,5},{5,9},{9,13},{13,1},{2,6},{6,10},{... | collective-permute-start | bytes 3244040 | tf_op jit(solution)/shard_map/ppermute | solution.py:424
  61.8 10.8 %copy-start.10 = (bf16[128,4224]{1,0:T(8,128)(2,1)}, bf16[128,4224]{1,0:T(8,128)(2,1)S(1)}, u32[]{:S(2)}) copy-start(bf16[128,4224]{1,0:T(8,128)(2,1)S(1)} %collective-permute-done.5.refs_0_) | copy-start | bytes 3244036
  61.8 24.4 %collective-permute-start.8 = (bf16[128,4224]{1,0:T(8,128)(2,1)S(1)}, bf16[128,4224]{1,0:T(8,128)(2,1)}, u32[]{:S(2)}, u32[]{:S(2)}) collective-permute-start(bf16[128,4224]{1,0:T(8,128)(2,1)S(1)} %collective-permute-done.5.refs_0_), channel_id=1, source_target_pairs={{0,2},{1,3},{2,0},{3,1},{4,6},{5,7},{6,4},{7,5},{8,10},{9,11},{10,... | collective-permute-start | bytes 3244040 | tf_op jit(solution)/shard_map/ppermute | solution.py:427
  62.5 26.1 %collective-permute-start.7 = (bf16[128,4224]{1,0:T(8,128)(2,1)S(1)}, bf16[128,4224]{1,0:T(8,128)(2,1)}, u32[]{:S(2)}, u32[]{:S(2)}) collective-permute-start(bf16[128,4224]{1,0:T(8,128)(2,1)S(1)} %collective-permute-done.5.refs_0_), channel_id=1, source_target_pairs={{0,4},{4,8},{8,12},{12,0},{1,5},{5,9},{9,13},{13,1},{2,6},{6,10},{... | collective-permute-start | bytes 3244040 | tf_op jit(solution)/shard_map/ppermute | solution.py:424
  86.2 21.6 %collective-permute-start.10 = (bf16[128,2176]{1,0:T(8,128)(2,1)}, bf16[128,2176]{1,0:T(8,128)(2,1)}, u32[]{:S(2)}, u32[]{:S(2)}) collective-permute-start(bf16[128,2176]{1,0:T(8,128)(2,1)} %get-tuple-element.73), channel_id=1, source_target_pairs={{0,2},{1,3},{2,0},{3,1},{4,6},{5,7},{6,4},{7,5},{8,10},{9,11},{10,... | collective-permute-start | bytes 1671176 | tf_op jit(solution)/shard_map/ppermute | solution.py:427
  88.6 25.3 %collective-permute-start.9 = (bf16[128,4224]{1,0:T(8,128)(2,1)}, bf16[128,4224]{1,0:T(8,128)(2,1)}, u32[]{:S(2)}, u32[]{:S(2)}) collective-permute-start(bf16[128,4224]{1,0:T(8,128)(2,1)} %collective-permute-done.8.refs_1_), channel_id=1, source_target_pairs={{0,4},{4,8},{8,12},{12,0},{1,5},{5,9},{9,13},{13,1},{2,6},{6,10},{... | collective-permute-start | bytes 3244040 | tf_op jit(solution)/shard_map/ppermute | solution.py:424
  98.7 9.1 %copy-start.3 = (f32[128,2176]{1,0:T(8,128)S(1)}, f32[128,2176]{1,0:T(8,128)}, u32[]{:S(2)}) copy-start(f32[128,2176]{1,0:T(8,128)} %get-tuple-element.92) | copy-start | bytes 3342340
  107.7 39.1 %collective-permute-start.11 = (bf16[1152,2048]{1,0:T(8,128)(2,1)}, bf16[1152,2048]{1,0:T(8,128)(2,1)}, u32[]{:S(2)}, u32[]{:S(2)}) collective-permute-start(bf16[1152,2048]{1,0:T(8,128)(2,1)} %shard_map.114.refs_18_), channel_id=1, source_target_pairs={{0,1},{1,0},{2,3},{3,2},{4,5},{5,4},{6,7},{7,6},{8,9},{9,8},{10,11... | collective-permute-start | bytes 14155784 | tf_op jit(solution)/shard_map/ppermute | solution.py:430
  107.8 6.1 %copy-start.12 = (bf16[128,2176]{1,0:T(8,128)(2,1)S(1)}, bf16[128,2176]{1,0:T(8,128)(2,1)}, u32[]{:S(2)}) copy-start(bf16[128,2176]{1,0:T(8,128)(2,1)} %get-tuple-element.103) | copy-start | bytes 1671172
  109.0 5.9 %copy-start.4 = (bf16[128,2176]{1,0:T(8,128)(2,1)}, bf16[128,2176]{1,0:T(8,128)(2,1)S(1)}, u32[]{:S(2)}) copy-start(bf16[128,2176]{1,0:T(8,128)(2,1)S(1)} %add_convert_fusion.2.refs_19_) | copy-start | bytes 1671172
  109.1 17.2 %collective-permute-start.17 = (bf16[128,2176]{1,0:T(8,128)(2,1)S(1)}, bf16[128,2176]{1,0:T(8,128)(2,1)S(1)}, u32[]{:S(2)}, u32[]{:S(2)}) collective-permute-start(bf16[128,2176]{1,0:T(8,128)(2,1)S(1)} %add_convert_fusion.2.refs_19_), channel_id=1, source_target_pairs={{0,4},{4,8},{8,12},{12,0},{1,5},{5,9},{9,13},{13,1},{2,6},{6,10},{... | collective-permute-start | bytes 1671176 | tf_op jit(solution)/shard_map/ppermute | solution.py:424
  113.9 12.4 %collective-permute-start.16 = (bf16[128,2176]{1,0:T(8,128)(2,1)S(1)}, bf16[128,2176]{1,0:T(8,128)(2,1)S(1)}, u32[]{:S(2)}, u32[]{:S(2)}) collective-permute-start(bf16[128,2176]{1,0:T(8,128)(2,1)S(1)} %copy-done.12), channel_id=1, source_target_pairs={{0,2},{1,3},{2,0},{3,1},{4,6},{5,7},{6,4},{7,5},{8,10},{9,11},{10,... | collective-permute-start | bytes 1671176 | tf_op jit(solution)/shard_map/ppermute | solution.py:427
  115.0 12.1 %copy-start.2 = (f32[128,2176]{1,0:T(8,128)S(1)}, f32[128,2176]{1,0:T(8,128)}, u32[]{:S(2)}) copy-start(f32[128,2176]{1,0:T(8,128)} %get-tuple-element.101) | copy-start | bytes 3342340
  125.2 11.7 %collective-permute-start.15 = (bf16[128,2176]{1,0:T(8,128)(2,1)}, bf16[128,2176]{1,0:T(8,128)(2,1)S(1)}, u32[]{:S(2)}, u32[]{:S(2)}) collective-permute-start(bf16[128,2176]{1,0:T(8,128)(2,1)} %get-tuple-element.100), channel_id=1, source_target_pairs={{0,2},{1,3},{2,0},{3,1},{4,6},{5,7},{6,4},{7,5},{8,10},{9,11},{10,... | collective-permute-start | bytes 1671176 | tf_op jit(solution)/shard_map/ppermute | solution.py:427
  126.3 0.8 copy-start.5
  127.1 18.7 %copy-start.1 = (f32[128,2176]{1,0:T(8,128)S(1)}, f32[128,2176]{1,0:T(8,128)}, u32[]{:S(2)}) copy-start(f32[128,2176]{1,0:T(8,128)} %get-tuple-element.99) | copy-start | bytes 3342340
  128.4 16.2 %collective-permute-start.18 = (bf16[128,2176]{1,0:T(8,128)(2,1)S(1)}, bf16[128,2176]{1,0:T(8,128)(2,1)S(1)}, u32[]{:S(2)}, u32[]{:S(2)}) collective-permute-start(bf16[128,2176]{1,0:T(8,128)(2,1)S(1)} %add_convert_fusion.1), channel_id=1, source_target_pairs={{0,4},{4,8},{8,12},{12,0},{1,5},{5,9},{9,13},{13,1},{2,6},{6,10},{... | collective-permute-start | bytes 1671176 | tf_op jit(solution)/shard_map/ppermute | solution.py:424
  128.5 18.3 %collective-permute-start.13 = (bf16[128,4224]{1,0:T(8,128)(2,1)}, bf16[128,4224]{1,0:T(8,128)(2,1)}, u32[]{:S(2)}, u32[]{:S(2)}) collective-permute-start(bf16[128,4224]{1,0:T(8,128)(2,1)} %collective-permute-done.7.refs_0_), channel_id=1, source_target_pairs={{0,1},{1,0},{2,3},{3,2},{4,5},{5,4},{6,7},{7,6},{8,9},{9,8},{10,11... | collective-permute-start | bytes 3244040 | tf_op jit(solution)/shard_map/ppermute | solution.py:430
  128.5 18.2 %collective-permute-start.14 = (bf16[128,4224]{1,0:T(8,128)(2,1)}, bf16[128,4224]{1,0:T(8,128)(2,1)}, u32[]{:S(2)}, u32[]{:S(2)}) collective-permute-start(bf16[128,4224]{1,0:T(8,128)(2,1)} %collective-permute-done.9.refs_1_), channel_id=1, source_target_pairs={{0,1},{1,0},{2,3},{3,2},{4,5},{5,4},{6,7},{7,6},{8,9},{9,8},{10,11... | collective-permute-start | bytes 3244040 | tf_op jit(solution)/shard_map/ppermute | solution.py:430
  136.9 9.9 %collective-permute-start.12 = (bf16[256,1152]{1,0:T(8,128)(2,1)}, bf16[256,1152]{1,0:T(8,128)(2,1)S(1)}, u32[]{:S(2)}, u32[]{:S(2)}) collective-permute-start(bf16[256,1152]{1,0:T(8,128)(2,1)} %get-tuple-element.98), channel_id=1, source_target_pairs={{0,1},{1,0},{2,3},{3,2},{4,5},{5,4},{6,7},{7,6},{8,9},{9,8},{10,11... | collective-permute-start | bytes 1769480 | tf_op jit(solution)/shard_map/ppermute | solution.py:430
  144.6 15.7 %collective-permute-start.19 = (bf16[128,2176]{1,0:T(8,128)(2,1)}, bf16[128,2176]{1,0:T(8,128)(2,1)}, u32[]{:S(2)}, u32[]{:S(2)}) collective-permute-start(bf16[128,2176]{1,0:T(8,128)(2,1)} %get-tuple-element.106), channel_id=1, source_target_pairs={{0,2},{1,3},{2,0},{3,1},{4,6},{5,7},{6,4},{7,5},{8,10},{9,11},{10,... | collective-permute-start | bytes 1671176 | tf_op jit(solution)/shard_map/ppermute | solution.py:427
  146.8 15.4 %collective-permute-start.20 = (bf16[128,2176]{1,0:T(8,128)(2,1)}, bf16[128,2176]{1,0:T(8,128)(2,1)}, u32[]{:S(2)}, u32[]{:S(2)}) collective-permute-start(bf16[128,2176]{1,0:T(8,128)(2,1)} %add_convert_fusion.refs_9_), channel_id=1, source_target_pairs={{0,4},{4,8},{8,12},{12,0},{1,5},{5,9},{9,13},{13,1},{2,6},{6,10},{... | collective-permute-start | bytes 1671176 | tf_op jit(solution)/shard_map/ppermute | solution.py:424
  146.8 0.8 copy-start.11
  147.6 14.6 %copy-start = (f32[128,2176]{1,0:T(8,128)S(1)}, f32[128,2176]{1,0:T(8,128)}, u32[]{:S(2)}) copy-start(f32[128,2176]{1,0:T(8,128)} %get-tuple-element.105) | copy-start | bytes 3342340
  163.5 1.0 copy-start.6
  163.6 0.9 copy-start.7

commit v5 on v4

--- a/solution.py
+++ b/solution.py
@@ -136,7 +136,7 @@
 
 
 def work_cost(rows, depth, width):
-    return pl.CostEstimate(flops=60 * rows * depth * width, bytes_accessed=2 * rows * depth, transcendentals=0)
+    return pl.CostEstimate(flops=24 * rows * depth * width, bytes_accessed=2 * rows * depth, transcendentals=0)
 
 
 def step_kernel(lines, step, steps, passed, waited, token_count, model_width, f, *refs):

time: 166 us -> 162 us (0.976)
  other arithmetic: 6.18 us -> 3.05 us
    convert_element_type x3, other arithmetic: 3.48 us -> 1.57 us  [home(): return line.astype(jnp.bfloat16) if d else line]
  transfers between devices with their start and end apart: 21 -> 21, of which waited for: 9 -> 9; matrix products, arithmetic and copies ran while one was open for 3% -> 1% of each run, Pallas kernels for 39% -> 40%
where the time goes in v5:
time: 162 us; the launch traced here: 161 us
  waiting for transfers between devices  77.4 us (48%)
  Pallas kernels  64.6 us (40%)
  starting transfers between devices  12.6 us (8%)
  other arithmetic  3.05 us (2%)
  local copies, waits for them, and re-layouts  2.7 us (2%)
    ppermute x7, waiting for transfers between devices, z_shift(): lax.ppermute(value, 'expert', [(i, (i + step) % z_count) for i in range(z...  42.2 us
    pallas_call x4, Pallas kernels, one_step(): pl.pallas_call(lambda *refs: step_kernel(lines, step, steps, len(passed),...  40.8 us
    ppermute x7, waiting for transfers between devices, x_shift(): lax.ppermute(value, 'dp', [(i, (i + CORES * step) % dp_count) for i in ra...  35.1 us
    pallas_call x1, Pallas kernels, finish(): pl.pallas_call(lambda *refs: finish_kernel(lines, *refs), out_shape=[jax....  12.7 us
    pallas_call x1, Pallas kernels, mate_products(): pl.pallas_call(lambda *refs: mate_kernel(count, *refs), out_shape=jax.Sha...  8.94 us
    ppermute x7, starting transfers between devices, x_shift(): lax.ppermute(value, 'dp', [(i, (i + CORES * step) % dp_count) for i in ra...  7.83 us
  transfers between devices with their start and end apart: 21, of which 9 were waited for; matrix products, arithmetic and copies ran while one was open for 1% of the time, Pallas kernels for 40%

profile of v5, /device:TPU:0, one launch (start us, length us, event | category | flops | bytes accessed | tf_op | source)
XLA Modules:
  0.0 161.2 jit_solution(8879696368927009478)
XLA Ops:
  0.6 0.5 collective-permute-start.2
  1.1 0.1 collective-permute-start.3
  1.2 0.4 collective-permute-start.4
  1.7 2.2 %shard_map.110.refs_0_ = bf16[128,4224]{1,0:T(8,128)(2,1)} custom-call(bf16[128,2048]{1,0:T(8,128)(2,1)} %tok_ref.1, bf16[128,2048]{1,0:T(8,128)(2,1)} %cot_ref.1, s32[8,128]{1,0:T(8,128)} %bitcast.24, bf16[8,128]{1,0:T(8,128)(2,1)} %bitcast.25), custom_call_target="tpu_custom_call" | custom-call | tf_op jit(solution)/shard_map/pallas_call | solution.py:404
  3.9 2.7 %collective-permute-start.1 = (bf16[128,4224]{1,0:T(8,128)(2,1)}, bf16[128,4224]{1,0:T(8,128)(2,1)}, u32[]{:S(2)}, u32[]{:S(2)}) collective-permute-start(bf16[128,4224]{1,0:T(8,128)(2,1)} %shard_map.110.refs_0_), channel_id=1, source_target_pairs={{0,4},{4,8},{8,12},{12,0},{1,5},{5,9},{9,13},{13,1},{2,6},{6,10},{... | collective-permute-start | bytes 3244040 | tf_op jit(solution)/shard_map/ppermute | solution.py:424
  6.6 1.5 collective-permute-start
  8.1 0.6 fusion.1.refs_2_
  8.7 24.7 %collective-permute-done.1.refs_0_ = bf16[128,4224]{1,0:T(8,128)(2,1)} collective-permute-done((bf16[128,4224]{1,0:T(8,128)(2,1)}, bf16[128,4224]{1,0:T(8,128)(2,1)}, u32[]{:S(2)}, u32[]{:S(2)}) %collective-permute-start.1) | collective-permute-done | bytes 1081376 | tf_op jit(solution)/shard_map/ppermute | solution.py:424
  33.4 0.0 collective-permute-done.2.refs_4_
  33.4 0.0 collective-permute-done.3.refs_6_
  33.4 0.0 collective-permute-done.4.refs_8_
  33.4 1.6 collective-permute-start.6
  34.9 0.0 collective-permute-start.5
  35.0 0.0 collective-permute-done.refs_1_
  35.0 0.0 copy-done.8
  35.0 10.2 %shard_map.111 = (f32[128,2176]{1,0:T(8,128)}, bf16[128,2176]{1,0:T(8,128)(2,1)}, bf16[1024,2048]{1,0:T(8,128)(2,1)}, bf16[1024,2048]{1,0:T(8,128)(2,1)}, bf16[1...) custom-call(bf16[128,4224]{1,0:T(8,128)(2,1)} %shard_map.110.refs_0_, ...), custom_call_target="tpu_custom_call" | custom-call | flops 48318382080 | bytes 1048576 | tf_op jit(solution)/shard_map/pallas_call | solution.py:271
  45.2 14.2 %collective-permute-done.6.refs_1_ = bf16[128,4224]{1,0:T(8,128)(2,1)} collective-permute-done((bf16[128,4224]{1,0:T(8,128)(2,1)}, bf16[128,4224]{1,0:T(8,128)(2,1)}, u32[]{:S(2)}, u32[]{:S(2)}) %collective-permute-start.6) | collective-permute-done | bytes 1081376 | tf_op jit(solution)/shard_map/ppermute | solution.py:427
  59.4 2.8 %collective-permute-done.5.refs_0_ = bf16[128,4224]{1,0:T(8,128)(2,1)S(1)} collective-permute-done((bf16[128,4224]{1,0:T(8,128)(2,1)}, bf16[128,4224]{1,0:T(8,128)(2,1)S(1)}, u32[]{:S(2)}, u32[]{:S(2)}) %collective-permute-start.5) | collective-permute-done | bytes 1081376 | tf_op jit(solution)/shard_map/ppermute | solution.py:424
  62.2 0.7 collective-permute-start.8
  62.8 0.0 collective-permute-start.7
  62.8 10.1 %shard_map.112 = (f32[128,2176]{1,0:T(8,128)}, bf16[128,2176]{1,0:T(8,128)(2,1)}, bf16[1024,2048]{1,0:T(8,128)(2,1)}, bf16[1024,2048]{1,0:T(8,128)(2,1)}, bf16[1...) custom-call(bf16[128,4224]{1,0:T(8,128)(2,1)} %collective-permute-do, ...), custom_call_target="tpu_custom_call", output_to_operand_aliasing={{2}: (9, {}), {3}: (10, {}), {4}: (11, {}), {5}: (12, {}), ... | custom-call | flops 48318382080 | bytes 1048576 | tf_op jit(solution)/shard_map/pallas_call | solution.py:271
  73.0 13.5 %collective-permute-done.8.refs_1_ = bf16[128,4224]{1,0:T(8,128)(2,1)} collective-permute-done((bf16[128,4224]{1,0:T(8,128)(2,1)S(1)}, bf16[128,4224]{1,0:T(8,128)(2,1)}, u32[]{:S(2)}, u32[]{:S(2)}) %collective-permute-start.8) | collective-permute-done | bytes 1081376 | tf_op jit(solution)/shard_map/ppermute | solution.py:427
  86.5 0.8 collective-permute-start.10
  87.4 1.5 collective-permute-done.7.refs_0_
  88.9 0.0 collective-permute-start.9
  88.9 10.2 %shard_map.113 = (f32[128,2176]{1,0:T(8,128)}, bf16[128,2176]{1,0:T(8,128)(2,1)}, bf16[1024,2048]{1,0:T(8,128)(2,1)}, bf16[1024,2048]{1,0:T(8,128)(2,1)}, bf16[1...) custom-call(bf16[128,4224]{1,0:T(8,128)(2,1)} %copy-done.9, ...), custom_call_target="tpu_custom_call", output_to_operand_aliasing={{2}: (9, {}), {3}: (10, {}), {4}: (11, {}), {5}: (12, {}), ... | custom-call | flops 48318382080 | bytes 1048576 | tf_op jit(solution)/shard_map/pallas_call | solution.py:271
  99.1 0.0 copy-start.3
  99.1 8.9 %shard_map.114.refs_18_ = bf16[1152,2048]{1,0:T(8,128)(2,1)} custom-call(bf16[1024,2048]{1,0:T(8,128)(2,1)} %get-tuple-element.84.refs_0_.refs_9_, bf16[1024,2048]{1,0:T(8,128)(2,1)} %get-tuple-element.85.refs_1_.refs_10_, bf16[1024,384]{1,0:T(8,128)(2,1)} %get-tuple-element.87.refs_2_.refs_12_, bf16[1024,384]{1,0:T(8,128)(2,1)} %get-tuple-element.89.refs_3_.refs_14_, ...), custom_call_target="tpu_custom_call" | custom-call | flops 43486543872 | bytes 3145728 | tf_op jit(solution)/shard_map/pallas_call | solution.py:308
  108.0 0.1 collective-permute-start.11
  108.1 0.0 collective-permute-done.10
  108.1 0.1 add_convert_fusion.2.refs_19_
  108.2 0.1 collective-permute-start.17
  108.3 6.6 %collective-permute-done.9.refs_1_ = bf16[128,4224]{1,0:T(8,128)(2,1)} collective-permute-done((bf16[128,4224]{1,0:T(8,128)(2,1)}, bf16[128,4224]{1,0:T(8,128)(2,1)}, u32[]{:S(2)}, u32[]{:S(2)}) %collective-permute-start.9) | collective-permute-done | bytes 1081376 | tf_op jit(solution)/shard_map/ppermute | solution.py:424
  114.8 0.9 collective-permute-start.16
  115.8 10.3 %shard_map.115 = (f32[128,2176]{1,0:T(8,128)}, bf16[128,2176]{1,0:T(8,128)(2,1)}, bf16[1024,2048]{1,0:T(8,128)(2,1)}, bf16[1024,2048]{1,0:T(8,128)(2,1)}, bf16[1...) custom-call(bf16[128,4224]{1,0:T(8,128)(2,1)} %collective-permute-do, ...), custom_call_target="tpu_custom_call", output_to_operand_aliasing={{2}: (9, {}), {3}: (10, {}), {4}: (11, {}), {5}: (12, {}), ... | custom-call | flops 48318382080 | bytes 1048576 | tf_op jit(solution)/shard_map/pallas_call | solution.py:271
  126.0 1.2 collective-permute-start.15
  127.2 0.0 collective-permute-done.17
  127.2 0.0 collective-permute-done.16
  127.2 0.8 copy-done.5
  128.0 1.3 add_convert_fusion.1
  129.4 0.1 collective-permute-start.18
  129.4 0.1 collective-permute-start.13
  129.5 0.5 collective-permute-start.14
  130.0 0.1 stack.67
  130.1 7.4 %collective-permute-done.15 = bf16[128,2176]{1,0:T(8,128)(2,1)S(1)} collective-permute-done((bf16[128,2176]{1,0:T(8,128)(2,1)}, bf16[128,2176]{1,0:T(8,128)(2,1)S(1)}, u32[]{:S(2)}, u32[]{:S(2)}) %collective-permute-start.15) | collective-permute-done | bytes 557088 | tf_op jit(solution)/shard_map/ppermute | solution.py:427
  137.4 0.0 collective-permute-start.12
  137.4 6.6 %collective-permute-done.18 = bf16[128,2176]{1,0:T(8,128)(2,1)S(1)} collective-permute-done((bf16[128,2176]{1,0:T(8,128)(2,1)S(1)}, bf16[128,2176]{1,0:T(8,128)(2,1)S(1)}, u32[]{:S(2)}, u32[]{:S(2)}) %collective-permute-start.18) | collective-permute-done | bytes 557088 | tf_op jit(solution)/shard_map/ppermute | solution.py:424
  144.1 1.2 collective-permute-start.19
  145.3 0.2 add_convert_fusion.refs_9_
  145.4 0.0 collective-permute-done.13.refs_7_
  145.5 0.3 collective-permute-start.20
  145.7 0.0 collective-permute-done.12.refs_6_
  145.8 0.0 collective-permute-done.14.refs_8_
  145.8 0.0 collective-permute-done.11.refs_5_
  145.8 0.5 copy-done.6
  146.2 0.4 copy-done.10
  146.6 12.7 %shard_map.116 = (bf16[2048,384]{1,0:T(8,128)(2,1)}, bf16[2048,384]{1,0:T(8,128)(2,1)}, bf16[384,2048]{1,0:T(8,128)(2,1)}) custom-call(bf16[1024,2048]{1,0:T(8,128)(2,1)} %get-tuple-element.93.refs_0_, bf16[1024,2048]{1,0:T(8,128)(2,1)} %get-tuple-element.94.refs_1_, bf16[1024,384]{1,0:T(8,128)(2,1)} %get-tuple-element.95.refs_2_, ...), custom_call_target="tpu_custom_call" | custom-call | flops 72477573120 | bytes 5242880 | tf_op jit(solution)/shard_map/pallas_call | solution.py:365
  159.4 0.0 collective-permute-done.19
  159.4 0.1 collective-permute-done.20
  159.5 0.1 convert_add_fusion
  159.6 0.0 copy-start.7
  159.6 0.9 slice.12
  160.5 0.1 copy.38
  160.6 0.7 select_reduce_fusion
  (19 shorter events, 0.0 us)
Async XLA Ops:
  0.6 32.7 %collective-permute-start.2 = (bf16[2048,384]{1,0:T(8,128)(2,1)}, bf16[2048,384]{1,0:T(8,128)(2,1)S(1)}, u32[]{:S(2)}, u32[]{:S(2)}) collective-permute-start(bf16[2048,384]{1,0:T(8,128)(2,1)} %bitcast.26), channel_id=1, source_target_pairs={{0,1},{1,0},{2,3},{3,2},{4,5},{5,4},{6,7},{7,6},{8,9},{9,8},{10,11... | collective-permute-start | bytes 4718600 | tf_op jit(solution)/shard_map/ppermute | solution.py:430
  1.1 32.2 %collective-permute-start.3 = (bf16[2048,384]{1,0:T(8,128)(2,1)}, bf16[2048,384]{1,0:T(8,128)(2,1)}, u32[]{:S(2)}, u32[]{:S(2)}) collective-permute-start(bf16[2048,384]{1,0:T(8,128)(2,1)} %bitcast.31), channel_id=1, source_target_pairs={{0,1},{1,0},{2,3},{3,2},{4,5},{5,4},{6,7},{7,6},{8,9},{9,8},{10,11... | collective-permute-start | bytes 4718600 | tf_op jit(solution)/shard_map/ppermute | solution.py:430
  1.2 32.2 %collective-permute-start.4 = (bf16[384,2048]{1,0:T(8,128)(2,1)}, bf16[384,2048]{1,0:T(8,128)(2,1)}, u32[]{:S(2)}, u32[]{:S(2)}) collective-permute-start(bf16[384,2048]{1,0:T(8,128)(2,1)} %bitcast.36), channel_id=1, source_target_pairs={{0,1},{1,0},{2,3},{3,2},{4,5},{5,4},{6,7},{7,6},{8,9},{9,8},{10,11... | collective-permute-start | bytes 4718600 | tf_op jit(solution)/shard_map/ppermute | solution.py:430
  3.9 29.5 %collective-permute-start.1 = (bf16[128,4224]{1,0:T(8,128)(2,1)}, bf16[128,4224]{1,0:T(8,128)(2,1)}, u32[]{:S(2)}, u32[]{:S(2)}) collective-permute-start(bf16[128,4224]{1,0:T(8,128)(2,1)} %shard_map.110.refs_0_), channel_id=1, source_target_pairs={{0,4},{4,8},{8,12},{12,0},{1,5},{5,9},{9,13},{13,1},{2,6},{6,10},{... | collective-permute-start | bytes 3244040 | tf_op jit(solution)/shard_map/ppermute | solution.py:424
  6.6 28.4 %collective-permute-start = (bf16[128,4224]{1,0:T(8,128)(2,1)}, bf16[128,4224]{1,0:T(8,128)(2,1)}, u32[]{:S(2)}, u32[]{:S(2)}) collective-permute-start(bf16[128,4224]{1,0:T(8,128)(2,1)} %shard_map.110.refs_0_), channel_id=1, source_target_pairs={{0,2},{1,3},{2,0},{3,1},{4,6},{5,7},{6,4},{7,5},{8,10},{9,11},{10,... | collective-permute-start | bytes 3244040 | tf_op jit(solution)/shard_map/ppermute | solution.py:427
  33.4 1.6 copy-start.8
  33.4 26.0 %collective-permute-start.6 = (bf16[128,4224]{1,0:T(8,128)(2,1)}, bf16[128,4224]{1,0:T(8,128)(2,1)}, u32[]{:S(2)}, u32[]{:S(2)}) collective-permute-start(bf16[128,4224]{1,0:T(8,128)(2,1)} %collective-permute-done.1.refs_0_), channel_id=1, source_target_pairs={{0,2},{1,3},{2,0},{3,1},{4,6},{5,7},{6,4},{7,5},{8,10},{9,11},{10,... | collective-permute-start | bytes 3244040 | tf_op jit(solution)/shard_map/ppermute | solution.py:427
  34.9 27.2 %collective-permute-start.5 = (bf16[128,4224]{1,0:T(8,128)(2,1)}, bf16[128,4224]{1,0:T(8,128)(2,1)S(1)}, u32[]{:S(2)}, u32[]{:S(2)}) collective-permute-start(bf16[128,4224]{1,0:T(8,128)(2,1)} %collective-permute-done.1.refs_0_), channel_id=1, source_target_pairs={{0,4},{4,8},{8,12},{12,0},{1,5},{5,9},{9,13},{13,1},{2,6},{6,10},{... | collective-permute-start | bytes 3244040 | tf_op jit(solution)/shard_map/ppermute | solution.py:424
  62.2 10.8 %copy-start.9 = (bf16[128,4224]{1,0:T(8,128)(2,1)}, bf16[128,4224]{1,0:T(8,128)(2,1)S(1)}, u32[]{:S(2)}) copy-start(bf16[128,4224]{1,0:T(8,128)(2,1)S(1)} %collective-permute-done.5.refs_0_) | copy-start | bytes 3244036
  62.2 24.4 %collective-permute-start.8 = (bf16[128,4224]{1,0:T(8,128)(2,1)S(1)}, bf16[128,4224]{1,0:T(8,128)(2,1)}, u32[]{:S(2)}, u32[]{:S(2)}) collective-permute-start(bf16[128,4224]{1,0:T(8,128)(2,1)S(1)} %collective-permute-done.5.refs_0_), channel_id=1, source_target_pairs={{0,2},{1,3},{2,0},{3,1},{4,6},{5,7},{6,4},{7,5},{8,10},{9,11},{10,... | collective-permute-start | bytes 3244040 | tf_op jit(solution)/shard_map/ppermute | solution.py:427
  62.8 26.1 %collective-permute-start.7 = (bf16[128,4224]{1,0:T(8,128)(2,1)S(1)}, bf16[128,4224]{1,0:T(8,128)(2,1)}, u32[]{:S(2)}, u32[]{:S(2)}) collective-permute-start(bf16[128,4224]{1,0:T(8,128)(2,1)S(1)} %collective-permute-done.5.refs_0_), channel_id=1, source_target_pairs={{0,4},{4,8},{8,12},{12,0},{1,5},{5,9},{9,13},{13,1},{2,6},{6,10},{... | collective-permute-start | bytes 3244040 | tf_op jit(solution)/shard_map/ppermute | solution.py:424
  86.5 21.5 %collective-permute-start.10 = (bf16[128,2176]{1,0:T(8,128)(2,1)}, bf16[128,2176]{1,0:T(8,128)(2,1)S(1)}, u32[]{:S(2)}, u32[]{:S(2)}) collective-permute-start(bf16[128,2176]{1,0:T(8,128)(2,1)} %get-tuple-element.73), channel_id=1, source_target_pairs={{0,2},{1,3},{2,0},{3,1},{4,6},{5,7},{6,4},{7,5},{8,10},{9,11},{10,... | collective-permute-start | bytes 1671176 | tf_op jit(solution)/shard_map/ppermute | solution.py:427
  88.9 26.0 %collective-permute-start.9 = (bf16[128,4224]{1,0:T(8,128)(2,1)}, bf16[128,4224]{1,0:T(8,128)(2,1)}, u32[]{:S(2)}, u32[]{:S(2)}) collective-permute-start(bf16[128,4224]{1,0:T(8,128)(2,1)} %collective-permute-done.8.refs_1_), channel_id=1, source_target_pairs={{0,4},{4,8},{8,12},{12,0},{1,5},{5,9},{9,13},{13,1},{2,6},{6,10},{... | collective-permute-start | bytes 3244040 | tf_op jit(solution)/shard_map/ppermute | solution.py:424
  99.1 9.1 %copy-start.3 = (f32[128,2176]{1,0:T(8,128)S(1)}, f32[128,2176]{1,0:T(8,128)}, u32[]{:S(2)}) copy-start(f32[128,2176]{1,0:T(8,128)} %get-tuple-element.92) | copy-start | bytes 3342340
  108.0 37.8 %collective-permute-start.11 = (bf16[1152,2048]{1,0:T(8,128)(2,1)}, bf16[1152,2048]{1,0:T(8,128)(2,1)}, u32[]{:S(2)}, u32[]{:S(2)}) collective-permute-start(bf16[1152,2048]{1,0:T(8,128)(2,1)} %shard_map.114.refs_18_), channel_id=1, source_target_pairs={{0,1},{1,0},{2,3},{3,2},{4,5},{5,4},{6,7},{7,6},{8,9},{9,8},{10,11... | collective-permute-start | bytes 14155784 | tf_op jit(solution)/shard_map/ppermute | solution.py:430
  108.2 7.5 %copy-start.4 = (bf16[128,2176]{1,0:T(8,128)(2,1)}, bf16[128,2176]{1,0:T(8,128)(2,1)S(1)}, u32[]{:S(2)}) copy-start(bf16[128,2176]{1,0:T(8,128)(2,1)S(1)} %add_convert_fusion.2.refs_19_) | copy-start | bytes 1671172
  108.2 19.0 %collective-permute-start.17 = (bf16[128,2176]{1,0:T(8,128)(2,1)S(1)}, bf16[128,2176]{1,0:T(8,128)(2,1)S(1)}, u32[]{:S(2)}, u32[]{:S(2)}) collective-permute-start(bf16[128,2176]{1,0:T(8,128)(2,1)S(1)} %add_convert_fusion.2.refs_19_), channel_id=1, source_target_pairs={{0,4},{4,8},{8,12},{12,0},{1,5},{5,9},{9,13},{13,1},{2,6},{6,10},{... | collective-permute-start | bytes 1671176 | tf_op jit(solution)/shard_map/ppermute | solution.py:424
  114.8 12.4 %collective-permute-start.16 = (bf16[128,2176]{1,0:T(8,128)(2,1)}, bf16[128,2176]{1,0:T(8,128)(2,1)S(1)}, u32[]{:S(2)}, u32[]{:S(2)}) collective-permute-start(bf16[128,2176]{1,0:T(8,128)(2,1)} %get-tuple-element.103), channel_id=1, source_target_pairs={{0,2},{1,3},{2,0},{3,1},{4,6},{5,7},{6,4},{7,5},{8,10},{9,11},{10,... | collective-permute-start | bytes 1671176 | tf_op jit(solution)/shard_map/ppermute | solution.py:427
  115.8 12.3 %copy-start.2 = (f32[128,2176]{1,0:T(8,128)S(1)}, f32[128,2176]{1,0:T(8,128)}, u32[]{:S(2)}) copy-start(f32[128,2176]{1,0:T(8,128)} %get-tuple-element.101) | copy-start | bytes 3342340
  126.0 11.4 %collective-permute-start.15 = (bf16[128,2176]{1,0:T(8,128)(2,1)}, bf16[128,2176]{1,0:T(8,128)(2,1)S(1)}, u32[]{:S(2)}, u32[]{:S(2)}) collective-permute-start(bf16[128,2176]{1,0:T(8,128)(2,1)} %get-tuple-element.100), channel_id=1, source_target_pairs={{0,2},{1,3},{2,0},{3,1},{4,6},{5,7},{6,4},{7,5},{8,10},{9,11},{10,... | collective-permute-start | bytes 1671176 | tf_op jit(solution)/shard_map/ppermute | solution.py:427
  127.2 0.8 copy-start.5
  128.0 17.2 %copy-start.1 = (f32[128,2176]{1,0:T(8,128)S(1)}, f32[128,2176]{1,0:T(8,128)}, u32[]{:S(2)}) copy-start(f32[128,2176]{1,0:T(8,128)} %get-tuple-element.99) | copy-start | bytes 3342340
  129.4 14.7 %collective-permute-start.18 = (bf16[128,2176]{1,0:T(8,128)(2,1)S(1)}, bf16[128,2176]{1,0:T(8,128)(2,1)S(1)}, u32[]{:S(2)}, u32[]{:S(2)}) collective-permute-start(bf16[128,2176]{1,0:T(8,128)(2,1)S(1)} %add_convert_fusion.1), channel_id=1, source_target_pairs={{0,4},{4,8},{8,12},{12,0},{1,5},{5,9},{9,13},{13,1},{2,6},{6,10},{... | collective-permute-start | bytes 1671176 | tf_op jit(solution)/shard_map/ppermute | solution.py:424
  129.4 16.0 %collective-permute-start.13 = (bf16[128,4224]{1,0:T(8,128)(2,1)}, bf16[128,4224]{1,0:T(8,128)(2,1)}, u32[]{:S(2)}, u32[]{:S(2)}) collective-permute-start(bf16[128,4224]{1,0:T(8,128)(2,1)} %collective-permute-done.7.refs_0_), channel_id=1, source_target_pairs={{0,1},{1,0},{2,3},{3,2},{4,5},{5,4},{6,7},{7,6},{8,9},{9,8},{10,11... | collective-permute-start | bytes 3244040 | tf_op jit(solution)/shard_map/ppermute | solution.py:430
  129.5 16.3 %collective-permute-start.14 = (bf16[128,4224]{1,0:T(8,128)(2,1)}, bf16[128,4224]{1,0:T(8,128)(2,1)}, u32[]{:S(2)}, u32[]{:S(2)}) collective-permute-start(bf16[128,4224]{1,0:T(8,128)(2,1)} %collective-permute-done.9.refs_1_), channel_id=1, source_target_pairs={{0,1},{1,0},{2,3},{3,2},{4,5},{5,4},{6,7},{7,6},{8,9},{9,8},{10,11... | collective-permute-start | bytes 3244040 | tf_op jit(solution)/shard_map/ppermute | solution.py:430
  137.4 8.3 %collective-permute-start.12 = (bf16[256,1152]{1,0:T(8,128)(2,1)}, bf16[256,1152]{1,0:T(8,128)(2,1)S(1)}, u32[]{:S(2)}, u32[]{:S(2)}) collective-permute-start(bf16[256,1152]{1,0:T(8,128)(2,1)} %get-tuple-element.98), channel_id=1, source_target_pairs={{0,1},{1,0},{2,3},{3,2},{4,5},{5,4},{6,7},{7,6},{8,9},{9,8},{10,11... | collective-permute-start | bytes 1769480 | tf_op jit(solution)/shard_map/ppermute | solution.py:430
  144.1 15.3 %collective-permute-start.19 = (bf16[128,2176]{1,0:T(8,128)(2,1)}, bf16[128,2176]{1,0:T(8,128)(2,1)S(1)}, u32[]{:S(2)}, u32[]{:S(2)}) collective-permute-start(bf16[128,2176]{1,0:T(8,128)(2,1)} %get-tuple-element.106), channel_id=1, source_target_pairs={{0,2},{1,3},{2,0},{3,1},{4,6},{5,7},{6,4},{7,5},{8,10},{9,11},{10,... | collective-permute-start | bytes 1671176 | tf_op jit(solution)/shard_map/ppermute | solution.py:427
  145.4 0.8 copy-start.6
  145.5 14.0 %collective-permute-start.20 = (bf16[128,2176]{1,0:T(8,128)(2,1)S(1)}, bf16[128,2176]{1,0:T(8,128)(2,1)S(1)}, u32[]{:S(2)}, u32[]{:S(2)}) collective-permute-start(bf16[128,2176]{1,0:T(8,128)(2,1)S(1)} %add_convert_fusion.refs_9_), channel_id=1, source_target_pairs={{0,4},{4,8},{8,12},{12,0},{1,5},{5,9},{9,13},{13,1},{2,6},{6,10},{... | collective-permute-start | bytes 1671176 | tf_op jit(solution)/shard_map/ppermute | solution.py:424
  145.8 0.9 copy-start.10
  146.6 12.8 %copy-start = (f32[128,2176]{1,0:T(8,128)S(1)}, f32[128,2176]{1,0:T(8,128)}, u32[]{:S(2)}) copy-start(f32[128,2176]{1,0:T(8,128)} %get-tuple-element.105) | copy-start | bytes 3342340
  159.6 0.9 copy-start.7

commit v6 on v5

--- a/solution.py
+++ b/solution.py
@@ -136,7 +136,7 @@
 
 
 def work_cost(rows, depth, width):
-    return pl.CostEstimate(flops=24 * rows * depth * width, bytes_accessed=2 * rows * depth, transcendentals=0)
+    return pl.CostEstimate(flops=12 * rows * depth * width, bytes_accessed=2 * rows * depth, transcendentals=0)
 
 
 def step_kernel(lines, step, steps, passed, waited, token_count, model_width, f, *refs):

time: 162 us -> 162 us (level)
  no operation moved by 1% of the time
where the time goes in v6:
time: 162 us; the launch traced here: 161 us
  waiting for transfers between devices  77.4 us (48%)
  Pallas kernels  64.6 us (40%)
  starting transfers between devices  12.6 us (8%)
  other arithmetic  3.05 us (2%)
  local copies, waits for them, and re-layouts  2.7 us (2%)
    ppermute x7, waiting for transfers between devices, z_shift(): lax.ppermute(value, 'expert', [(i, (i + step) % z_count) for i in range(z...  42.2 us
    pallas_call x4, Pallas kernels, one_step(): pl.pallas_call(lambda *refs: step_kernel(lines, step, steps, len(passed),...  40.8 us
    ppermute x7, waiting for transfers between devices, x_shift(): lax.ppermute(value, 'dp', [(i, (i + CORES * step) % dp_count) for i in ra...  35.1 us
    pallas_call x1, Pallas kernels, finish(): pl.pallas_call(lambda *refs: finish_kernel(lines, *refs), out_shape=[jax....  12.7 us
    pallas_call x1, Pallas kernels, mate_products(): pl.pallas_call(lambda *refs: mate_kernel(count, *refs), out_shape=jax.Sha...  8.94 us
    ppermute x7, starting transfers between devices, x_shift(): lax.ppermute(value, 'dp', [(i, (i + CORES * step) % dp_count) for i in ra...  7.83 us
  transfers between devices with their start and end apart: 21, of which 9 were waited for; matrix products, arithmetic and copies ran while one was open for 1% of the time, Pallas kernels for 40%

profile of v6, /device:TPU:0, one launch (start us, length us, event | category | flops | bytes accessed | tf_op | source)
XLA Modules:
  0.0 161.2 jit_solution(8879696368927009478)
XLA Ops:
  0.6 0.5 collective-permute-start.2
  1.1 0.1 collective-permute-start.3
  1.2 0.4 collective-permute-start.4
  1.7 2.2 %shard_map.110.refs_0_ = bf16[128,4224]{1,0:T(8,128)(2,1)} custom-call(bf16[128,2048]{1,0:T(8,128)(2,1)} %tok_ref.1, bf16[128,2048]{1,0:T(8,128)(2,1)} %cot_ref.1, s32[8,128]{1,0:T(8,128)} %bitcast.24, bf16[8,128]{1,0:T(8,128)(2,1)} %bitcast.25), custom_call_target="tpu_custom_call" | custom-call | tf_op jit(solution)/shard_map/pallas_call | solution.py:404
  3.9 2.7 %collective-permute-start.1 = (bf16[128,4224]{1,0:T(8,128)(2,1)}, bf16[128,4224]{1,0:T(8,128)(2,1)}, u32[]{:S(2)}, u32[]{:S(2)}) collective-permute-start(bf16[128,4224]{1,0:T(8,128)(2,1)} %shard_map.110.refs_0_), channel_id=1, source_target_pairs={{0,4},{4,8},{8,12},{12,0},{1,5},{5,9},{9,13},{13,1},{2,6},{6,10},{... | collective-permute-start | bytes 3244040 | tf_op jit(solution)/shard_map/ppermute | solution.py:424
  6.6 1.5 collective-permute-start
  8.1 0.6 fusion.1.refs_2_
  8.7 24.7 %collective-permute-done.1.refs_0_ = bf16[128,4224]{1,0:T(8,128)(2,1)} collective-permute-done((bf16[128,4224]{1,0:T(8,128)(2,1)}, bf16[128,4224]{1,0:T(8,128)(2,1)}, u32[]{:S(2)}, u32[]{:S(2)}) %collective-permute-start.1) | collective-permute-done | bytes 1081376 | tf_op jit(solution)/shard_map/ppermute | solution.py:424
  33.4 0.0 collective-permute-done.2.refs_4_
  33.4 0.0 collective-permute-done.3.refs_6_
  33.4 0.0 collective-permute-done.4.refs_8_
  33.4 1.6 collective-permute-start.6
  34.9 0.0 collective-permute-start.5
  35.0 0.0 collective-permute-done.refs_1_
  35.0 0.0 copy-done.8
  35.0 10.2 %shard_map.111 = (f32[128,2176]{1,0:T(8,128)}, bf16[128,2176]{1,0:T(8,128)(2,1)}, bf16[1024,2048]{1,0:T(8,128)(2,1)}, bf16[1024,2048]{1,0:T(8,128)(2,1)}, bf16[1...) custom-call(bf16[128,4224]{1,0:T(8,128)(2,1)} %shard_map.110.refs_0_, ...), custom_call_target="tpu_custom_call" | custom-call | flops 24159191040 | bytes 1048576 | tf_op jit(solution)/shard_map/pallas_call | solution.py:271
  45.2 14.2 %collective-permute-done.6.refs_1_ = bf16[128,4224]{1,0:T(8,128)(2,1)} collective-permute-done((bf16[128,4224]{1,0:T(8,128)(2,1)}, bf16[128,4224]{1,0:T(8,128)(2,1)}, u32[]{:S(2)}, u32[]{:S(2)}) %collective-permute-start.6) | collective-permute-done | bytes 1081376 | tf_op jit(solution)/shard_map/ppermute | solution.py:427
  59.4 2.8 %collective-permute-done.5.refs_0_ = bf16[128,4224]{1,0:T(8,128)(2,1)S(1)} collective-permute-done((bf16[128,4224]{1,0:T(8,128)(2,1)}, bf16[128,4224]{1,0:T(8,128)(2,1)S(1)}, u32[]{:S(2)}, u32[]{:S(2)}) %collective-permute-start.5) | collective-permute-done | bytes 1081376 | tf_op jit(solution)/shard_map/ppermute | solution.py:424
  62.2 0.7 collective-permute-start.8
  62.8 0.0 collective-permute-start.7
  62.8 10.1 %shard_map.112 = (f32[128,2176]{1,0:T(8,128)}, bf16[128,2176]{1,0:T(8,128)(2,1)}, bf16[1024,2048]{1,0:T(8,128)(2,1)}, bf16[1024,2048]{1,0:T(8,128)(2,1)}, bf16[1...) custom-call(bf16[128,4224]{1,0:T(8,128)(2,1)} %collective-permute-do, ...), custom_call_target="tpu_custom_call", output_to_operand_aliasing={{2}: (9, {}), {3}: (10, {}), {4}: (11, {}), {5}: (12, {}), ... | custom-call | flops 24159191040 | bytes 1048576 | tf_op jit(solution)/shard_map/pallas_call | solution.py:271
  73.0 13.5 %collective-permute-done.8.refs_1_ = bf16[128,4224]{1,0:T(8,128)(2,1)} collective-permute-done((bf16[128,4224]{1,0:T(8,128)(2,1)S(1)}, bf16[128,4224]{1,0:T(8,128)(2,1)}, u32[]{:S(2)}, u32[]{:S(2)}) %collective-permute-start.8) | collective-permute-done | bytes 1081376 | tf_op jit(solution)/shard_map/ppermute | solution.py:427
  86.5 0.8 collective-permute-start.10
  87.4 1.5 collective-permute-done.7.refs_0_
  88.9 0.0 collective-permute-start.9
  88.9 10.2 %shard_map.113 = (f32[128,2176]{1,0:T(8,128)}, bf16[128,2176]{1,0:T(8,128)(2,1)}, bf16[1024,2048]{1,0:T(8,128)(2,1)}, bf16[1024,2048]{1,0:T(8,128)(2,1)}, bf16[1...) custom-call(bf16[128,4224]{1,0:T(8,128)(2,1)} %copy-done.9, ...), custom_call_target="tpu_custom_call", output_to_operand_aliasing={{2}: (9, {}), {3}: (10, {}), {4}: (11, {}), {5}: (12, {}), ... | custom-call | flops 24159191040 | bytes 1048576 | tf_op jit(solution)/shard_map/pallas_call | solution.py:271
  99.1 0.0 copy-start.3
  99.1 8.9 %shard_map.114.refs_18_ = bf16[1152,2048]{1,0:T(8,128)(2,1)} custom-call(bf16[1024,2048]{1,0:T(8,128)(2,1)} %get-tuple-element.84.refs_0_.refs_9_, bf16[1024,2048]{1,0:T(8,128)(2,1)} %get-tuple-element.85.refs_1_.refs_10_, bf16[1024,384]{1,0:T(8,128)(2,1)} %get-tuple-element.87.refs_2_.refs_12_, bf16[1024,384]{1,0:T(8,128)(2,1)} %get-tuple-element.89.refs_3_.refs_14_, ...), custom_call_target="tpu_custom_call" | custom-call | flops 21743271936 | bytes 3145728 | tf_op jit(solution)/shard_map/pallas_call | solution.py:308
  108.0 0.1 collective-permute-start.11
  108.1 0.0 collective-permute-done.10
  108.1 0.1 add_convert_fusion.2.refs_19_
  108.2 0.1 collective-permute-start.17
  108.3 6.6 %collective-permute-done.9.refs_1_ = bf16[128,4224]{1,0:T(8,128)(2,1)} collective-permute-done((bf16[128,4224]{1,0:T(8,128)(2,1)}, bf16[128,4224]{1,0:T(8,128)(2,1)}, u32[]{:S(2)}, u32[]{:S(2)}) %collective-permute-start.9) | collective-permute-done | bytes 1081376 | tf_op jit(solution)/shard_map/ppermute | solution.py:424
  114.8 0.9 collective-permute-start.16
  115.8 10.3 %shard_map.115 = (f32[128,2176]{1,0:T(8,128)}, bf16[128,2176]{1,0:T(8,128)(2,1)}, bf16[1024,2048]{1,0:T(8,128)(2,1)}, bf16[1024,2048]{1,0:T(8,128)(2,1)}, bf16[1...) custom-call(bf16[128,4224]{1,0:T(8,128)(2,1)} %collective-permute-do, ...), custom_call_target="tpu_custom_call", output_to_operand_aliasing={{2}: (9, {}), {3}: (10, {}), {4}: (11, {}), {5}: (12, {}), ... | custom-call | flops 24159191040 | bytes 1048576 | tf_op jit(solution)/shard_map/pallas_call | solution.py:271
  126.0 1.2 collective-permute-start.15
  127.2 0.0 collective-permute-done.17
  127.2 0.0 collective-permute-done.16
  127.2 0.8 copy-done.5
  128.0 1.3 add_convert_fusion.1
  129.4 0.1 collective-permute-start.18
  129.4 0.1 collective-permute-start.13
  129.5 0.5 collective-permute-start.14
  130.0 0.1 stack.67
  130.1 7.4 %collective-permute-done.15 = bf16[128,2176]{1,0:T(8,128)(2,1)S(1)} collective-permute-done((bf16[128,2176]{1,0:T(8,128)(2,1)}, bf16[128,2176]{1,0:T(8,128)(2,1)S(1)}, u32[]{:S(2)}, u32[]{:S(2)}) %collective-permute-start.15) | collective-permute-done | bytes 557088 | tf_op jit(solution)/shard_map/ppermute | solution.py:427
  137.4 0.0 collective-permute-start.12
  137.4 6.6 %collective-permute-done.18 = bf16[128,2176]{1,0:T(8,128)(2,1)S(1)} collective-permute-done((bf16[128,2176]{1,0:T(8,128)(2,1)S(1)}, bf16[128,2176]{1,0:T(8,128)(2,1)S(1)}, u32[]{:S(2)}, u32[]{:S(2)}) %collective-permute-start.18) | collective-permute-done | bytes 557088 | tf_op jit(solution)/shard_map/ppermute | solution.py:424
  144.1 1.2 collective-permute-start.19
  145.3 0.2 add_convert_fusion.refs_9_
  145.4 0.0 collective-permute-done.13.refs_7_
  145.5 0.3 collective-permute-start.20
  145.7 0.0 collective-permute-done.12.refs_6_
  145.8 0.0 collective-permute-done.14.refs_8_
  145.8 0.0 collective-permute-done.11.refs_5_
  145.8 0.5 copy-done.6
  146.2 0.4 copy-done.10
  146.6 12.7 %shard_map.116 = (bf16[2048,384]{1,0:T(8,128)(2,1)}, bf16[2048,384]{1,0:T(8,128)(2,1)}, bf16[384,2048]{1,0:T(8,128)(2,1)}) custom-call(bf16[1024,2048]{1,0:T(8,128)(2,1)} %get-tuple-element.93.refs_0_, bf16[1024,2048]{1,0:T(8,128)(2,1)} %get-tuple-element.94.refs_1_, bf16[1024,384]{1,0:T(8,128)(2,1)} %get-tuple-element.95.refs_2_, ...), custom_call_target="tpu_custom_call" | custom-call | flops 36238786560 | bytes 5242880 | tf_op jit(solution)/shard_map/pallas_call | solution.py:365
  159.4 0.0 collective-permute-done.19
  159.4 0.1 collective-permute-done.20
  159.5 0.1 convert_add_fusion
  159.6 0.0 copy-start.7
  159.6 0.9 slice.12
  160.5 0.1 copy.38
  160.6 0.7 select_reduce_fusion
  (19 shorter events, 0.0 us)
Async XLA Ops:
  0.6 32.7 %collective-permute-start.2 = (bf16[2048,384]{1,0:T(8,128)(2,1)}, bf16[2048,384]{1,0:T(8,128)(2,1)S(1)}, u32[]{:S(2)}, u32[]{:S(2)}) collective-permute-start(bf16[2048,384]{1,0:T(8,128)(2,1)} %bitcast.26), channel_id=1, source_target_pairs={{0,1},{1,0},{2,3},{3,2},{4,5},{5,4},{6,7},{7,6},{8,9},{9,8},{10,11... | collective-permute-start | bytes 4718600 | tf_op jit(solution)/shard_map/ppermute | solution.py:430
  1.1 32.2 %collective-permute-start.3 = (bf16[2048,384]{1,0:T(8,128)(2,1)}, bf16[2048,384]{1,0:T(8,128)(2,1)}, u32[]{:S(2)}, u32[]{:S(2)}) collective-permute-start(bf16[2048,384]{1,0:T(8,128)(2,1)} %bitcast.31), channel_id=1, source_target_pairs={{0,1},{1,0},{2,3},{3,2},{4,5},{5,4},{6,7},{7,6},{8,9},{9,8},{10,11... | collective-permute-start | bytes 4718600 | tf_op jit(solution)/shard_map/ppermute | solution.py:430
  1.2 32.2 %collective-permute-start.4 = (bf16[384,2048]{1,0:T(8,128)(2,1)}, bf16[384,2048]{1,0:T(8,128)(2,1)}, u32[]{:S(2)}, u32[]{:S(2)}) collective-permute-start(bf16[384,2048]{1,0:T(8,128)(2,1)} %bitcast.36), channel_id=1, source_target_pairs={{0,1},{1,0},{2,3},{3,2},{4,5},{5,4},{6,7},{7,6},{8,9},{9,8},{10,11... | collective-permute-start | bytes 4718600 | tf_op jit(solution)/shard_map/ppermute | solution.py:430
  3.9 29.5 %collective-permute-start.1 = (bf16[128,4224]{1,0:T(8,128)(2,1)}, bf16[128,4224]{1,0:T(8,128)(2,1)}, u32[]{:S(2)}, u32[]{:S(2)}) collective-permute-start(bf16[128,4224]{1,0:T(8,128)(2,1)} %shard_map.110.refs_0_), channel_id=1, source_target_pairs={{0,4},{4,8},{8,12},{12,0},{1,5},{5,9},{9,13},{13,1},{2,6},{6,10},{... | collective-permute-start | bytes 3244040 | tf_op jit(solution)/shard_map/ppermute | solution.py:424
  6.6 28.4 %collective-permute-start = (bf16[128,4224]{1,0:T(8,128)(2,1)}, bf16[128,4224]{1,0:T(8,128)(2,1)}, u32[]{:S(2)}, u32[]{:S(2)}) collective-permute-start(bf16[128,4224]{1,0:T(8,128)(2,1)} %shard_map.110.refs_0_), channel_id=1, source_target_pairs={{0,2},{1,3},{2,0},{3,1},{4,6},{5,7},{6,4},{7,5},{8,10},{9,11},{10,... | collective-permute-start | bytes 3244040 | tf_op jit(solution)/shard_map/ppermute | solution.py:427
  33.4 1.6 copy-start.8
  33.4 26.0 %collective-permute-start.6 = (bf16[128,4224]{1,0:T(8,128)(2,1)}, bf16[128,4224]{1,0:T(8,128)(2,1)}, u32[]{:S(2)}, u32[]{:S(2)}) collective-permute-start(bf16[128,4224]{1,0:T(8,128)(2,1)} %collective-permute-done.1.refs_0_), channel_id=1, source_target_pairs={{0,2},{1,3},{2,0},{3,1},{4,6},{5,7},{6,4},{7,5},{8,10},{9,11},{10,... | collective-permute-start | bytes 3244040 | tf_op jit(solution)/shard_map/ppermute | solution.py:427
  34.9 27.2 %collective-permute-start.5 = (bf16[128,4224]{1,0:T(8,128)(2,1)}, bf16[128,4224]{1,0:T(8,128)(2,1)S(1)}, u32[]{:S(2)}, u32[]{:S(2)}) collective-permute-start(bf16[128,4224]{1,0:T(8,128)(2,1)} %collective-permute-done.1.refs_0_), channel_id=1, source_target_pairs={{0,4},{4,8},{8,12},{12,0},{1,5},{5,9},{9,13},{13,1},{2,6},{6,10},{... | collective-permute-start | bytes 3244040 | tf_op jit(solution)/shard_map/ppermute | solution.py:424
  62.2 10.8 %copy-start.9 = (bf16[128,4224]{1,0:T(8,128)(2,1)}, bf16[128,4224]{1,0:T(8,128)(2,1)S(1)}, u32[]{:S(2)}) copy-start(bf16[128,4224]{1,0:T(8,128)(2,1)S(1)} %collective-permute-done.5.refs_0_) | copy-start | bytes 3244036
  62.2 24.4 %collective-permute-start.8 = (bf16[128,4224]{1,0:T(8,128)(2,1)S(1)}, bf16[128,4224]{1,0:T(8,128)(2,1)}, u32[]{:S(2)}, u32[]{:S(2)}) collective-permute-start(bf16[128,4224]{1,0:T(8,128)(2,1)S(1)} %collective-permute-done.5.refs_0_), channel_id=1, source_target_pairs={{0,2},{1,3},{2,0},{3,1},{4,6},{5,7},{6,4},{7,5},{8,10},{9,11},{10,... | collective-permute-start | bytes 3244040 | tf_op jit(solution)/shard_map/ppermute | solution.py:427
  62.8 26.1 %collective-permute-start.7 = (bf16[128,4224]{1,0:T(8,128)(2,1)S(1)}, bf16[128,4224]{1,0:T(8,128)(2,1)}, u32[]{:S(2)}, u32[]{:S(2)}) collective-permute-start(bf16[128,4224]{1,0:T(8,128)(2,1)S(1)} %collective-permute-done.5.refs_0_), channel_id=1, source_target_pairs={{0,4},{4,8},{8,12},{12,0},{1,5},{5,9},{9,13},{13,1},{2,6},{6,10},{... | collective-permute-start | bytes 3244040 | tf_op jit(solution)/shard_map/ppermute | solution.py:424
  86.5 21.5 %collective-permute-start.10 = (bf16[128,2176]{1,0:T(8,128)(2,1)}, bf16[128,2176]{1,0:T(8,128)(2,1)S(1)}, u32[]{:S(2)}, u32[]{:S(2)}) collective-permute-start(bf16[128,2176]{1,0:T(8,128)(2,1)} %get-tuple-element.73), channel_id=1, source_target_pairs={{0,2},{1,3},{2,0},{3,1},{4,6},{5,7},{6,4},{7,5},{8,10},{9,11},{10,... | collective-permute-start | bytes 1671176 | tf_op jit(solution)/shard_map/ppermute | solution.py:427
  88.9 26.0 %collective-permute-start.9 = (bf16[128,4224]{1,0:T(8,128)(2,1)}, bf16[128,4224]{1,0:T(8,128)(2,1)}, u32[]{:S(2)}, u32[]{:S(2)}) collective-permute-start(bf16[128,4224]{1,0:T(8,128)(2,1)} %collective-permute-done.8.refs_1_), channel_id=1, source_target_pairs={{0,4},{4,8},{8,12},{12,0},{1,5},{5,9},{9,13},{13,1},{2,6},{6,10},{... | collective-permute-start | bytes 3244040 | tf_op jit(solution)/shard_map/ppermute | solution.py:424
  99.1 9.1 %copy-start.3 = (f32[128,2176]{1,0:T(8,128)S(1)}, f32[128,2176]{1,0:T(8,128)}, u32[]{:S(2)}) copy-start(f32[128,2176]{1,0:T(8,128)} %get-tuple-element.92) | copy-start | bytes 3342340
  108.0 37.8 %collective-permute-start.11 = (bf16[1152,2048]{1,0:T(8,128)(2,1)}, bf16[1152,2048]{1,0:T(8,128)(2,1)}, u32[]{:S(2)}, u32[]{:S(2)}) collective-permute-start(bf16[1152,2048]{1,0:T(8,128)(2,1)} %shard_map.114.refs_18_), channel_id=1, source_target_pairs={{0,1},{1,0},{2,3},{3,2},{4,5},{5,4},{6,7},{7,6},{8,9},{9,8},{10,11... | collective-permute-start | bytes 14155784 | tf_op jit(solution)/shard_map/ppermute | solution.py:430
  108.2 7.5 %copy-start.4 = (bf16[128,2176]{1,0:T(8,128)(2,1)}, bf16[128,2176]{1,0:T(8,128)(2,1)S(1)}, u32[]{:S(2)}) copy-start(bf16[128,2176]{1,0:T(8,128)(2,1)S(1)} %add_convert_fusion.2.refs_19_) | copy-start | bytes 1671172
  108.2 19.0 %collective-permute-start.17 = (bf16[128,2176]{1,0:T(8,128)(2,1)S(1)}, bf16[128,2176]{1,0:T(8,128)(2,1)S(1)}, u32[]{:S(2)}, u32[]{:S(2)}) collective-permute-start(bf16[128,2176]{1,0:T(8,128)(2,1)S(1)} %add_convert_fusion.2.refs_19_), channel_id=1, source_target_pairs={{0,4},{4,8},{8,12},{12,0},{1,5},{5,9},{9,13},{13,1},{2,6},{6,10},{... | collective-permute-start | bytes 1671176 | tf_op jit(solution)/shard_map/ppermute | solution.py:424
  114.8 12.4 %collective-permute-start.16 = (bf16[128,2176]{1,0:T(8,128)(2,1)}, bf16[128,2176]{1,0:T(8,128)(2,1)S(1)}, u32[]{:S(2)}, u32[]{:S(2)}) collective-permute-start(bf16[128,2176]{1,0:T(8,128)(2,1)} %get-tuple-element.103), channel_id=1, source_target_pairs={{0,2},{1,3},{2,0},{3,1},{4,6},{5,7},{6,4},{7,5},{8,10},{9,11},{10,... | collective-permute-start | bytes 1671176 | tf_op jit(solution)/shard_map/ppermute | solution.py:427
  115.8 12.3 %copy-start.2 = (f32[128,2176]{1,0:T(8,128)S(1)}, f32[128,2176]{1,0:T(8,128)}, u32[]{:S(2)}) copy-start(f32[128,2176]{1,0:T(8,128)} %get-tuple-element.101) | copy-start | bytes 3342340
  126.0 11.4 %collective-permute-start.15 = (bf16[128,2176]{1,0:T(8,128)(2,1)}, bf16[128,2176]{1,0:T(8,128)(2,1)S(1)}, u32[]{:S(2)}, u32[]{:S(2)}) collective-permute-start(bf16[128,2176]{1,0:T(8,128)(2,1)} %get-tuple-element.100), channel_id=1, source_target_pairs={{0,2},{1,3},{2,0},{3,1},{4,6},{5,7},{6,4},{7,5},{8,10},{9,11},{10,... | collective-permute-start | bytes 1671176 | tf_op jit(solution)/shard_map/ppermute | solution.py:427
  127.2 0.8 copy-start.5
  128.0 17.2 %copy-start.1 = (f32[128,2176]{1,0:T(8,128)S(1)}, f32[128,2176]{1,0:T(8,128)}, u32[]{:S(2)}) copy-start(f32[128,2176]{1,0:T(8,128)} %get-tuple-element.99) | copy-start | bytes 3342340
  129.4 14.7 %collective-permute-start.18 = (bf16[128,2176]{1,0:T(8,128)(2,1)S(1)}, bf16[128,2176]{1,0:T(8,128)(2,1)S(1)}, u32[]{:S(2)}, u32[]{:S(2)}) collective-permute-start(bf16[128,2176]{1,0:T(8,128)(2,1)S(1)} %add_convert_fusion.1), channel_id=1, source_target_pairs={{0,4},{4,8},{8,12},{12,0},{1,5},{5,9},{9,13},{13,1},{2,6},{6,10},{... | collective-permute-start | bytes 1671176 | tf_op jit(solution)/shard_map/ppermute | solution.py:424
  129.4 16.0 %collective-permute-start.13 = (bf16[128,4224]{1,0:T(8,128)(2,1)}, bf16[128,4224]{1,0:T(8,128)(2,1)}, u32[]{:S(2)}, u32[]{:S(2)}) collective-permute-start(bf16[128,4224]{1,0:T(8,128)(2,1)} %collective-permute-done.7.refs_0_), channel_id=1, source_target_pairs={{0,1},{1,0},{2,3},{3,2},{4,5},{5,4},{6,7},{7,6},{8,9},{9,8},{10,11... | collective-permute-start | bytes 3244040 | tf_op jit(solution)/shard_map/ppermute | solution.py:430
  129.5 16.3 %collective-permute-start.14 = (bf16[128,4224]{1,0:T(8,128)(2,1)}, bf16[128,4224]{1,0:T(8,128)(2,1)}, u32[]{:S(2)}, u32[]{:S(2)}) collective-permute-start(bf16[128,4224]{1,0:T(8,128)(2,1)} %collective-permute-done.9.refs_1_), channel_id=1, source_target_pairs={{0,1},{1,0},{2,3},{3,2},{4,5},{5,4},{6,7},{7,6},{8,9},{9,8},{10,11... | collective-permute-start | bytes 3244040 | tf_op jit(solution)/shard_map/ppermute | solution.py:430
  137.4 8.3 %collective-permute-start.12 = (bf16[256,1152]{1,0:T(8,128)(2,1)}, bf16[256,1152]{1,0:T(8,128)(2,1)S(1)}, u32[]{:S(2)}, u32[]{:S(2)}) collective-permute-start(bf16[256,1152]{1,0:T(8,128)(2,1)} %get-tuple-element.98), channel_id=1, source_target_pairs={{0,1},{1,0},{2,3},{3,2},{4,5},{5,4},{6,7},{7,6},{8,9},{9,8},{10,11... | collective-permute-start | bytes 1769480 | tf_op jit(solution)/shard_map/ppermute | solution.py:430
  144.1 15.3 %collective-permute-start.19 = (bf16[128,2176]{1,0:T(8,128)(2,1)}, bf16[128,2176]{1,0:T(8,128)(2,1)S(1)}, u32[]{:S(2)}, u32[]{:S(2)}) collective-permute-start(bf16[128,2176]{1,0:T(8,128)(2,1)} %get-tuple-element.106), channel_id=1, source_target_pairs={{0,2},{1,3},{2,0},{3,1},{4,6},{5,7},{6,4},{7,5},{8,10},{9,11},{10,... | collective-permute-start | bytes 1671176 | tf_op jit(solution)/shard_map/ppermute | solution.py:427
  145.4 0.8 copy-start.6
  145.5 14.0 %collective-permute-start.20 = (bf16[128,2176]{1,0:T(8,128)(2,1)S(1)}, bf16[128,2176]{1,0:T(8,128)(2,1)S(1)}, u32[]{:S(2)}, u32[]{:S(2)}) collective-permute-start(bf16[128,2176]{1,0:T(8,128)(2,1)S(1)} %add_convert_fusion.refs_9_), channel_id=1, source_target_pairs={{0,4},{4,8},{8,12},{12,0},{1,5},{5,9},{9,13},{13,1},{2,6},{6,10},{... | collective-permute-start | bytes 1671176 | tf_op jit(solution)/shard_map/ppermute | solution.py:424
  145.8 0.9 copy-start.10
  146.6 12.8 %copy-start = (f32[128,2176]{1,0:T(8,128)S(1)}, f32[128,2176]{1,0:T(8,128)}, u32[]{:S(2)}) copy-start(f32[128,2176]{1,0:T(8,128)} %get-tuple-element.105) | copy-start | bytes 3342340
  159.6 0.9 copy-start.7
